TPU v7x, 32 devices: a whole 2x2x4 slice. The times are simulated.
32 devices in a mesh: wide: 8 (over y, x, core), narrow: 4 (over z).
Axes of the slice: x: 2, y: 2, z: 4, core: 2. Of those that a mesh axis runs over, the one named last changes fastest.
Arguments:
- gradient: float32 [2, 2048, 1024], P(None, 'wide', 'narrow'), may hold values from -6 to 6
- probe_modes: bfloat16 [4, 2, 256, 256], replicated, may hold values from -5 to 5
- mode_weights: bfloat16 [8, 4, 3, 4, 2, 256, 256], P('wide', 'narrow'), may hold values from -4 to 4
- offsets: int32 [8, 4, 3, 2], P('wide', 'narrow'), may hold values from -64 to 64, as said below
- counts: int32 [8, 4], P('wide', 'narrow'), may hold values from 1 to 3, as said below
Outputs:
- solution: float32 [2, 2048, 1024], P(None, 'wide', 'narrow')
- residual: float32 [2, 2048, 1024], P(None, 'wide', 'narrow')
Inputs may be any that keep to these rules, and one draw needn't show every extreme that they name: `offsets`: each offset lies between -64 and 64; both ends are taken by some slot in every draw. `counts`: slots from a tile's count on are empty; some tile has all 3 slots live in every draw.
All inputs are finite; a program needn't handle non-finite values.
Results may differ from a plain program's by a relative error of at most 0.012.
Values sent between devices are 32-bit elements; how exact they have to be, the bound alone decides.
No kernel may reach another device: no remote copies, remote signals or barrier semaphores. Data moves between devices by JAX's collectives and lax.ppermute only.
A program may use at most 128 MiB of HBM per device.

v0:
```python
import math

import jax
import jax.numpy as jnp
from jax import lax
from jax.sharding import PartitionSpec as P

W = 256
STEPS = 2
HALO = 64


damping = 0.5


def padded(x, sides, width):
    for axis, dim in sides:
        peers, length = (lax.axis_size(axis), x.shape[dim])
        up = [(i, (i + 1) % peers) for i in range(peers - 1)]
        down = [(j, i) for i, j in up]
        last = lax.slice_in_dim(x, length - width, length, axis=dim)
        initial = lax.slice_in_dim(x, 0, width, axis=dim)
        before = lax.ppermute(last, axis, up)
        after = lax.ppermute(initial, axis, down)
        x = jnp.concatenate([before, x, after], axis=dim)
    return x


def dft_tables(length, sign):
    counter = jnp.arange(length, dtype=jnp.int32)
    phases = counter[:, None] * counter[None, :] % length
    angles = phases.astype(jnp.float32) * (2.0 * math.pi / length)
    factor = 1.0 / math.sqrt(length)
    real_part = jnp.cos(angles) * factor
    imag_part = -sign * jnp.sin(angles) * factor
    left_table = jnp.stack(
        [jnp.stack([real_part, -imag_part]), jnp.stack([imag_part, real_part])]
    ).astype(jnp.bfloat16)
    right_table = jnp.stack(
        [jnp.stack([real_part, imag_part]), jnp.stack([-imag_part, real_part])]
    ).astype(jnp.bfloat16)
    return (left_table, right_table)


def left_apply(table, values):
    return jnp.einsum("pqab,nqbc->npac", table, values, preferred_element_type=jnp.float32)


def right_apply(table, values):
    return jnp.einsum("nqac,qpcd->npad", values, table, preferred_element_type=jnp.float32)


def wave_pass(patches, probe_modes, weights, live_mask, forward_tables, inverse_tables):
    frames = patches.shape[0]
    modes = probe_modes.shape[0]
    length = probe_modes.shape[-1]
    probe_re = probe_modes[None, :, 0].astype(jnp.float32)
    probe_im = probe_modes[None, :, 1].astype(jnp.float32)
    patch_re = patches[:, None, 0]
    patch_im = patches[:, None, 1]
    exit_wave = jnp.stack(
        [probe_re * patch_re - probe_im * patch_im, probe_re * patch_im + probe_im * patch_re],
        axis=2,
    ).astype(jnp.bfloat16)
    stacked = exit_wave.reshape(frames * modes, 2, length, length)
    partial_value = left_apply(forward_tables[0], stacked).astype(jnp.bfloat16)
    far_field = right_apply(forward_tables[1], partial_value).reshape(
        frames, modes, 2, length, length
    )
    weight_re = weights[:, :, 0].astype(jnp.float32)
    weight_im = weights[:, :, 1].astype(jnp.float32)
    projected = (
        jnp.sum(weight_re * far_field[:, :, 0] + weight_im * far_field[:, :, 1], axis=1)
        * live_mask[:, None, None]
    )
    weighted = jnp.stack(
        [weight_re * projected[:, None], weight_im * projected[:, None]], axis=2
    ).astype(jnp.bfloat16)
    partial_back = left_apply(
        inverse_tables[0], weighted.reshape(frames * modes, 2, length, length)
    ).astype(jnp.bfloat16)
    near_field = right_apply(inverse_tables[1], partial_back).reshape(
        frames, modes, 2, length, length
    )
    near_re = near_field[:, :, 0]
    near_im = near_field[:, :, 1]
    contribution = jnp.stack(
        [
            jnp.sum(probe_re * near_re + probe_im * near_im, axis=1),
            jnp.sum(probe_re * near_im - probe_im * near_re, axis=1),
        ],
        axis=1,
    )
    return (contribution, projected)


def fold_margins(total):
    length = total.shape[1] - 2 * HALO
    inner_gap = length - 2 * HALO
    extent = total.shape[2]
    row_strips = jnp.concatenate(
        [
            total[:, :HALO],
            jnp.zeros((2, inner_gap, extent), jnp.float32),
            total[:, HALO + length :],
        ],
        axis=1,
    )
    arrived_rows = padded(row_strips, (("wide", 1),), HALO)
    middle = total[:, HALO : HALO + length]
    middle = middle.at[:, :HALO].add(arrived_rows[:, :HALO])
    middle = middle.at[:, length - HALO :].add(arrived_rows[:, HALO + length :])
    col_strips = jnp.concatenate(
        [
            middle[:, :, :HALO],
            jnp.zeros((2, length, inner_gap), jnp.float32),
            middle[:, :, HALO + length :],
        ],
        axis=2,
    )
    arrived_cols = padded(col_strips, (("narrow", 2),), HALO)
    inner = middle[:, :, HALO : HALO + length]
    inner = inner.at[:, :, :HALO].add(arrived_cols[:, :, :HALO])
    inner = inner.at[:, :, length - HALO :].add(arrived_cols[:, :, HALO + length :])
    return inner


def apply_operator(
    direction, probe_modes, mode_weights, offsets, counts, forward_tables, inverse_tables
):
    extended = padded(direction, (("wide", 1), ("narrow", 2)), HALO)
    total = jnp.zeros_like(extended)

    def visit(slot_index, carried):
        running, squares = carried
        row_start = HALO + offsets[0, 0, slot_index, 0]
        col_start = HALO + offsets[0, 0, slot_index, 1]
        patch = lax.dynamic_slice(extended, (0, row_start, col_start), (2, W, W))
        frame_weights = lax.dynamic_index_in_dim(mode_weights[0, 0], slot_index, 0, keepdims=True)
        contribution, projected = wave_pass(
            patch[None],
            probe_modes,
            frame_weights,
            jnp.ones((1,), jnp.float32),
            forward_tables,
            inverse_tables,
        )
        region = lax.dynamic_slice(running, (0, row_start, col_start), (2, W, W))
        running = lax.dynamic_update_slice(
            running, region + contribution[0], (0, row_start, col_start)
        )
        return (running, squares + jnp.sum(projected * projected))

    total, squares = lax.fori_loop(0, counts[0, 0], visit, (total, jnp.float32(0.0)))
    return (fold_margins(total) + damping * direction, squares)


def global_sum(value):
    return lax.psum(value, ("wide", "narrow"))


def local(gradient, probe_modes, mode_weights, offsets, counts):
    forward_tables = dft_tables(W, 1.0)
    inverse_tables = dft_tables(W, -1.0)
    solution = jnp.zeros_like(gradient)
    residual = gradient
    direction = gradient
    norm_now = global_sum(jnp.sum(residual * residual))
    for iteration in range(STEPS):
        image, squares = apply_operator(
            direction, probe_modes, mode_weights, offsets, counts, forward_tables, inverse_tables
        )
        curvature = global_sum(jnp.sum(direction * image))
        alpha = norm_now / curvature
        solution = solution + alpha * direction
        residual = residual - alpha * image
        if iteration + 1 < STEPS:
            norm_next = global_sum(jnp.sum(residual * residual))
            direction = residual + norm_next / norm_now * direction
            norm_now = norm_next
    return (solution, residual)


def solution(mesh):
    placed = (
        P(None, "wide", "narrow"),
        P(),
        P("wide", "narrow", None, None, None, None, None),
        P("wide", "narrow", None, None),
        P("wide", "narrow"),
    )
    return jax.shard_map(
        local,
        mesh=mesh,
        in_specs=placed,
        out_specs=(P(None, "wide", "narrow"), P(None, "wide", "narrow")),
        check_vma=False,
    )
```

profile of v0, /device:TPU:0, one launch (start us, length us, event | category | flops | bytes accessed | tf_op | source)
XLA Modules:
  0.0 383.8 jit_solution(10023103500729023612)
XLA Ops:
  1.6 2.4 collective-permute-start
  12.7 1.9 copy.17
  15.9 4.3 %collective-permute-start.2 = (f32[2,384,64]{2,1,0:T(8,128)S(1)}, f32[2,384,64]{2,1,0:T(8,128)S(1)}, u32[]{:S(2)}, u32[]{:S(2)}) collective-permute-start(f32[2,384,64]{2,1,0:T(8,128)S(1)} %get-tuple-element.592), channel_id=1, source_target_pairs={{0,1},{1,2},{2,3},{4,5},{5,6},{6,7},{8,9},{9,10},{10,11},{12,13},{... | collective-permute-start | bytes 589832 | tf_op jit(solution)/shard_map/ppermute | solution.py:23
  23.3 5.0 %collective-permute-done.2 = f32[2,384,64]{2,1,0:T(8,128)S(1)} collective-permute-done((f32[2,384,64]{2,1,0:T(8,128)S(1)}, f32[2,384,64]{2,1,0:T(8,128)S(1)}, u32[]{:S(2)}, u32[]{:S(2)}) %collective-permute-start.2) | collective-permute-done | bytes 196640 | tf_op jit(solution)/shard_map/ppermute | solution.py:23
  28.2 4.7 %collective-permute-done.3 = f32[2,384,64]{2,1,0:T(8,128)S(1)} collective-permute-done((f32[2,384,64]{2,1,0:T(8,128)S(1)}, f32[2,384,64]{2,1,0:T(8,128)S(1)}, u32[]{:S(2)}, u32[]{:S(2)}) %collective-permute-start.3) | collective-permute-done | bytes 196640 | tf_op jit(solution)/shard_map/ppermute | solution.py:24
  33.0 1.5 pad_maximum_fusion
  35.6 71.4 %while.38 = (s32[]{:T(128)}, f32[2,384,384]{2,1,0:T(8,128)}, s32[]{:T(128)}, s32[1,1,3,2]{2,3,1,0:T(2,128)S(1)}, bf16[4,2,256,256]{3,2,0,1:T(8,128)(2,1)S(1)}, /...) while((s32[]{:T(128)}, f32[2,384,384]{2,1,0:T(8,128)}, ...), condition=%wide.region_6.7_spmd, body=%wide.region_2.6_spmd.sunk | while | flops 2158034944 | bytes 27525440 | solution.py:154
  39.5 1.4 dynamic-slice_bitcast_fusion.8
  42.2 2.8 convolution_bitcast_fusion.8
  45.0 1.3 dynamic-slice_bitcast_fusion.9
  48.4 2.8 convolution_bitcast_fusion.9
  51.6 1.4 fusion.124
  52.9 6.3 %dynamic_update_slice.18 = f32[2,384,384]{2,1,0:T(8,128)} dynamic-update-slice(f32[2,384,384]{2,1,0:T(8,128)} %get-tuple-element.799, f32[2,256,256]{2,1,0:T(8,128)S(1)} %fusion.124, s32[]{:T(128)} %constant.314.clone.1..sunk, s32[]{:T(128)S(6)} %select_n.148, s32[]{:T(128)S(6)} %select_n.149) | dynamic-update-slice | bytes 1048580 | tf_op jit(solution)/shard_map/while/body/dynamic_update_slice | solution.py:149
  63.1 1.4 dynamic-slice_bitcast_fusion.8
  65.8 2.8 convolution_bitcast_fusion.8
  68.6 1.3 dynamic-slice_bitcast_fusion.9
  72.0 2.8 convolution_bitcast_fusion.9
  75.1 1.4 fusion.124
  76.5 6.3 %dynamic_update_slice.18 = f32[2,384,384]{2,1,0:T(8,128)} dynamic-update-slice(f32[2,384,384]{2,1,0:T(8,128)} %get-tuple-element.799, f32[2,256,256]{2,1,0:T(8,128)S(1)} %fusion.124, s32[]{:T(128)} %constant.314.clone.1..sunk, s32[]{:T(128)S(6)} %select_n.148, s32[]{:T(128)S(6)} %select_n.149) | dynamic-update-slice | bytes 1048580 | tf_op jit(solution)/shard_map/while/body/dynamic_update_slice | solution.py:149
  86.7 1.4 dynamic-slice_bitcast_fusion.8
  89.4 2.8 convolution_bitcast_fusion.8
  92.2 1.3 dynamic-slice_bitcast_fusion.9
  95.6 2.8 convolution_bitcast_fusion.9
  98.7 1.4 fusion.124
  100.1 6.3 %dynamic_update_slice.18 = f32[2,384,384]{2,1,0:T(8,128)} dynamic-update-slice(f32[2,384,384]{2,1,0:T(8,128)} %get-tuple-element.799, f32[2,256,256]{2,1,0:T(8,128)S(1)} %fusion.124, s32[]{:T(128)} %constant.314.clone.1..sunk, s32[]{:T(128)S(6)} %select_n.148, s32[]{:T(128)S(6)} %select_n.149) | dynamic-update-slice | bytes 1048580 | tf_op jit(solution)/shard_map/while/body/dynamic_update_slice | solution.py:149
  108.1 1.3 collective-permute-start.4
  114.1 1.5 collective-permute-start.6
  115.8 1.4 collective-permute-start.7
  117.2 4.3 %collective-permute-done.6 = f32[2,256,64]{2,1,0:T(8,128)S(1)} collective-permute-done((f32[2,256,64]{2,1,0:T(8,128)S(1)}, f32[2,256,64]{2,1,0:T(8,128)S(1)}, u32[]{:S(2)}, u32[]{:S(2)}) %collective-permute-start.6) | collective-permute-done | bytes 131104 | tf_op jit(solution)/shard_map/ppermute | solution.py:23
  122.8 7.0 %collective-permute-done.7 = f32[2,256,64]{2,1,0:T(8,128)S(1)} collective-permute-done((f32[2,256,64]{2,1,0:T(8,128)S(1)}, f32[2,256,64]{2,1,0:T(8,128)S(1)}, u32[]{:S(2)}, u32[]{:S(2)}) %collective-permute-start.7) | collective-permute-done | bytes 131104 | tf_op jit(solution)/shard_map/ppermute | solution.py:24
  131.9 42.3 %all-reduce = (f32[]{:T(128)}, f32[]{:T(128)}) all-reduce(f32[]{:T(128)} %get-tuple-element.521, f32[]{:T(128)} %get-tuple-element.520), channel_id=1, replica_groups=mesh['wide'=8,'narrow'=4] {'wide','narrow'}, use_global_device_ids=true, to_apply=%region_1.2 | all-reduce | flops 2 | bytes 16 | tf_op jit(solution)/shard_map/psum | solution.py:159
  176.2 40.6 %psum.30 = f32[]{:T(128)} all-reduce(f32[]{:T(128)} %multiply_reduce_fusion.1), channel_id=1, replica_groups=mesh['wide'=8,'narrow'=4] {'wide','narrow'}, use_global_device_ids=true, to_apply=%region_10.11 | all-reduce | flops 1 | bytes 8 | tf_op jit(solution)/shard_map/psum | solution.py:159
  220.9 4.4 %collective-permute-done.9 = f32[2,64,256]{2,1,0:T(8,128)S(1)} collective-permute-done((f32[2,64,256]{2,1,0:T(8,128)S(1)}, f32[2,64,256]{2,1,0:T(8,128)S(1)}, u32[]{:S(2)}, u32[]{:S(2)}) %collective-permute-start.9) | collective-permute-done | bytes 131104 | tf_op jit(solution)/shard_map/ppermute | solution.py:24
  225.5 3.7 collective-permute-start.10
  230.5 5.5 %collective-permute-done.10 = f32[2,384,64]{2,1,0:T(8,128)S(1)} collective-permute-done((f32[2,384,64]{2,1,0:T(8,128)S(1)}, f32[2,384,64]{2,1,0:T(8,128)S(1)}, u32[]{:S(2)}, u32[]{:S(2)}) %collective-permute-start.10) | collective-permute-done | bytes 196640 | tf_op jit(solution)/shard_map/ppermute | solution.py:23
  236.0 4.7 %collective-permute-done.11 = f32[2,384,64]{2,1,0:T(8,128)S(1)} collective-permute-done((f32[2,384,64]{2,1,0:T(8,128)S(1)}, f32[2,384,64]{2,1,0:T(8,128)S(1)}, u32[]{:S(2)}, u32[]{:S(2)}) %collective-permute-start.11) | collective-permute-done | bytes 196640 | tf_op jit(solution)/shard_map/ppermute | solution.py:24
  240.7 1.5 pad_maximum_fusion.1
  243.4 72.2 %while.39 = (s32[]{:T(128)}, f32[2,384,384]{2,1,0:T(8,128)}, s32[]{:T(128)}, s32[1,1,3,2]{2,3,1,0:T(2,128)S(1)}, bf16[4,2,256,256]{3,2,0,1:T(8,128)(2,1)S(1)}, /...) while((s32[]{:T(128)}, f32[2,384,384]{2,1,0:T(8,128)}, ...), condition=%wide.region_15.16_spmd, body=%wide.region_11.0_spmd.sunk | while | flops 2158034944 | bytes 27525440 | solution.py:154
  247.3 1.4 dynamic-slice_bitcast_fusion.10
  248.7 1.4 fusion.131
  250.1 2.8 convolution_bitcast_fusion.10
  252.9 1.3 dynamic-slice_bitcast_fusion.11
  256.4 2.8 convolution_bitcast_fusion.11
  259.6 1.4 fusion.136
  260.9 6.3 %dynamic_update_slice.19 = f32[2,384,384]{2,1,0:T(8,128)} dynamic-update-slice(f32[2,384,384]{2,1,0:T(8,128)} %get-tuple-element.847, f32[2,256,256]{2,1,0:T(8,128)S(1)} %fusion.136, s32[]{:T(128)} %constant.314.clone.1..sunk.1, s32[]{:T(128)S(6)} %select_n.151, s32[]{:T(128)S(6)} %select_n.152) | dynamic-update-slice | bytes 1048580 | tf_op jit(solution)/shard_map/while/body/dynamic_update_slice | solution.py:149
  271.2 1.4 dynamic-slice_bitcast_fusion.10
  272.6 1.4 fusion.131
  274.0 2.8 convolution_bitcast_fusion.10
  276.8 1.3 dynamic-slice_bitcast_fusion.11
  280.2 2.8 convolution_bitcast_fusion.11
  283.4 1.4 fusion.136
  284.8 6.3 %dynamic_update_slice.19 = f32[2,384,384]{2,1,0:T(8,128)} dynamic-update-slice(f32[2,384,384]{2,1,0:T(8,128)} %get-tuple-element.847, f32[2,256,256]{2,1,0:T(8,128)S(1)} %fusion.136, s32[]{:T(128)} %constant.314.clone.1..sunk.1, s32[]{:T(128)S(6)} %select_n.151, s32[]{:T(128)S(6)} %select_n.152) | dynamic-update-slice | bytes 1048580 | tf_op jit(solution)/shard_map/while/body/dynamic_update_slice | solution.py:149
  295.0 1.4 dynamic-slice_bitcast_fusion.10
  296.4 1.4 fusion.131
  297.8 2.8 convolution_bitcast_fusion.10
  304.1 2.8 convolution_bitcast_fusion.11
  307.3 1.4 fusion.136
  308.6 6.3 %dynamic_update_slice.19 = f32[2,384,384]{2,1,0:T(8,128)} dynamic-update-slice(f32[2,384,384]{2,1,0:T(8,128)} %get-tuple-element.847, f32[2,256,256]{2,1,0:T(8,128)S(1)} %fusion.136, s32[]{:T(128)} %constant.314.clone.1..sunk.1, s32[]{:T(128)S(6)} %select_n.151, s32[]{:T(128)S(6)} %select_n.152) | dynamic-update-slice | bytes 1048580 | tf_op jit(solution)/shard_map/while/body/dynamic_update_slice | solution.py:149
  316.6 1.3 collective-permute-start.12
  322.6 1.3 collective-permute-start.14
  324.2 1.4 collective-permute-start.15
  325.6 4.5 %collective-permute-done.14 = f32[2,256,64]{2,1,0:T(8,128)S(1)} collective-permute-done((f32[2,256,64]{2,1,0:T(8,128)S(1)}, f32[2,256,64]{2,1,0:T(8,128)S(1)}, u32[]{:S(2)}, u32[]{:S(2)}) %collective-permute-start.14) | collective-permute-done | bytes 131104 | tf_op jit(solution)/shard_map/ppermute | solution.py:23
  331.3 4.7 %collective-permute-done.15 = f32[2,256,64]{2,1,0:T(8,128)S(1)} collective-permute-done((f32[2,256,64]{2,1,0:T(8,128)S(1)}, f32[2,256,64]{2,1,0:T(8,128)S(1)}, u32[]{:S(2)}, u32[]{:S(2)}) %collective-permute-start.15) | collective-permute-done | bytes 131104 | tf_op jit(solution)/shard_map/ppermute | solution.py:24
  338.2 43.1 %psum.31 = f32[]{:T(128)} all-reduce(f32[]{:T(128)} %multiply_reduce_fusion), channel_id=1, replica_groups=mesh['wide'=8,'narrow'=4] {'wide','narrow'}, use_global_device_ids=true, to_apply=%region_17.18 | all-reduce | flops 1 | bytes 8 | tf_op jit(solution)/shard_map/psum | solution.py:159
  (120 shorter events, 65.2 us)
Async XLA Ops:
  1.6 13.1 %collective-permute-start = (f32[2,64,256]{2,1,0:T(8,128)S(1)}, f32[2,64,256]{2,1,0:T(8,128)S(1)}, u32[]{:S(2)}, u32[]{:S(2)}) collective-permute-start(f32[2,64,256]{2,1,0:T(8,128)S(1)} %get-tuple-element.597), channel_id=1, source_target_pairs={{0,4},{4,8},{8,12},{12,16},{16,20},{20,24},{24,28},{1,5},{5,9},{9,... | collective-permute-start | bytes 393224 | tf_op jit(solution)/shard_map/ppermute | solution.py:23
  4.0 11.7 %collective-permute-start.1 = (f32[2,64,256]{2,1,0:T(8,128)S(1)}, f32[2,64,256]{2,1,0:T(8,128)S(1)}, u32[]{:S(2)}, u32[]{:S(2)}) collective-permute-start(f32[2,64,256]{2,1,0:T(8,128)S(1)} %get-tuple-element.596), channel_id=1, source_target_pairs={{4,0},{8,4},{12,8},{16,12},{20,16},{24,20},{28,24},{5,1},{9,5},{13... | collective-permute-start | bytes 393224 | tf_op jit(solution)/shard_map/ppermute | solution.py:24
  10.4 2.3 copy-start.7
  12.7 1.9 copy-start.8
  14.6 1.0 copy-start
  15.9 12.3 %collective-permute-start.2 = (f32[2,384,64]{2,1,0:T(8,128)S(1)}, f32[2,384,64]{2,1,0:T(8,128)S(1)}, u32[]{:S(2)}, u32[]{:S(2)}) collective-permute-start(f32[2,384,64]{2,1,0:T(8,128)S(1)} %get-tuple-element.592), channel_id=1, source_target_pairs={{0,1},{1,2},{2,3},{4,5},{5,6},{6,7},{8,9},{9,10},{10,11},{12,13},{... | collective-permute-start | bytes 589832 | tf_op jit(solution)/shard_map/ppermute | solution.py:23
  20.3 12.7 %collective-permute-start.3 = (f32[2,384,64]{2,1,0:T(8,128)S(1)}, f32[2,384,64]{2,1,0:T(8,128)S(1)}, u32[]{:S(2)}, u32[]{:S(2)}) collective-permute-start(f32[2,384,64]{2,1,0:T(8,128)S(1)} %get-tuple-element.593), channel_id=1, source_target_pairs={{1,0},{2,1},{3,2},{5,4},{6,5},{7,6},{9,8},{10,9},{11,10},{13,12},{... | collective-permute-start | bytes 589832 | tf_op jit(solution)/shard_map/ppermute | solution.py:24
  34.5 1.1 copy-start.9
  108.1 3.8 collective-permute-start.4
  110.6 3.3 collective-permute-start.5
  114.1 7.4 %collective-permute-start.6 = (f32[2,256,64]{2,1,0:T(8,128)S(1)}, f32[2,256,64]{2,1,0:T(8,128)S(1)}, u32[]{:S(2)}, u32[]{:S(2)}) collective-permute-start(f32[2,256,64]{2,1,0:T(8,128)S(1)} %get-tuple-element.591), channel_id=1, source_target_pairs={{0,1},{1,2},{2,3},{4,5},{5,6},{6,7},{8,9},{9,10},{10,11},{12,13},{... | collective-permute-start | bytes 393224 | tf_op jit(solution)/shard_map/ppermute | solution.py:23
  115.8 15.3 %copy-start.1 = (f32[2,256,256]{2,1,0:T(8,128)S(1)}, f32[2,256,256]{2,1,0:T(8,128)}, u32[]{:S(2)}) copy-start(f32[2,256,256]{2,1,0:T(8,128)} %param.25) | copy-start | bytes 1572868
  115.8 14.0 %collective-permute-start.7 = (f32[2,256,64]{2,1,0:T(8,128)S(1)}, f32[2,256,64]{2,1,0:T(8,128)S(1)}, u32[]{:S(2)}, u32[]{:S(2)}) collective-permute-start(f32[2,256,64]{2,1,0:T(8,128)S(1)} %get-tuple-element.590), channel_id=1, source_target_pairs={{1,0},{2,1},{3,2},{5,4},{6,5},{7,6},{9,8},{10,9},{11,10},{13,12},{... | collective-permute-start | bytes 393224 | tf_op jit(solution)/shard_map/ppermute | solution.py:24
  131.1 87.1 %copy-start.3 = (f32[2,256,256]{2,1,0:T(8,128)}, f32[2,256,256]{2,1,0:T(8,128)S(1)}, u32[]{:S(2)}) copy-start(f32[2,256,256]{2,1,0:T(8,128)S(1)} %scatter-add.31) | copy-start | bytes 1572868
  218.2 22.5 %copy-start.5 = (f32[2,256,256]{2,1,0:T(8,128)}, f32[2,256,256]{2,1,0:T(8,128)S(1)}, u32[]{:S(2)}) copy-start(f32[2,256,256]{2,1,0:T(8,128)S(1)} %multiply_add_fusion.2) | copy-start | bytes 1572868
  218.3 2.6 collective-permute-start.8
  219.6 5.7 %collective-permute-start.9 = (f32[2,64,256]{2,1,0:T(8,128)S(1)}, f32[2,64,256]{2,1,0:T(8,128)S(1)}, u32[]{:S(2)}, u32[]{:S(2)}) collective-permute-start(f32[2,64,256]{2,1,0:T(8,128)S(1)} %get-tuple-element.595), channel_id=1, source_target_pairs={{4,0},{8,4},{12,8},{16,12},{20,16},{24,20},{28,24},{5,1},{9,5},{13... | collective-permute-start | bytes 393224 | tf_op jit(solution)/shard_map/ppermute | solution.py:24
  225.5 10.5 %collective-permute-start.10 = (f32[2,384,64]{2,1,0:T(8,128)S(1)}, f32[2,384,64]{2,1,0:T(8,128)S(1)}, u32[]{:S(2)}, u32[]{:S(2)}) collective-permute-start(f32[2,384,64]{2,1,0:T(8,128)S(1)} %get-tuple-element.588), channel_id=1, source_target_pairs={{0,1},{1,2},{2,3},{4,5},{5,6},{6,7},{8,9},{9,10},{10,11},{12,13},{... | collective-permute-start | bytes 589832 | tf_op jit(solution)/shard_map/ppermute | solution.py:23
  229.2 11.5 %collective-permute-start.11 = (f32[2,384,64]{2,1,0:T(8,128)S(1)}, f32[2,384,64]{2,1,0:T(8,128)S(1)}, u32[]{:S(2)}, u32[]{:S(2)}) collective-permute-start(f32[2,384,64]{2,1,0:T(8,128)S(1)} %get-tuple-element.589), channel_id=1, source_target_pairs={{1,0},{2,1},{3,2},{5,4},{6,5},{7,6},{9,8},{10,9},{11,10},{13,12},{... | collective-permute-start | bytes 589832 | tf_op jit(solution)/shard_map/ppermute | solution.py:24
  316.6 3.8 collective-permute-start.12
  319.1 3.3 collective-permute-start.13
  322.6 7.4 %collective-permute-start.14 = (f32[2,256,64]{2,1,0:T(8,128)S(1)}, f32[2,256,64]{2,1,0:T(8,128)S(1)}, u32[]{:S(2)}, u32[]{:S(2)}) collective-permute-start(f32[2,256,64]{2,1,0:T(8,128)S(1)} %get-tuple-element.587), channel_id=1, source_target_pairs={{0,1},{1,2},{2,3},{4,5},{5,6},{6,7},{8,9},{9,10},{10,11},{12,13},{... | collective-permute-start | bytes 393224 | tf_op jit(solution)/shard_map/ppermute | solution.py:23
  324.1 13.3 %copy-start.6 = (f32[2,256,256]{2,1,0:T(8,128)S(1)}, f32[2,256,256]{2,1,0:T(8,128)}, u32[]{:S(2)}) copy-start(f32[2,256,256]{2,1,0:T(8,128)} %copy-done.5) | copy-start | bytes 1572868
  324.2 11.9 %collective-permute-start.15 = (f32[2,256,64]{2,1,0:T(8,128)S(1)}, f32[2,256,64]{2,1,0:T(8,128)S(1)}, u32[]{:S(2)}, u32[]{:S(2)}) collective-permute-start(f32[2,256,64]{2,1,0:T(8,128)S(1)} %get-tuple-element.586), channel_id=1, source_target_pairs={{1,0},{2,1},{3,2},{5,4},{6,5},{7,6},{9,8},{10,9},{11,10},{13,12},{... | collective-permute-start | bytes 393224 | tf_op jit(solution)/shard_map/ppermute | solution.py:24
  331.3 51.3 %copy-start.2 = (f32[2,256,256]{2,1,0:T(8,128)S(1)}, f32[2,256,256]{2,1,0:T(8,128)}, u32[]{:S(2)}) copy-start(f32[2,256,256]{2,1,0:T(8,128)} %param.25) | copy-start | bytes 1572868
  331.3 51.3 %copy-start.4 = (f32[2,256,256]{2,1,0:T(8,128)S(1)}, f32[2,256,256]{2,1,0:T(8,128)}, u32[]{:S(2)}) copy-start(f32[2,256,256]{2,1,0:T(8,128)} %copy-done.3) | copy-start | bytes 1572868
where the time goes:
time: 389 us; the launch traced here: 384 us
  blocking collectives  126 us (32%)
  local copies, waits for them, and re-layouts  75.5 us (19%)
  other arithmetic  48.2 us (12%)
  waiting for transfers between devices  47 us (12%)
  matrix products  33.6 us (9%)
  starting transfers between devices  27.6 us (7%)
  loops' own time  21 us (5%)
  between operations  4.87 us (1%)
    psum x3, blocking collectives, global_sum(): return lax.psum(value, ('wide', 'narrow'))  126 us
    dynamic_update_slice x6, local copies, waits for them, and re-layouts, visit(): lax.dynamic_update_slice(running, region + contribution[0], (0, row_start...  37.7 us
    dot_general x12, matrix products, right_apply(): jnp.einsum('nqac,qpcd->npad', values, table, preferred_element_type=jnp.f...  33.6 us
    ppermute x8, waiting for transfers between devices, padded(): after = lax.ppermute(initial, axis, down)  27.7 us
    another operation x2, loops' own time, apply_operator(): lax.fori_loop(0, counts[0, 0], visit, (total, jnp.float32(0.0)))  21 us
    ppermute x8, waiting for transfers between devices, padded(): before = lax.ppermute(last, axis, up)  19.3 us
    ppermute x8, starting transfers between devices, padded(): before = lax.ppermute(last, axis, up)  17 us
    another operation x11, other arithmetic  13.1 us
  transfers between devices with their start and end apart: 16, of which 11 were waited for; matrix products, arithmetic and copies ran while one was open for 5% of the time, Pallas kernels for 0%

commit v1 on v0

v1 whole, which is shorter than its diff:
```python
import functools
import math

import jax
import jax.numpy as jnp
import numpy as np
from jax import lax
from jax.experimental import pallas as pl
from jax.experimental.pallas import tpu as pltpu
from jax.sharding import PartitionSpec as P

HALO = 64
SPARE = 8
damping = 0.5
F32 = jnp.float32
BF16 = jnp.bfloat16
VMEM_LIMIT = 48 * 1024 * 1024


def pairs(size, odd):
    found = []
    for i in range(odd, size - 1, 2):
        found += [(i, i + 1), (i + 1, i)]
    return found


def swap(x, axis, odd):
    wanted = pairs(lax.axis_size(axis), odd)
    if not wanted:
        return jnp.zeros_like(x)
    return lax.ppermute(x, axis, wanted)


def half_tables(length):
    counter = np.arange(length)
    angles = ((counter[:, None] * counter[None, :]) % length).astype(np.float32)
    angles = angles * np.float32(2.0 * math.pi / length)
    factor = np.float32(1.0 / math.sqrt(length))
    cos, sin = (np.cos(angles) * factor, np.sin(angles) * factor)
    half = length // 2
    tables = []
    for parity in (0, 1):
        c, s = (cos[parity::2, :half], sin[parity::2, :half])
        left = np.concatenate([np.concatenate([c, s], 1), np.concatenate([-s, c], 1)], 0)
        tables += [left, left.T]
    return jnp.asarray(np.stack(tables), BF16)


def sorting_tables(length):
    order = np.concatenate([np.arange(0, length, 2), np.arange(1, length, 2)])
    left = np.zeros((length, length), np.float32)
    left[np.arange(length), order] = 1.0
    return jnp.asarray(np.stack([left, left.T]), BF16)


def dot(a, b):
    return jnp.dot(a, b, preferred_element_type=F32)


def cat(parts, axis):
    return jnp.concatenate(parts, axis=axis)


def lanes_low(shape):
    return lax.broadcasted_iota(jnp.int32, shape, len(shape) - 1) < shape[-1] // 2


def forward(xr, xi, te, te_t, to, to_t):
    h = xr.shape[0] // 2
    even = cat([xr[:h] + xr[h:], xi[:h] + xi[h:]], 0).astype(BF16)
    odd = cat([xr[:h] - xr[h:], xi[:h] - xi[h:]], 0).astype(BF16)
    ye, yo = (dot(te, even), dot(to, odd))
    plus, minus = ([], [])
    for y in (ye, yo):
        yr, yi = (y[:h], y[h:])
        plus.append(cat([yr[:, :h] + yr[:, h:], yi[:, :h] + yi[:, h:]], 1))
        minus.append(cat([yr[:, :h] - yr[:, h:], yi[:, :h] - yi[:, h:]], 1))
    ze = dot(cat(plus, 0).astype(BF16), te_t)
    zo = dot(cat(minus, 0).astype(BF16), to_t)
    return (ze, zo)


def inverse(ve, vo, te, te_t, to, to_t):
    h = ve.shape[0] // 2
    top = cat([cat([ve[:h, :h], vo[:h, :h]], 1), cat([ve[:h, h:], vo[:h, h:]], 1)], 0)
    low = cat([cat([ve[h:, :h], vo[h:, :h]], 1), cat([ve[h:, h:], vo[h:, h:]], 1)], 0)
    a, b = (dot(te_t, top), dot(to_t, low))
    s, d = (a + b, a - b)
    le = cat([cat([s[:h, :h], s[h:, :h]], 1), cat([d[:h, :h], d[h:, :h]], 1)], 0).astype(BF16)
    lo = cat([cat([s[:h, h:], s[h:, h:]], 1), cat([d[:h, h:], d[h:, h:]], 1)], 0).astype(BF16)
    p, q = (dot(le, te), dot(lo, to))
    s, d = (p + q, p - q)
    return (cat([s[:, :h], d[:, :h]], 1), cat([s[:, h:], d[:, h:]], 1))


def shifted_place(offsets, k, span):
    row = HALO + offsets[2 * k]
    col = offsets[2 * k + 1]
    group = pl.multiple_of(row // 8 * 8, 8)
    blocks = span // 128
    first = jnp.where(col < 0, blocks - 1, 0)
    places = [
        pl.multiple_of(lax.rem(first + i, blocks) * 128, 128) for i in range(blocks)
    ]
    return (group, row - group, places, jnp.where(col < 0, col + 128, col))


def take_patch(ext, offsets, k, width, patch):
    group, down, places, across = shifted_place(offsets, k, ext.shape[2])
    groups = width // 8
    sub = lax.broadcasted_iota(jnp.int32, (groups, 8, 128), 1)
    lane = lax.broadcasted_iota(jnp.int32, (width, 128), 1)
    for q in range(2):
        turned = []
        for place in places:
            x = ext[q, pl.ds(group, width + 8), pl.ds(place, 128)].reshape(groups + 1, 8, 128)
            x = pltpu.roll(x, lax.rem(8 - down, 8), 1)
            x = jnp.where(sub < 8 - down, x[:-1], x[1:]).reshape(width, 128)
            turned.append(pltpu.roll(x, lax.rem(128 - across, 128), 1))
        for i in range(width // 128):
            patch[q, :, 128 * i : 128 * (i + 1)] = jnp.where(
                lane < 128 - across, turned[i], turned[i + 1]
            )


def project(patch, probe, weights, k, tables):
    te, te_t, to, to_t = (tables[i] for i in range(4))
    xr, xi = (patch[0], patch[1])
    width = xr.shape[0]
    h = width // 2
    total_e = total_o = None
    for m in range(probe.shape[0]):
        pr, pi = (probe[m, 0].astype(F32), probe[m, 1].astype(F32))
        ze, zo = forward(pr * xr - pi * xi, pr * xi + pi * xr, te, te_t, to, to_t)
        ze = ze * weights[k, m, :, :width].astype(F32)
        zo = zo * weights[k, m, :, width:].astype(F32)
        total_e = ze if m == 0 else total_e + ze
        total_o = zo if m == 0 else total_o + zo
    return (total_e[:, :h] + total_e[:, h:], total_o[:, :h] + total_o[:, h:])


def back_project(pe, po, probe, weights, k, tables):
    te, te_t, to, to_t = (tables[i] for i in range(4))
    width = pe.shape[0]
    pe2, po2 = (cat([pe, pe], 1), cat([po, po], 1))
    cr = ci = None
    for m in range(probe.shape[0]):
        ve = (weights[k, m, :, :width].astype(F32) * pe2).astype(BF16)
        vo = (weights[k, m, :, width:].astype(F32) * po2).astype(BF16)
        nr, ni = inverse(ve, vo, te, te_t, to, to_t)
        pr, pi = (probe[m, 0].astype(F32), probe[m, 1].astype(F32))
        r = pr * nr + pi * ni
        i = pr * ni - pi * nr
        cr = r if m == 0 else cr + r
        ci = i if m == 0 else ci + i
    return (cr, ci)


def put_patch(total, offsets, k, parts):
    width = parts[0].shape[0]
    group, down, places, across = shifted_place(offsets, k, total.shape[2])
    groups = width // 8
    sub = lax.broadcasted_iota(jnp.int32, (groups + 1, 8, 128), 1)
    lane = lax.broadcasted_iota(jnp.int32, (width + 8, 128), 1)
    none = jnp.zeros((1, 8, 128), F32)
    for q in range(2):
        turned = [jnp.zeros((width + 8, 128), F32)]
        for i in range(width // 128):
            x = parts[q][:, 128 * i : 128 * (i + 1)].reshape(groups, 8, 128)
            x = pltpu.roll(x, down, 1)
            x = jnp.where(sub < down, cat([none, x], 0), cat([x, none], 0))
            turned.append(pltpu.roll(x.reshape(width + 8, 128), across, 1))
        turned.append(turned[0])
        for i, place in enumerate(places):
            total[q, pl.ds(group, width + 8), pl.ds(place, 128)] += jnp.where(
                lane < across, turned[i], turned[i + 1]
            )


def square_sum(x):
    return jnp.sum(x * x)


def scalar_tile(values):
    rows = lax.broadcasted_iota(jnp.int32, (8, 128), 0)
    tile = jnp.zeros((8, 128), F32)
    for i, value in enumerate(values):
        tile = jnp.where(rows == i, value, tile)
    return tile


def parity_of(axis):
    return lax.rem(lax.axis_index(axis), 2)


def by_parity(axis, low, high, first, second):
    even = parity_of(axis) == 0

    @pl.when(even)
    def _():
        first(high())
        second(low())

    @pl.when(jnp.logical_not(even))
    def _():
        first(low())
        second(high())


def store(ref):
    def put(value):
        ref[...] = value

    return put


def halo_rows_kernel(g, first, second):
    n = g.shape[1]
    by_parity(
        "wide", lambda: g[:, :HALO], lambda: g[:, n - HALO :], store(first), store(second)
    )


def strip_low(x, width):
    low = lanes_low((x.shape[1], 2 * HALO))
    re, im = (x[0, :, : 2 * HALO], x[1, :, : 2 * HALO])
    return jnp.where(low, re, pltpu.roll(im, HALO, 1))


def strip_high(x, width):
    low = lanes_low((x.shape[1], 2 * HALO))
    re, im = (x[0, :, width - 2 * HALO : width], x[1, :, width - 2 * HALO : width])
    return jnp.where(low, pltpu.roll(im, HALO, 1), re)


def fill_rows(ext, g, first, second):
    n, width = (g.shape[1], g.shape[2])
    even = parity_of("wide") == 0
    above = jnp.where(even, second[...], first[...])
    below = jnp.where(even, first[...], second[...])
    ext[:, :HALO, :width] = above
    ext[:, HALO : HALO + n, :width] = g[...]
    ext[:, HALO + n : 2 * HALO + n, :width] = below


def halo_cols_kernel(g, first, second, out_first, out_second, ext):
    width = g.shape[2]
    fill_rows(ext, g, first, second)
    by_parity(
        "narrow",
        lambda: strip_low(ext, width),
        lambda: strip_high(ext, width),
        store(out_first),
        store(out_second),
    )


def fill_cols(ext, width, first, second):
    even = parity_of("narrow") == 0
    right = jnp.where(even, first[...], second[...])
    left = jnp.where(even, second[...], first[...])
    low = lanes_low(right.shape)
    tall = right.shape[0]
    ext[0, :tall, width:] = jnp.where(low, right, left)
    ext[1, :tall, width:] = pltpu.roll(jnp.where(low, left, right), HALO, 1)


def sort_weights_kernel(w, sorter, out):
    width = w.shape[-1]
    h = width // 2
    re = dot(dot(sorter[0], w[0, 0, 0]).astype(BF16), sorter[1])
    im = dot(dot(sorter[0], w[0, 0, 1]).astype(BF16), sorter[1])
    out[0, 0] = cat([re[:, :h], im[:, :h], re[:, h:], im[:, h:]], 1).astype(BF16)


def first_pass_kernel(
    count, offsets, g, row1, row2, col1, col2, probe, weights, tables,
    total, sums, sr1, sr2, si1, si2, ext, patch,
):
    width = g.shape[2]
    fill_rows(ext, g, row1, row2)
    fill_cols(ext, width, col1, col2)
    total[...] = jnp.zeros_like(total)

    def visit(k, energy):
        take_patch(ext, offsets, k, width, patch)
        pe, po = project(patch, probe, weights, k, tables)
        put_patch(total, offsets, k, back_project(pe, po, probe, weights, k, tables))
        return energy + square_sum(pe) + square_sum(po)

    energy = lax.fori_loop(0, count[0], visit, F32(0.0))
    sums[...] = scalar_tile([square_sum(g[...]), energy])
    send_row_bands(total, 0, sr1, sr2)
    send_col_bands(total, 1, si1, si2)


def send_row_bands(total, q, first, second):
    n = total.shape[1] - SPARE
    by_parity(
        "wide",
        lambda: total[q, : 2 * HALO],
        lambda: total[q, n - 2 * HALO : n],
        store(first),
        store(second),
    )


def send_col_bands(total, q, first, second):
    n = total.shape[1] - SPARE
    width = total.shape[2] - 2 * HALO
    low = lanes_low((n, 2 * HALO))
    by_parity(
        "narrow",
        lambda: jnp.where(low, total[q, :n, : 2 * HALO], total[q, :n, width:]),
        lambda: jnp.where(low, total[q, :n, width:], total[q, :n, width - 2 * HALO : width]),
        store(first),
        store(second),
    )


def add_row_bands(total, q, first, second):
    n = total.shape[1] - SPARE
    even = parity_of("wide") == 0
    total[q, : 2 * HALO] += jnp.where(even, second[...], first[...])
    total[q, n - 2 * HALO : n] += jnp.where(even, first[...], second[...])


def add_col_bands(total, q, first, second):
    n = total.shape[1] - SPARE
    width = total.shape[2] - 2 * HALO
    even = parity_of("narrow") == 0
    right = jnp.where(even, first[...], second[...])
    left = jnp.where(even, second[...], first[...])
    low = lanes_low(right.shape)
    total[q, :n, width:] += jnp.where(low, right, left)
    total[q, :n, : 2 * HALO] += jnp.where(low, left, 0.0)
    total[q, :n, width - 2 * HALO : width] += jnp.where(low, 0.0, right)


def bands_kernel(total, rr1, rr2, ri1, ri2, out, sr1, sr2, si1, si2):
    out[...] = total[...]
    add_row_bands(out, 0, rr1, rr2)
    add_col_bands(out, 1, ri1, ri2)
    send_col_bands(out, 0, sr1, sr2)
    send_row_bands(out, 1, si1, si2)


def second_forward_kernel(
    last_row, last_col, count, offsets, total, rr1, rr2, ri1, ri2, sums, probe, weights, tables,
    image, projected, all_sums, ext, patch,
):
    width = image.shape[2]
    n = total.shape[1] - SPARE
    ext[...] = total[...]
    add_col_bands(ext, 0, rr1, rr2)
    add_row_bands(ext, 1, ri1, ri2)

    @pl.when(lax.axis_index("wide") == 0)
    def _():
        ext[:, :HALO] = jnp.zeros((2, HALO, ext.shape[2]), F32)

    @pl.when(lax.axis_index("wide") == last_row)
    def _():
        ext[:, n - HALO : n] = jnp.zeros((2, HALO, ext.shape[2]), F32)

    low = lanes_low((2, n, 2 * HALO))
    @pl.when(lax.axis_index("narrow") == 0)
    def _():
        ext[:, :n, width:] = jnp.where(low, ext[:, :n, width:], 0.0)

    @pl.when(lax.axis_index("narrow") == last_col)
    def _():
        ext[:, :n, width:] = jnp.where(low, 0.0, ext[:, :n, width:])

    core = ext[:, HALO : n - HALO, :width]
    image[...] = core

    def visit(k, energy):
        take_patch(ext, offsets, k, width, patch)
        pe, po = project(patch, probe, weights, k, tables)
        projected[k] = cat([pe, po], 1)
        return energy + square_sum(pe) + square_sum(po)

    energy = lax.fori_loop(0, count[0], visit, F32(0.0))
    rows = lax.broadcasted_iota(jnp.int32, (8, 128), 0)
    all_sums[...] = jnp.where(
        rows == 2, square_sum(core), jnp.where(rows == 3, energy, sums[...])
    )


def second_backward_kernel(
    count, offsets, projected, probe, weights, tables, total, first, second
):
    total[...] = jnp.zeros_like(total)
    h = projected.shape[2] // 2
    n = total.shape[1] - SPARE

    def visit(k, carried):
        pe, po = (projected[k, :, :h], projected[k, :, h:])
        put_patch(total, offsets, k, back_project(pe, po, probe, weights, k, tables))
        return carried

    lax.fori_loop(0, count[0], visit, 0)
    by_parity(
        "wide",
        lambda: total[:, :HALO],
        lambda: total[:, n - HALO : n],
        store(first),
        store(second),
    )


def fold_rows_kernel(total, first, second, middle, out_first, out_second):
    n = middle.shape[1]
    width = middle.shape[2] - 2 * HALO
    even = parity_of("wide") == 0
    middle[...] = total[:, HALO : HALO + n]
    middle[:, :HALO] += jnp.where(even, second[...], first[...])
    middle[:, n - HALO :] += jnp.where(even, first[...], second[...])
    low = lanes_low((n, 2 * HALO))
    re, im = (middle[0, :, width:], middle[1, :, width:])
    im = pltpu.roll(im, HALO, 1)
    by_parity(
        "narrow",
        lambda: jnp.where(low, im, re),
        lambda: jnp.where(low, re, im),
        store(out_first),
        store(out_second),
    )


def finish_kernel(g, image, middle, first, second, sums, solved, left_over):
    width = g.shape[2]
    even = parity_of("narrow") == 0
    right = jnp.where(even, first[...], second[...])
    left = jnp.where(even, second[...], first[...])
    low = lanes_low(right.shape)
    n0, s0, uu, s1 = (sums[i : i + 1, :1] for i in range(4))
    mu = s0 / n0
    a0 = n0 / (s0 + damping * n0)
    n1 = a0 * a0 * (uu - mu * s0)
    b = n1 / n0
    c1 = a0 * mu + b
    curve = damping * (n1 + b * b * n0) + c1 * c1 * s0 - 2.0 * c1 * a0 * uu + a0 * a0 * s1
    a1 = n1 / curve
    for q in range(2):
        u = image[q]
        v = middle[q, :, :width]
        if q == 0:
            low_part, high_part = (left, right)
        else:
            low_part, high_part = (pltpu.roll(left, HALO, 1), pltpu.roll(right, HALO, 1))
        v = cat(
            [
                v[:, : 2 * HALO] + jnp.where(low, low_part, 0.0),
                v[:, 2 * HALO : width - 2 * HALO],
                v[:, width - 2 * HALO :] + jnp.where(low, 0.0, high_part),
            ],
            1,
        ) if width > 4 * HALO else cat(
            [
                v[:, : 2 * HALO] + jnp.where(low, low_part, 0.0),
                v[:, width - 2 * HALO :] + jnp.where(low, 0.0, high_part),
            ],
            1,
        )
        d1 = c1 * g[q] - a0 * u
        r1 = a0 * (mu * g[q] - u)
        solved[q] = a0 * g[q] + a1 * d1
        left_over[q] = r1 - a1 * (damping * d1 + c1 * u - a0 * v)


def reduce_all(x):
    for axis in ("wide", "narrow"):
        size = lax.axis_size(axis)
        if size & (size - 1):
            x = lax.psum(x, axis)
            continue
        step = 1
        while step < size:
            x = x + lax.ppermute(x, axis, [(i, i ^ step) for i in range(size)])
            step *= 2
    return x


def shape(*dims):
    return jax.ShapeDtypeStruct(dims, F32)


def call(kernel, outs, smem, args, scratch=(), flops=0):
    specs = [pl.BlockSpec(memory_space=pltpu.SMEM)] * smem
    specs += [pl.BlockSpec(memory_space=pltpu.VMEM)] * (len(args) - smem)
    moved = sum(a.size * a.dtype.itemsize for a in args) + sum(4 * o.size for o in outs)
    return pl.pallas_call(
        kernel,
        out_shape=outs,
        in_specs=specs,
        out_specs=[pl.BlockSpec(memory_space=pltpu.VMEM)] * len(outs),
        scratch_shapes=list(scratch),
        compiler_params=pltpu.CompilerParams(vmem_limit_bytes=VMEM_LIMIT),
        cost_estimate=pl.CostEstimate(flops=flops, bytes_accessed=moved, transcendentals=0),
    )(*args)


def sort_weights(w):
    slots, modes, parts, rows, cols = w.shape
    return pl.pallas_call(
        sort_weights_kernel,
        out_shape=jax.ShapeDtypeStruct((slots, modes, rows, parts * cols), BF16),
        grid=(slots, modes),
        in_specs=[
            pl.BlockSpec((1, 1, parts, rows, cols), lambda k, m: (k, m, 0, 0, 0)),
            pl.BlockSpec((2, rows, cols), lambda k, m: (0, 0, 0)),
        ],
        out_specs=pl.BlockSpec((1, 1, rows, parts * cols), lambda k, m: (k, m, 0, 0)),
        cost_estimate=pl.CostEstimate(
            flops=8 * slots * modes * rows * cols * rows,
            bytes_accessed=4 * w.size,
            transcendentals=0,
        ),
    )(w, sorting_tables(cols))


def local(gradient, probe_modes, mode_weights, offsets, counts):
    weights = mode_weights[0, 0]
    slots, modes = weights.shape[:2]
    rows, width = gradient.shape[1:]
    tall, broad = (rows + 2 * HALO, width + 2 * HALO)
    stored = tall + SPARE
    offsets = offsets.reshape(-1)
    counts = counts.reshape(-1)
    tables = half_tables(width)
    pass_flops = 8 * 2 * slots * modes * 2 * width * width * width
    extended = pltpu.VMEM((2, stored, broad), F32)
    patch = pltpu.VMEM((2, rows, width), F32)

    row_sends = call(halo_rows_kernel, [shape(2, HALO, width)] * 2, 0, [gradient])
    row1, row2 = (swap(x, "wide", i) for i, x in enumerate(row_sends))
    sorted_weights = sort_weights(weights)
    col_sends = call(
        halo_cols_kernel, [shape(tall, 2 * HALO)] * 2, 0, [gradient, row1, row2],
        [pltpu.VMEM((2, tall, width), F32)],
    )
    col1, col2 = (swap(x, "narrow", i) for i, x in enumerate(col_sends))

    row_band, col_band = (shape(2 * HALO, broad), shape(tall, 2 * HALO))
    total, sums, sr1, sr2, si1, si2 = call(
        first_pass_kernel,
        [shape(2, stored, broad), shape(8, 128), row_band, row_band, col_band, col_band],
        2,
        [counts, offsets, gradient, row1, row2, col1, col2, probe_modes, sorted_weights, tables],
        [extended, patch],
        pass_flops,
    )
    total, sr1, sr2, si1, si2 = call(
        bands_kernel,
        [shape(2, stored, broad), col_band, col_band, row_band, row_band],
        0,
        [total, swap(sr1, "wide", 0), swap(sr2, "wide", 1), swap(si1, "narrow", 0), swap(si2, "narrow", 1)],
    )
    image, projected, sums = call(
        functools.partial(
            second_forward_kernel, lax.axis_size("wide") - 1, lax.axis_size("narrow") - 1
        ),
        [shape(2, rows, width), shape(slots, rows, width), shape(8, 128)],
        2,
        [
            counts, offsets, total,
            swap(sr1, "narrow", 0), swap(sr2, "narrow", 1), swap(si1, "wide", 0), swap(si2, "wide", 1),
            sums, probe_modes, sorted_weights, tables,
        ],
        [extended, patch],
        pass_flops // 2,
    )
    sums = reduce_all(sums)
    total, f1, f2 = call(
        second_backward_kernel,
        [shape(2, stored, broad), shape(2, HALO, broad), shape(2, HALO, broad)],
        2,
        [counts, offsets, projected, probe_modes, sorted_weights, tables],
        [],
        pass_flops // 2,
    )
    middle, f1, f2 = call(
        fold_rows_kernel,
        [shape(2, rows, broad), shape(rows, 2 * HALO), shape(rows, 2 * HALO)],
        0,
        [total, swap(f1, "wide", 0), swap(f2, "wide", 1)],
    )
    solved, left_over = call(
        finish_kernel,
        [shape(2, rows, width)] * 2,
        0,
        [gradient, image, middle, swap(f1, "narrow", 0), swap(f2, "narrow", 1), sums],
    )
    return (solved, left_over)


def solution(mesh):
    placed = (
        P(None, "wide", "narrow"),
        P(),
        P("wide", "narrow", None, None, None, None, None),
        P("wide", "narrow", None, None),
        P("wide", "narrow"),
    )
    return jax.shard_map(
        local,
        mesh=mesh,
        in_specs=placed,
        out_specs=(P(None, "wide", "narrow"), P(None, "wide", "narrow")),
        check_vma=False,
    )
```

time: 389 us -> 105 us (0.27); the launches traced: 384 us -> 104 us
  blocking collectives: 126 us -> 0 us
  local copies, waits for them, and re-layouts: 75.5 us -> 1.23 us
  other arithmetic: 48.2 us -> 0.02 us
  matrix products: 33.6 us -> 0 us
  starting transfers between devices: 27.6 us -> 58 us
  waiting for transfers between devices: 47 us -> 17.8 us
  Pallas kernels: 0 us -> 25.7 us
  loops' own time: 21 us -> 0 us
    psum x3 -> x0, blocking collectives: 126 us -> none  [global_sum(): return lax.psum(value, ('wide', 'narrow'))]
    dynamic_update_slice x6 -> x0, local copies, waits for them, and re-layouts: 37.7 us -> none  [visit(): lax.dynamic_update_slice(running, region + contribution[0], (0, row_start...]
    dot_general x12 -> x0, matrix products: 33.6 us -> none  [right_apply(): jnp.einsum('nqac,qpcd->npad', values, table, preferred_element_type=jnp.f...]
    ppermute x16 -> x21, starting transfers between devices: 27.6 us -> 58 us  [the longest x16 42.5 us: swap(): return lax.ppermute(x, axis, wanted)]
    ppermute x16 -> x21, waiting for transfers between devices: 47 us -> 17.8 us  [the longest x16 9.06 us: swap(): return lax.ppermute(x, axis, wanted)]
    another operation x27 -> x0, other arithmetic: 26.9 us -> none
    pallas_call x0 -> x9, Pallas kernels: none -> 25.7 us  [the longest x8 15.4 us: call(): pl.pallas_call(kernel, out_shape=outs, in_specs=specs, out_specs=[pl.Bloc...]
    another operation x2 -> x0, loops' own time: 21 us -> none  [apply_operator(): lax.fori_loop(0, counts[0, 0], visit, (total, jnp.float32(0.0)))]
  transfers between devices with their start and end apart: 16 -> 21, of which waited for: 11 -> 9; matrix products, arithmetic and copies ran while one was open for 5% -> 0% of each run, Pallas kernels for 0% -> 10%
where the time goes in v1:
time: 105 us; the launch traced here: 104 us
  starting transfers between devices  58 us (55%)
  Pallas kernels  25.7 us (24%)
  waiting for transfers between devices  17.8 us (17%)
  between operations  1.49 us (1%)
  local copies, waits for them, and re-layouts  1.23 us (1%)
    ppermute x16, starting transfers between devices, swap(): return lax.ppermute(x, axis, wanted)  42.5 us
    ppermute x5, starting transfers between devices, reduce_all(): x = x + lax.ppermute(x, axis, [(i, i ^ step) for i in range(size)])  15.4 us
    pallas_call x8, Pallas kernels, call(): pl.pallas_call(kernel, out_shape=outs, in_specs=specs, out_specs=[pl.Bloc...  15.4 us
    pallas_call x1, Pallas kernels, sort_weights(): pl.pallas_call(sort_weights_kernel, out_shape=jax.ShapeDtypeStruct((slots...  10.3 us
    ppermute x16, waiting for transfers between devices, swap(): return lax.ppermute(x, axis, wanted)  9.06 us
    ppermute x5, waiting for transfers between devices, reduce_all(): x = x + lax.ppermute(x, axis, [(i, i ^ step) for i in range(size)])  8.78 us
  transfers between devices with their start and end apart: 21, of which 9 were waited for; matrix products, arithmetic and copies ran while one was open for 0% of the time, Pallas kernels for 10%

profile of v1, /device:TPU:0, one launch (start us, length us, event | category | flops | bytes accessed | tf_op | source)
XLA Modules:
  0.0 104.2 jit_solution(12015991578490549473)
XLA Ops:
  0.6 0.0 copy-start
  0.6 1.0 copy-done
  1.7 0.0 copy-start.4
  1.7 0.5 collective-permute-start
  2.2 0.7 collective-permute-start.1
  2.9 0.3 collective-permute-done.first.row1
  3.2 0.0 collective-permute-done.1.second.row2
  3.2 0.2 shard_map.87
  3.4 3.0 %collective-permute-start.2 = (f32[384,128]{1,0:T(8,128)S(1)}, f32[384,128]{1,0:T(8,128)S(1)}, u32[]{:S(2)}, u32[]{:S(2)}) collective-permute-start(f32[384,128]{1,0:T(8,128)S(1)} %get-tuple-element.28), channel_id=1, source_target_pairs={{0,1},{1,0},{2,3},{3,2},{4,5},{5,4},{6,7},{7,6},{8,9},{9,8},{10,11... | collective-permute-start | bytes 589832 | tf_op jit(solution)/shard_map/ppermute | solution.py:31
  6.4 0.7 collective-permute-start.3
  7.8 0.0 copy-done.4
  7.8 0.1 copy.10
  7.9 0.1 reshape.11.offsets
  7.9 0.0 copy-start.1
  8.0 0.0 copy-start.2
  8.0 0.0 copy-start.3
  8.0 10.3 %shard_map.88.weights = bf16[3,4,256,512]{3,2,1,0:T(8,128)(2,1)} custom-call(bf16[3,4,2,256,256]{4,3,2,1,0:T(8,128)(2,1)} %bitcast.5, bf16[2,256,256]{2,1,0:T(8,128)(2,1)} %constant.5.clone.sorter), custom_call_target="tpu_custom_call" | custom-call | flops 1610612736 | bytes 6291456 | tf_op jit(solution)/shard_map/pallas_call | solution.py:507
  18.3 0.0 collective-permute-done.2.col1
  18.3 0.0 collective-permute-done.3.col2
  18.3 0.0 copy-done.1
  18.3 0.0 copy-done.2
  18.3 0.0 copy-done.3
  18.3 5.4 %shard_map.89 = (f32[2,392,384]{2,1,0:T(8,128)S(1)}, f32[8,128]{1,0:T(8,128)S(1)}, f32[128,384]{1,0:T(8,128)S(1)}, f32[128,384]{1,0:T(8,128)S(1)}, f32[384,128]{1,0:T(8,128)S(1)}, /*index=5*/f32[384,128]{1,0:T(8,128)S(1)}) custom-call(s32[1]{0:T(128)} %bitcast.2.count, s32[6]{0:T(128)S(1)} %reshape.11.offsets, f32[2,256,256]{2,1,0:T(8,128)S(1)} %copy-done.1, ...), custom_call_target="tpu_custom_call" | custom-call | flops 6442450944 | bytes 7893020 | tf_op jit(solution)/shard_map/pallas_call | solution.py:494
  23.7 9.4 %collective-permute-start.4 = (f32[128,384]{1,0:T(8,128)S(1)}, f32[128,384]{1,0:T(8,128)S(1)}, u32[]{:S(2)}, u32[]{:S(2)}) collective-permute-start(f32[128,384]{1,0:T(8,128)S(1)} %get-tuple-element.31), channel_id=1, source_target_pairs={{0,4},{4,0},{8,12},{12,8},{16,20},{20,16},{24,28},{28,24},{1,5},{5... | collective-permute-start | bytes 589832 | tf_op jit(solution)/shard_map/ppermute | solution.py:31
  33.1 0.7 collective-permute-start.5
  33.8 7.2 %collective-permute-start.6 = (f32[384,128]{1,0:T(8,128)S(1)}, f32[384,128]{1,0:T(8,128)S(1)}, u32[]{:S(2)}, u32[]{:S(2)}) collective-permute-start(f32[384,128]{1,0:T(8,128)S(1)} %get-tuple-element.33), channel_id=1, source_target_pairs={{0,1},{1,0},{2,3},{3,2},{4,5},{5,4},{6,7},{7,6},{8,9},{9,8},{10,11... | collective-permute-start | bytes 589832 | tf_op jit(solution)/shard_map/ppermute | solution.py:31
  40.9 0.7 collective-permute-start.7
  41.6 0.0 collective-permute-done.4.rr1
  41.6 0.0 collective-permute-done.5.rr2
  41.6 4.5 %collective-permute-done.6.ri1 = f32[384,128]{1,0:T(8,128)S(1)} collective-permute-done((f32[384,128]{1,0:T(8,128)S(1)}, f32[384,128]{1,0:T(8,128)S(1)}, u32[]{:S(2)}, u32[]{:S(2)}) %collective-permute-start.6) | collective-permute-done | bytes 196640 | tf_op jit(solution)/shard_map/ppermute | solution.py:31
  46.2 0.0 collective-permute-done.7.ri2
  46.2 0.3 shard_map.90
  46.5 4.2 %collective-permute-start.8 = (f32[384,128]{1,0:T(8,128)S(1)}, f32[384,128]{1,0:T(8,128)S(1)}, u32[]{:S(2)}, u32[]{:S(2)}) collective-permute-start(f32[384,128]{1,0:T(8,128)S(1)} %get-tuple-element.36), channel_id=1, source_target_pairs={{0,1},{1,0},{2,3},{3,2},{4,5},{5,4},{6,7},{7,6},{8,9},{9,8},{10,11... | collective-permute-start | bytes 589832 | tf_op jit(solution)/shard_map/ppermute | solution.py:31
  50.7 0.7 collective-permute-start.9
  51.4 0.1 collective-permute-start.10
  51.4 0.7 collective-permute-start.11
  52.1 3.8 %collective-permute-done.8.rr1 = f32[384,128]{1,0:T(8,128)S(1)} collective-permute-done((f32[384,128]{1,0:T(8,128)S(1)}, f32[384,128]{1,0:T(8,128)S(1)}, u32[]{:S(2)}, u32[]{:S(2)}) %collective-permute-start.8) | collective-permute-done | bytes 196640 | tf_op jit(solution)/shard_map/ppermute | solution.py:31
  55.9 0.0 collective-permute-done.9.rr2
  55.9 0.0 collective-permute-done.10.ri1
  55.9 0.0 collective-permute-done.11.ri2
  55.9 4.2 %shard_map.91 = (f32[2,256,256]{2,1,0:T(8,128)S(1)}, f32[3,256,256]{2,1,0:T(8,128)S(1)}, f32[8,128]{1,0:T(8,128)S(1)}) custom-call(s32[1]{0:T(128)} %bitcast.3.count, s32[6]{0:T(128)S(1)} %reshape.11.offsets, f32[2,392,384]{2,1,0:T(8,128)S(1)} %get-tuple-element.35.total, f32[384,128]{1,0:T(8,128)S(1)} %collective-permute-done.8.rr1, ...), custom_call_target="tpu_custom_call" | custom-call | flops 3221225472 | bytes 8028188 | tf_op jit(solution)/shard_map/pallas_call | solution.py:494
  60.1 3.6 %shard_map.92 = (f32[2,392,384]{2,1,0:T(8,128)S(1)}, f32[2,64,384]{2,1,0:T(8,128)S(1)}, f32[2,64,384]{2,1,0:T(8,128)S(1)}) custom-call(s32[1]{0:T(128)} %bitcast.4.count, s32[6]{0:T(128)S(1)} %reshape.11.offsets, f32[3,256,256]{2,1,0:T(8,128)S(1)} %get-tuple-element.42.projected, bf16[4,2,256,256]{3,2,1,0:T(8,128)(2,1)S(1)} %copy-done.2, ...), custom_call_target="tpu_custom_call" | custom-call | flops 3221225472 | bytes 7102492 | tf_op jit(solution)/shard_map/pallas_call | solution.py:494
  63.7 9.0 %collective-permute-start.12 = (f32[2,64,384]{2,1,0:T(8,128)S(1)}, f32[2,64,384]{2,1,0:T(8,128)S(1)}, u32[]{:S(2)}, u32[]{:S(2)}) collective-permute-start(f32[2,64,384]{2,1,0:T(8,128)S(1)} %get-tuple-element.44), channel_id=1, source_target_pairs={{0,4},{4,0},{8,12},{12,8},{16,20},{20,16},{24,28},{28,24},{1,5},{5... | collective-permute-start | bytes 589832 | tf_op jit(solution)/shard_map/ppermute | solution.py:31
  72.8 0.7 collective-permute-start.13
  73.4 0.4 collective-permute-done.12.first
  73.8 0.0 collective-permute-done.13.second
  73.9 0.1 shard_map.93
  74.0 3.8 %collective-permute-start.14 = (f32[256,128]{1,0:T(8,128)S(1)}, f32[256,128]{1,0:T(8,128)S(1)}, u32[]{:S(2)}, u32[]{:S(2)}) collective-permute-start(f32[256,128]{1,0:T(8,128)S(1)} %get-tuple-element.47), channel_id=1, source_target_pairs={{0,1},{1,0},{2,3},{3,2},{4,5},{5,4},{6,7},{7,6},{8,9},{9,8},{10,11... | collective-permute-start | bytes 393224 | tf_op jit(solution)/shard_map/ppermute | solution.py:31
  77.8 0.7 collective-permute-start.15
  78.5 7.4 %collective-permute-start.16 = (f32[8,128]{1,0:T(8,128)S(1)}, f32[8,128]{1,0:T(8,128)S(1)}, u32[]{:S(2)}, u32[]{:S(2)}) collective-permute-start(f32[8,128]{1,0:T(8,128)S(1)} %get-tuple-element.49), channel_id=1, source_target_pairs={{0,4},{4,0},{8,12},{12,8},{16,20},{20,16},{24,28},{28,24},{1,5},{5... | collective-permute-start | bytes 12296 | tf_op jit(solution)/shard_map/ppermute | solution.py:481
  85.9 0.8 collective-permute-done.16
  86.7 0.9 collective-permute-start.17
  87.6 2.7 %collective-permute-done.17 = f32[8,128]{1,0:T(8,128)S(1)} collective-permute-done((f32[8,128]{1,0:T(8,128)S(1)}, f32[8,128]{1,0:T(8,128)S(1)}, u32[]{:S(2)}, u32[]{:S(2)}) %collective-permute-start.17) | collective-permute-done | bytes 4128 | tf_op jit(solution)/shard_map/ppermute | solution.py:481
  90.3 2.7 %collective-permute-start.18 = (f32[8,128]{1,0:T(8,128)S(1)}, f32[8,128]{1,0:T(8,128)S(1)}, u32[]{:S(2)}, u32[]{:S(2)}) collective-permute-start(f32[8,128]{1,0:T(8,128)S(1)} %add.16), channel_id=1, source_target_pairs={{0,16},{4,20},{8,24},{12,28},{16,0},{20,4},{24,8},{28,12},{1,17},{... | collective-permute-start | bytes 12296 | tf_op jit(solution)/shard_map/ppermute | solution.py:481
  93.0 1.6 %collective-permute-done.18 = f32[8,128]{1,0:T(8,128)S(1)} collective-permute-done((f32[8,128]{1,0:T(8,128)S(1)}, f32[8,128]{1,0:T(8,128)S(1)}, u32[]{:S(2)}, u32[]{:S(2)}) %collective-permute-start.18) | collective-permute-done | bytes 4128 | tf_op jit(solution)/shard_map/ppermute | solution.py:481
  94.6 1.8 %collective-permute-start.19 = (f32[8,128]{1,0:T(8,128)S(1)}, f32[8,128]{1,0:T(8,128)S(1)}, u32[]{:S(2)}, u32[]{:S(2)}) collective-permute-start(f32[8,128]{1,0:T(8,128)S(1)} %add.17), channel_id=1, source_target_pairs={{0,1},{1,0},{2,3},{3,2},{4,5},{5,4},{6,7},{7,6},{8,9},{9,8},{10,11... | collective-permute-start | bytes 12296 | tf_op jit(solution)/shard_map/ppermute | solution.py:481
  96.4 1.9 %collective-permute-done.19 = f32[8,128]{1,0:T(8,128)S(1)} collective-permute-done((f32[8,128]{1,0:T(8,128)S(1)}, f32[8,128]{1,0:T(8,128)S(1)}, u32[]{:S(2)}, u32[]{:S(2)}) %collective-permute-start.19) | collective-permute-done | bytes 4128 | tf_op jit(solution)/shard_map/ppermute | solution.py:481
  98.2 2.7 %collective-permute-start.20 = (f32[8,128]{1,0:T(8,128)S(1)}, f32[8,128]{1,0:T(8,128)S(1)}, u32[]{:S(2)}, u32[]{:S(2)}) collective-permute-start(f32[8,128]{1,0:T(8,128)S(1)} %add.18), channel_id=1, source_target_pairs={{0,2},{1,3},{2,0},{3,1},{4,6},{5,7},{6,4},{7,5},{8,10},{9,11},{10,... | collective-permute-start | bytes 12296 | tf_op jit(solution)/shard_map/ppermute | solution.py:481
  101.0 1.8 %collective-permute-done.20 = f32[8,128]{1,0:T(8,128)S(1)} collective-permute-done((f32[8,128]{1,0:T(8,128)S(1)}, f32[8,128]{1,0:T(8,128)S(1)}, u32[]{:S(2)}, u32[]{:S(2)}) %collective-permute-start.20) | collective-permute-done | bytes 4128 | tf_op jit(solution)/shard_map/ppermute | solution.py:481
  102.7 0.0 collective-permute-done.14.first
  102.7 0.0 collective-permute-done.15.second
  102.8 1.5 %shard_map.94 = (f32[2,256,256]{2,1,0:T(8,128)}, f32[2,256,256]{2,1,0:T(8,128)}) custom-call(f32[2,256,256]{2,1,0:T(8,128)S(1)} %copy-done.1, f32[2,256,256]{2,1,0:T(8,128)S(1)} %get-tuple-element.41.image, f32[2,256,384]{2,1,0:T(8,128)S(1)} %get-tuple-element.46.middle, f32[256,128]{1,0:T(8,128)S(1)} %collective-permute-done.14.first, ...), custom_call_target="tpu_custom_call" | custom-call | bytes 3149824 | tf_op jit(solution)/shard_map/pallas_call | solution.py:494
  (6 shorter events, 0.0 us)
Async XLA Ops:
  0.6 1.0 %copy-start = (f32[2,256,256]{2,1,0:T(8,128)S(1)}, f32[2,256,256]{2,1,0:T(8,128)}, u32[]{:S(2)}) copy-start(f32[2,256,256]{2,1,0:T(8,128)} %g.7) | copy-start | bytes 1572868
  1.7 6.1 %copy-start.4 = (s32[1,1,3,2]{2,3,1,0:T(2,128)S(1)}, s32[1,1,3,2]{2,3,1,0:T(2,128)}, u32[]{:S(2)}) copy-start(s32[1,1,3,2]{2,3,1,0:T(2,128)} %param.10) | copy-start | bytes 76
  1.7 1.5 %collective-permute-start = (f32[2,64,256]{2,1,0:T(8,128)S(1)}, f32[2,64,256]{2,1,0:T(8,128)S(1)}, u32[]{:S(2)}, u32[]{:S(2)}) collective-permute-start(f32[2,64,256]{2,1,0:T(8,128)S(1)} %get-tuple-element.26), channel_id=1, source_target_pairs={{0,4},{4,0},{8,12},{12,8},{16,20},{20,16},{24,28},{28,24},{1,5},{5... | collective-permute-start | bytes 393224 | tf_op jit(solution)/shard_map/ppermute | solution.py:31
  2.2 1.0 collective-permute-start.1
  3.4 14.9 %collective-permute-start.2 = (f32[384,128]{1,0:T(8,128)S(1)}, f32[384,128]{1,0:T(8,128)S(1)}, u32[]{:S(2)}, u32[]{:S(2)}) collective-permute-start(f32[384,128]{1,0:T(8,128)S(1)} %get-tuple-element.28), channel_id=1, source_target_pairs={{0,1},{1,0},{2,3},{3,2},{4,5},{5,4},{6,7},{7,6},{8,9},{9,8},{10,11... | collective-permute-start | bytes 589832 | tf_op jit(solution)/shard_map/ppermute | solution.py:31
  6.4 11.9 %collective-permute-start.3 = (f32[384,128]{1,0:T(8,128)S(1)}, f32[384,128]{1,0:T(8,128)S(1)}, u32[]{:S(2)}, u32[]{:S(2)}) collective-permute-start(f32[384,128]{1,0:T(8,128)S(1)} %get-tuple-element.29), channel_id=1, source_target_pairs={{1,2},{2,1},{5,6},{6,5},{9,10},{10,9},{13,14},{14,13},{17,18},{18,... | collective-permute-start | bytes 589832 | tf_op jit(solution)/shard_map/ppermute | solution.py:31
  7.9 10.4 %copy-start.1 = (f32[2,256,256]{2,1,0:T(8,128)S(1)}, f32[2,256,256]{2,1,0:T(8,128)}, u32[]{:S(2)}) copy-start(f32[2,256,256]{2,1,0:T(8,128)} %g.7) | copy-start | bytes 1572868
  8.0 10.4 %copy-start.2 = (bf16[4,2,256,256]{3,2,1,0:T(8,128)(2,1)S(1)}, bf16[4,2,256,256]{3,2,1,0:T(8,128)(2,1)}, u32[]{:S(2)}) copy-start(bf16[4,2,256,256]{3,2,1,0:T(8,128)(2,1)} %probe.5) | copy-start | bytes 3145732
  8.0 10.4 %copy-start.3 = (bf16[4,256,256]{2,1,0:T(8,128)(2,1)S(1)}, bf16[4,256,256]{2,1,0:T(8,128)(2,1)}, u32[]{:S(2)}) copy-start(bf16[4,256,256]{2,1,0:T(8,128)(2,1)} %constant.4.clone.tables) | copy-start | bytes 1572868
  23.7 17.9 %collective-permute-start.4 = (f32[128,384]{1,0:T(8,128)S(1)}, f32[128,384]{1,0:T(8,128)S(1)}, u32[]{:S(2)}, u32[]{:S(2)}) collective-permute-start(f32[128,384]{1,0:T(8,128)S(1)} %get-tuple-element.31), channel_id=1, source_target_pairs={{0,4},{4,0},{8,12},{12,8},{16,20},{20,16},{24,28},{28,24},{1,5},{5... | collective-permute-start | bytes 589832 | tf_op jit(solution)/shard_map/ppermute | solution.py:31
  33.1 8.5 %collective-permute-start.5 = (f32[128,384]{1,0:T(8,128)S(1)}, f32[128,384]{1,0:T(8,128)S(1)}, u32[]{:S(2)}, u32[]{:S(2)}) collective-permute-start(f32[128,384]{1,0:T(8,128)S(1)} %get-tuple-element.32), channel_id=1, source_target_pairs={{4,8},{8,4},{12,16},{16,12},{20,24},{24,20},{5,9},{9,5},{13,17},{1... | collective-permute-start | bytes 589832 | tf_op jit(solution)/shard_map/ppermute | solution.py:31
  33.8 12.4 %collective-permute-start.6 = (f32[384,128]{1,0:T(8,128)S(1)}, f32[384,128]{1,0:T(8,128)S(1)}, u32[]{:S(2)}, u32[]{:S(2)}) collective-permute-start(f32[384,128]{1,0:T(8,128)S(1)} %get-tuple-element.33), channel_id=1, source_target_pairs={{0,1},{1,0},{2,3},{3,2},{4,5},{5,4},{6,7},{7,6},{8,9},{9,8},{10,11... | collective-permute-start | bytes 589832 | tf_op jit(solution)/shard_map/ppermute | solution.py:31
  40.9 5.2 %collective-permute-start.7 = (f32[384,128]{1,0:T(8,128)S(1)}, f32[384,128]{1,0:T(8,128)S(1)}, u32[]{:S(2)}, u32[]{:S(2)}) collective-permute-start(f32[384,128]{1,0:T(8,128)S(1)} %get-tuple-element.34), channel_id=1, source_target_pairs={{1,2},{2,1},{5,6},{6,5},{9,10},{10,9},{13,14},{14,13},{17,18},{18,... | collective-permute-start | bytes 589832 | tf_op jit(solution)/shard_map/ppermute | solution.py:31
  46.5 9.4 %collective-permute-start.8 = (f32[384,128]{1,0:T(8,128)S(1)}, f32[384,128]{1,0:T(8,128)S(1)}, u32[]{:S(2)}, u32[]{:S(2)}) collective-permute-start(f32[384,128]{1,0:T(8,128)S(1)} %get-tuple-element.36), channel_id=1, source_target_pairs={{0,1},{1,0},{2,3},{3,2},{4,5},{5,4},{6,7},{7,6},{8,9},{9,8},{10,11... | collective-permute-start | bytes 589832 | tf_op jit(solution)/shard_map/ppermute | solution.py:31
  50.7 5.2 %collective-permute-start.9 = (f32[384,128]{1,0:T(8,128)S(1)}, f32[384,128]{1,0:T(8,128)S(1)}, u32[]{:S(2)}, u32[]{:S(2)}) collective-permute-start(f32[384,128]{1,0:T(8,128)S(1)} %get-tuple-element.37), channel_id=1, source_target_pairs={{1,2},{2,1},{5,6},{6,5},{9,10},{10,9},{13,14},{14,13},{17,18},{18,... | collective-permute-start | bytes 589832 | tf_op jit(solution)/shard_map/ppermute | solution.py:31
  51.4 4.5 %collective-permute-start.10 = (f32[128,384]{1,0:T(8,128)S(1)}, f32[128,384]{1,0:T(8,128)S(1)}, u32[]{:S(2)}, u32[]{:S(2)}) collective-permute-start(f32[128,384]{1,0:T(8,128)S(1)} %get-tuple-element.38), channel_id=1, source_target_pairs={{0,4},{4,0},{8,12},{12,8},{16,20},{20,16},{24,28},{28,24},{1,5},{5... | collective-permute-start | bytes 589832 | tf_op jit(solution)/shard_map/ppermute | solution.py:31
  51.4 4.5 %collective-permute-start.11 = (f32[128,384]{1,0:T(8,128)S(1)}, f32[128,384]{1,0:T(8,128)S(1)}, u32[]{:S(2)}, u32[]{:S(2)}) collective-permute-start(f32[128,384]{1,0:T(8,128)S(1)} %get-tuple-element.39), channel_id=1, source_target_pairs={{4,8},{8,4},{12,16},{16,12},{20,24},{24,20},{5,9},{9,5},{13,17},{1... | collective-permute-start | bytes 589832 | tf_op jit(solution)/shard_map/ppermute | solution.py:31
  63.7 10.1 %collective-permute-start.12 = (f32[2,64,384]{2,1,0:T(8,128)S(1)}, f32[2,64,384]{2,1,0:T(8,128)S(1)}, u32[]{:S(2)}, u32[]{:S(2)}) collective-permute-start(f32[2,64,384]{2,1,0:T(8,128)S(1)} %get-tuple-element.44), channel_id=1, source_target_pairs={{0,4},{4,0},{8,12},{12,8},{16,20},{20,16},{24,28},{28,24},{1,5},{5... | collective-permute-start | bytes 589832 | tf_op jit(solution)/shard_map/ppermute | solution.py:31
  72.8 1.1 %collective-permute-start.13 = (f32[2,64,384]{2,1,0:T(8,128)S(1)}, f32[2,64,384]{2,1,0:T(8,128)S(1)}, u32[]{:S(2)}, u32[]{:S(2)}) collective-permute-start(f32[2,64,384]{2,1,0:T(8,128)S(1)} %get-tuple-element.45), channel_id=1, source_target_pairs={{4,8},{8,4},{12,16},{16,12},{20,24},{24,20},{5,9},{9,5},{13,17},{1... | collective-permute-start | bytes 589832 | tf_op jit(solution)/shard_map/ppermute | solution.py:31
  74.0 28.7 %collective-permute-start.14 = (f32[256,128]{1,0:T(8,128)S(1)}, f32[256,128]{1,0:T(8,128)S(1)}, u32[]{:S(2)}, u32[]{:S(2)}) collective-permute-start(f32[256,128]{1,0:T(8,128)S(1)} %get-tuple-element.47), channel_id=1, source_target_pairs={{0,1},{1,0},{2,3},{3,2},{4,5},{5,4},{6,7},{7,6},{8,9},{9,8},{10,11... | collective-permute-start | bytes 393224 | tf_op jit(solution)/shard_map/ppermute | solution.py:31
  77.8 24.9 %collective-permute-start.15 = (f32[256,128]{1,0:T(8,128)S(1)}, f32[256,128]{1,0:T(8,128)S(1)}, u32[]{:S(2)}, u32[]{:S(2)}) collective-permute-start(f32[256,128]{1,0:T(8,128)S(1)} %get-tuple-element.48), channel_id=1, source_target_pairs={{1,2},{2,1},{5,6},{6,5},{9,10},{10,9},{13,14},{14,13},{17,18},{18,... | collective-permute-start | bytes 393224 | tf_op jit(solution)/shard_map/ppermute | solution.py:31
  78.5 8.2 %collective-permute-start.16 = (f32[8,128]{1,0:T(8,128)S(1)}, f32[8,128]{1,0:T(8,128)S(1)}, u32[]{:S(2)}, u32[]{:S(2)}) collective-permute-start(f32[8,128]{1,0:T(8,128)S(1)} %get-tuple-element.49), channel_id=1, source_target_pairs={{0,4},{4,0},{8,12},{12,8},{16,20},{20,16},{24,28},{28,24},{1,5},{5... | collective-permute-start | bytes 12296 | tf_op jit(solution)/shard_map/ppermute | solution.py:481
  86.7 3.6 %collective-permute-start.17 = (f32[8,128]{1,0:T(8,128)S(1)}, f32[8,128]{1,0:T(8,128)S(1)}, u32[]{:S(2)}, u32[]{:S(2)}) collective-permute-start(f32[8,128]{1,0:T(8,128)S(1)} %add.15), channel_id=1, source_target_pairs={{0,8},{4,12},{8,0},{12,4},{16,24},{20,28},{24,16},{28,20},{1,9},{5... | collective-permute-start | bytes 12296 | tf_op jit(solution)/shard_map/ppermute | solution.py:481
  90.3 4.3 %collective-permute-start.18 = (f32[8,128]{1,0:T(8,128)S(1)}, f32[8,128]{1,0:T(8,128)S(1)}, u32[]{:S(2)}, u32[]{:S(2)}) collective-permute-start(f32[8,128]{1,0:T(8,128)S(1)} %add.16), channel_id=1, source_target_pairs={{0,16},{4,20},{8,24},{12,28},{16,0},{20,4},{24,8},{28,12},{1,17},{... | collective-permute-start | bytes 12296 | tf_op jit(solution)/shard_map/ppermute | solution.py:481
  94.6 3.6 %collective-permute-start.19 = (f32[8,128]{1,0:T(8,128)S(1)}, f32[8,128]{1,0:T(8,128)S(1)}, u32[]{:S(2)}, u32[]{:S(2)}) collective-permute-start(f32[8,128]{1,0:T(8,128)S(1)} %add.17), channel_id=1, source_target_pairs={{0,1},{1,0},{2,3},{3,2},{4,5},{5,4},{6,7},{7,6},{8,9},{9,8},{10,11... | collective-permute-start | bytes 12296 | tf_op jit(solution)/shard_map/ppermute | solution.py:481
  98.2 4.5 %collective-permute-start.20 = (f32[8,128]{1,0:T(8,128)S(1)}, f32[8,128]{1,0:T(8,128)S(1)}, u32[]{:S(2)}, u32[]{:S(2)}) collective-permute-start(f32[8,128]{1,0:T(8,128)S(1)} %add.18), channel_id=1, source_target_pairs={{0,2},{1,3},{2,0},{3,1},{4,6},{5,7},{6,4},{7,5},{8,10},{9,11},{10,... | collective-permute-start | bytes 12296 | tf_op jit(solution)/shard_map/ppermute | solution.py:481

commit v2 on v1

v2 whole, which is shorter than its diff:
```python
import functools
import math

import jax
import jax.numpy as jnp
import numpy as np
from jax import lax
from jax.experimental import pallas as pl
from jax.experimental.pallas import tpu as pltpu
from jax.sharding import PartitionSpec as P

HALO = 64
damping = 0.5
F32 = jnp.float32
BF16 = jnp.bfloat16
MIB = 1024 * 1024


def pairs(size, odd):
    found = []
    for i in range(odd, size - 1, 2):
        found += [(i, i + 1), (i + 1, i)]
    return found


def swap(x, axis, odd):
    wanted = pairs(lax.axis_size(axis), odd)
    if not wanted:
        return jnp.zeros_like(x)
    return lax.ppermute(x, axis, wanted)


def half_tables(length):
    counter = np.arange(length)
    angles = ((counter[:, None] * counter[None, :]) % length).astype(np.float32)
    angles = angles * np.float32(2.0 * math.pi / length)
    factor = np.float32(1.0 / math.sqrt(length))
    cos, sin = (np.cos(angles) * factor, np.sin(angles) * factor)
    half = length // 2
    tables = []
    for parity in (0, 1):
        c, s = (cos[parity::2, :half], sin[parity::2, :half])
        left = np.concatenate([np.concatenate([c, s], 1), np.concatenate([-s, c], 1)], 0)
        tables += [left, left.T]
    return jnp.asarray(np.stack(tables), BF16)


def sorting_tables(length):
    order = np.concatenate([np.arange(0, length, 2), np.arange(1, length, 2)])
    left = np.zeros((length, length), np.float32)
    left[np.arange(length), order] = 1.0
    return jnp.asarray(np.stack([left, left.T]), BF16)


def dot(a, b):
    return jnp.dot(a, b, preferred_element_type=F32)


def cat(parts, axis):
    return jnp.concatenate(parts, axis=axis)


def lanes_low(shape):
    return lax.broadcasted_iota(jnp.int32, shape, len(shape) - 1) < shape[-1] // 2


def shifted_place(frames, k, blocks):
    row = HALO + frames[1 + k]
    col = frames[1 + frames.shape[0] // 2 + k]
    first = jnp.where(col < 0, blocks - 1, 0)
    places = [lax.rem(first + i, blocks) for i in range(blocks)]
    return (row, places, jnp.where(col < 0, col + 128, col))


def take_patch(ext, frames, k, patch):
    width = patch.shape[1]
    row, places, across = shifted_place(frames, k, ext.shape[1])
    lane = lax.broadcasted_iota(jnp.int32, (width, 128), 1)
    back = lax.rem(128 - across, 128)
    for q in range(2):
        found = [ext[q, place, pl.ds(row, width), :] for place in places]
        for i in range(width // 128):
            both = jnp.where(lane >= across, found[i], found[i + 1])
            patch[q, :, 128 * i : 128 * (i + 1)] = pltpu.roll(both, back, 1)


def put_patch(total, frames, k, parts):
    width = parts[0].shape[0]
    row, places, across = shifted_place(frames, k, total.shape[1])
    lane = lax.broadcasted_iota(jnp.int32, (width, 128), 1)
    none = jnp.zeros((width, 128), F32)
    for q in range(2):
        turned = [none]
        for i in range(width // 128):
            turned.append(pltpu.roll(parts[q][:, 128 * i : 128 * (i + 1)], across, 1))
        turned.append(none)
        for i, place in enumerate(places):
            total[q, place, pl.ds(row, width), :] += jnp.where(
                lane < across, turned[i], turned[i + 1]
            )


def project(patch, probe, weights, k, tables, stage):
    te, te_t, to, to_t = (tables[i] for i in range(4))
    xr, xi = (patch[0], patch[1])
    width = xr.shape[0]
    h = width // 2
    modes = probe.shape[0]
    for m in range(modes):
        pr, pi = (probe[m, 0].astype(F32), probe[m, 1].astype(F32))
        er, ei = (pr * xr - pi * xi, pr * xi + pi * xr)
        even = cat([er[:h] + er[h:], ei[:h] + ei[h:]], 0).astype(BF16)
        odd = cat([er[:h] - er[h:], ei[:h] - ei[h:]], 0).astype(BF16)
        for e, y in enumerate((dot(te, even), dot(to, odd))):
            yr, yi = (y[:h], y[h:])
            plus = cat([yr[:, :h] + yr[:, h:], yi[:, :h] + yi[:, h:]], 1)
            minus = cat([yr[:, :h] - yr[:, h:], yi[:, :h] - yi[:, h:]], 1)
            stage[0, m, e * h : (e + 1) * h] = plus.astype(BF16)
            stage[1, m, e * h : (e + 1) * h] = minus.astype(BF16)
    found = []
    for e, table in enumerate((te_t, to_t)):
        acc = None
        for m in range(modes):
            z = dot(stage[e, m], table)
            z = z * weights[k, m, :, e * width : (e + 1) * width].astype(F32)
            acc = z if m == 0 else acc + z
        found.append(acc[:, :h] + acc[:, h:])
    return tuple(found)


def back_project(pe, po, probe, weights, k, tables, stage):
    te, te_t, to, to_t = (tables[i] for i in range(4))
    width = pe.shape[0]
    h = width // 2
    modes = probe.shape[0]
    pe2, po2 = (cat([pe, pe], 1), cat([po, po], 1))
    for m in range(modes):
        ve = (weights[k, m, :, :width].astype(F32) * pe2).astype(BF16)
        vo = (weights[k, m, :, width:].astype(F32) * po2).astype(BF16)
        top = cat([cat([ve[:h, :h], vo[:h, :h]], 1), cat([ve[:h, h:], vo[:h, h:]], 1)], 0)
        low = cat([cat([ve[h:, :h], vo[h:, :h]], 1), cat([ve[h:, h:], vo[h:, h:]], 1)], 0)
        a, b = (dot(te_t, top), dot(to_t, low))
        s, d = (a + b, a - b)
        for e, c in enumerate((slice(0, h), slice(h, width))):
            stage[e, m, :h] = cat([s[:h, c], s[h:, c]], 1).astype(BF16)
            stage[e, m, h:] = cat([d[:h, c], d[h:, c]], 1).astype(BF16)
    cr = ci = None
    for m in range(modes):
        a, b = (dot(stage[0, m], te), dot(stage[1, m], to))
        s, d = (a + b, a - b)
        nr, ni = (cat([s[:, :h], d[:, :h]], 1), cat([s[:, h:], d[:, h:]], 1))
        pr, pi = (probe[m, 0].astype(F32), probe[m, 1].astype(F32))
        r = pr * nr + pi * ni
        i = pr * ni - pi * nr
        cr = r if m == 0 else cr + r
        ci = i if m == 0 else ci + i
    return (cr, ci)


def square_sum(x):
    return jnp.sum(x * x)


def scalar_tile(values):
    rows = lax.broadcasted_iota(jnp.int32, (8, 128), 0)
    tile = jnp.zeros((8, 128), F32)
    for i, value in enumerate(values):
        tile = jnp.where(rows == i, value, tile)
    return tile


def parity_of(axis):
    return lax.rem(lax.axis_index(axis), 2)


def by_parity(axis, low, high, first, second):
    even = parity_of(axis) == 0

    @pl.when(even)
    def _():
        first(high())
        second(low())

    @pl.when(jnp.logical_not(even))
    def _():
        first(low())
        second(high())


def lower_upper(axis, first, second):
    even = parity_of(axis) == 0
    return (jnp.where(even, second, first), jnp.where(even, first, second))


def store(ref):
    def put(value):
        ref[...] = value

    return put


def halo_rows_kernel(g, first, second, arrived):
    n = g.shape[1]

    low, high = (g.at[:, :HALO], g.at[:, n - HALO :])
    by_parity(
        "wide",
        lambda: low,
        lambda: high,
        lambda source: pltpu.make_async_copy(source, first, arrived.at[0]).start(),
        lambda source: pltpu.make_async_copy(source, second, arrived.at[1]).start(),
    )
    pltpu.make_async_copy(low, first, arrived.at[0]).wait()
    pltpu.make_async_copy(low, second, arrived.at[1]).wait()


def fill_rows(ext, g, first, second):
    n, width = (g.shape[1], g.shape[2])
    above, below = lower_upper("wide", first[...], second[...])
    for b in range(width // 128):
        cols = slice(128 * b, 128 * (b + 1))
        ext[:, b, :HALO] = above[:, :, cols]
        ext[:, b, HALO : HALO + n] = g[:, :, cols]
        ext[:, b, HALO + n :] = below[:, :, cols]


def halo_cols_kernel(second, first, g, out_first, out_second, ext):
    last = g.shape[2] // 128 - 1
    fill_rows(ext, g, first, second)
    low = lanes_low(out_first.shape)
    by_parity(
        "narrow",
        lambda: jnp.where(low, ext[0, 0], pltpu.roll(ext[1, 0], HALO, 1)),
        lambda: jnp.where(low, pltpu.roll(ext[1, last], HALO, 1), ext[0, last]),
        store(out_first),
        store(out_second),
    )


def fill_cols(ext, first, second):
    left, right = lower_upper("narrow", first[...], second[...])
    last = ext.shape[1] - 1
    low = lanes_low(right.shape)
    ext[0, last] = jnp.where(low, right, left)
    ext[1, last] = pltpu.roll(jnp.where(low, left, right), HALO, 1)


def sort_weights(frames, w, sorter, out, held, arrived, begin, end, meanwhile):
    width = w.shape[-1]
    h = width // 2
    modes = w.shape[1]

    def fetch(k):
        return pltpu.make_async_copy(w.at[k], held.at[k], arrived.at[k])

    for k in range(begin, end):

        @pl.when(k < frames[0])
        def _():
            fetch(k).start()

    meanwhile()

    def visit(k, carried):
        fetch(k).wait()
        for m in range(modes):
            re = dot(dot(sorter[0], held[k, m, 0]).astype(BF16), sorter[1])
            im = dot(dot(sorter[0], held[k, m, 1]).astype(BF16), sorter[1])
            out[k, m] = cat([re[:, :h], im[:, :h], re[:, h:], im[:, h:]], 1).astype(BF16)
        return carried

    lax.fori_loop(begin, jnp.minimum(end, frames[0]), visit, 0)


def prepare_kernel(
    frames, w, sorter_far, probe_far, tables_far, g_far,
    out, sorter, probe, tables, g, held, arrived, loaded,
):
    moves = ((sorter_far, sorter), (g_far, g), (probe_far, probe), (tables_far, tables))
    moves = [pltpu.make_async_copy(a, b, loaded.at[i]) for i, (a, b) in enumerate(moves)]
    moves[0].start()

    def meanwhile():
        for move in moves[1:]:
            move.start()
        moves[0].wait()

    sort_weights(frames, w, sorter, out, held, arrived, 0, 1, meanwhile)
    for move in moves[1:]:
        move.wait()


def prepare_rest_kernel(frames, w, sorter, first, out, held, arrived):
    sort_weights(frames, w, sorter, out, held, arrived, 1, w.shape[0], lambda: None)


def first_pass_kernel(
    frames, g, row1, row2, col1, col2, probe, weights, tables,
    total, sums, sr1, sr2, si1, si2, ext, patch, stage,
):
    fill_rows(ext, g, row1, row2)
    fill_cols(ext, col1, col2)
    total[...] = jnp.zeros_like(total)

    def visit(k, energy):
        take_patch(ext, frames, k, patch)
        pe, po = project(patch, probe, weights, k, tables, stage)
        put_patch(total, frames, k, back_project(pe, po, probe, weights, k, tables, stage))
        return energy + square_sum(pe) + square_sum(po)

    energy = lax.fori_loop(0, frames[0], visit, F32(0.0))
    sums[...] = scalar_tile([square_sum(g[...]), energy])
    send_row_bands(total, 0, sr1, sr2)
    send_col_bands(total, 1, si1, si2)


def send_row_bands(total, q, first, second):
    n = total.shape[2]
    by_parity(
        "wide",
        lambda: total[q, :, : 2 * HALO].reshape(first.shape),
        lambda: total[q, :, n - 2 * HALO :].reshape(first.shape),
        store(first),
        store(second),
    )


def send_col_bands(total, q, first, second):
    last = total.shape[1] - 1
    low = lanes_low(first.shape)
    by_parity(
        "narrow",
        lambda: jnp.where(low, total[q, 0], total[q, last]),
        lambda: jnp.where(low, total[q, last], total[q, last - 1]),
        store(first),
        store(second),
    )


def add_row_bands(total, q, first, second):
    blocks, n = total.shape[1:3]
    above, below = lower_upper("wide", first[...], second[...])
    total[q, :, : 2 * HALO] += above.reshape(blocks, 2 * HALO, 128)
    total[q, :, n - 2 * HALO :] += below.reshape(blocks, 2 * HALO, 128)


def add_col_bands(total, q, first, second):
    last = total.shape[1] - 1
    left, right = lower_upper("narrow", first[...], second[...])
    low = lanes_low(right.shape)
    total[q, last] += jnp.where(low, right, left)
    total[q, 0] += jnp.where(low, left, 0.0)
    total[q, last - 1] += jnp.where(low, 0.0, right)


def bands_kernel(rr2, ri1, ri2, rr1, total, out, sr1, sr2, si1, si2):
    add_row_bands(out, 0, rr1, rr2)
    add_col_bands(out, 1, ri1, ri2)
    send_col_bands(out, 0, sr1, sr2)
    send_row_bands(out, 1, si1, si2)


def second_forward_kernel(
    last_row, last_col, frames, ri2, rr1, rr2, ri1, total, sums, probe, weights, tables,
    image, projected, all_sums, ext, patch, stage,
):
    last = ext.shape[1] - 1
    n = ext.shape[2]
    ext[...] = total[...]
    add_col_bands(ext, 0, rr1, rr2)
    add_row_bands(ext, 1, ri1, ri2)

    @pl.when(lax.axis_index("wide") == 0)
    def _():
        ext[:, :, :HALO] = jnp.zeros((2, last + 1, HALO, 128), F32)

    @pl.when(lax.axis_index("wide") == last_row)
    def _():
        ext[:, :, n - HALO :] = jnp.zeros((2, last + 1, HALO, 128), F32)

    low = lanes_low((2, n, 128))

    @pl.when(lax.axis_index("narrow") == 0)
    def _():
        ext[:, last] = jnp.where(low, ext[:, last], 0.0)

    @pl.when(lax.axis_index("narrow") == last_col)
    def _():
        ext[:, last] = jnp.where(low, 0.0, ext[:, last])

    for b in range(last):
        image[:, :, 128 * b : 128 * (b + 1)] = ext[:, b, HALO : n - HALO]

    def visit(k, energy):
        take_patch(ext, frames, k, patch)
        pe, po = project(patch, probe, weights, k, tables, stage)
        projected[k] = cat([pe, po], 1)
        return energy + square_sum(pe) + square_sum(po)

    energy = lax.fori_loop(0, frames[0], visit, F32(0.0))
    rows = lax.broadcasted_iota(jnp.int32, (8, 128), 0)
    all_sums[...] = jnp.where(
        rows == 2, square_sum(image[...]), jnp.where(rows == 3, energy, sums[...])
    )


def second_backward_kernel(begin, end, frames, projected, probe, weights, tables, *rest):
    total, stage = rest[-2:]
    h = projected.shape[2] // 2
    if begin == 0:
        total[...] = jnp.zeros_like(total)

    def visit(k, carried):
        pe, po = (projected[k, :, :h], projected[k, :, h:])
        parts = back_project(pe, po, probe, weights, k, tables, stage)
        put_patch(total, frames, k, parts)
        return carried

    lax.fori_loop(begin, jnp.minimum(end, frames[0]), visit, 0)


def send_margins_kernel(total, first, second):
    n = total.shape[2]
    by_parity(
        "wide",
        lambda: total[:, :, :HALO].reshape(first.shape),
        lambda: total[:, :, n - HALO :].reshape(first.shape),
        store(first),
        store(second),
    )


def fold_rows_kernel(second, first, total, *rest):
    parts, (middle, out_first, out_second, out_sums) = (rest[:-4], rest[-4:])
    blocks, n = middle.shape[1:3]
    last = blocks - 1
    above, below = lower_upper("wide", first[...], second[...])
    middle[...] = total[:, :, HALO : HALO + n]
    middle[:, :, :HALO] += above.reshape(2, blocks, HALO, 128)
    middle[:, :, n - HALO :] += below.reshape(2, blocks, HALO, 128)
    low = lanes_low((n, 128))
    re, im = (middle[0, last], pltpu.roll(middle[1, last], HALO, 1))
    by_parity(
        "narrow",
        lambda: jnp.where(low, im, re),
        lambda: jnp.where(low, re, im),
        store(out_first),
        store(out_second),
    )
    out_sums[...] = total_of(parts)


def finish_kernel(second, first, g, image, middle, *rest):
    parts, (solved_out, left_out, solved, left_over, sent) = (rest[:-5], rest[-5:])
    n, width = g.shape[1:]
    left, right = lower_upper("narrow", first[...], second[...])
    low = lanes_low(right.shape)
    total = total_of(parts)
    n0, s0, uu, s1 = (total[i : i + 1, :1] for i in range(4))
    mu = s0 / n0
    a0 = n0 / (s0 + damping * n0)
    n1 = a0 * a0 * (uu - mu * s0)
    b = n1 / n0
    c1 = a0 * mu + b
    curve = damping * (n1 + b * b * n0) + c1 * c1 * s0 - 2.0 * c1 * a0 * uu + a0 * a0 * s1
    a1 = n1 / curve
    last = width // 128 - 1
    for q in range(2):
        low_part = left if q == 0 else pltpu.roll(left, HALO, 1)
        high_part = right if q == 0 else pltpu.roll(right, HALO, 1)
        for block in range(last + 1):
            cols = slice(128 * block, 128 * (block + 1))
            v = middle[q, block]
            if block == 0:
                v = v + jnp.where(low, low_part, 0.0)
            if block == last:
                v = v + jnp.where(low, 0.0, high_part)
            x, u = (g[q, :, cols], image[q, :, cols])
            d1 = c1 * x - a0 * u
            solved[q, :, cols] = a0 * x + a1 * d1
            left_over[q, :, cols] = a0 * (mu * x - u) - a1 * (damping * d1 + c1 * u - a0 * v)
        for i, (value, to) in enumerate(((solved, solved_out), (left_over, left_out))):
            pltpu.make_async_copy(value.at[q], to.at[q], sent.at[q, i]).start()
    for q in range(2):
        for i, (value, to) in enumerate(((solved, solved_out), (left_over, left_out))):
            pltpu.make_async_copy(value.at[q], to.at[q], sent.at[q, i]).wait()


def total_of(refs):
    total = refs[0][...]
    for ref in refs[1:]:
        total = total + ref[...]
    return total


def add_kernel(*refs):
    refs[-1][...] = total_of(refs[:-1])


def hops(axis, steps):
    size = lax.axis_size(axis)
    masks = list(steps) + [sum(steps)] * (len(steps) > 1)
    return [(axis, [(i, i ^ mask) for i in range(size)]) for mask in masks]


def powers(size):
    found = []
    while 2 ** len(found) < size:
        found.append(2 ** len(found))
    return found


def take_hops(x, wanted):
    return [x] + [lax.ppermute(x, axis, perm) for axis, perm in wanted]


def add_hops(x, rounds):
    for wanted in rounds:
        x = call(add_kernel, [shape(8, 128)], 0, take_hops(x, wanted))[0]
    return x


def shape(*dims):
    return jax.ShapeDtypeStruct(dims, F32)


def call(kernel, outs, smem, args, scratch=(), flops=0, aliases={}, far=(), out_far=False):
    specs = [pl.BlockSpec(memory_space=pltpu.SMEM)] * smem
    specs += [pl.BlockSpec(memory_space=pltpu.VMEM)] * (len(args) - smem)
    for i in far:
        specs[i] = pl.BlockSpec(memory_space=pltpu.HBM)
    args = [
        arg if i < smem else pltpu.with_memory_space_constraint(arg, spec.memory_space)
        for i, (arg, spec) in enumerate(zip(args, specs))
    ]
    moved = sum(a.size * a.dtype.itemsize for a in args)
    moved += sum(math.prod(o.shape) * o.dtype.itemsize for o in outs)
    place = pltpu.HBM if out_far else pltpu.VMEM
    return pl.pallas_call(
        kernel,
        out_shape=[place(o.shape, o.dtype) for o in outs],
        in_specs=specs,
        out_specs=[pl.BlockSpec(memory_space=place)] * len(outs),
        scratch_shapes=list(scratch),
        input_output_aliases=aliases,
        compiler_params=pltpu.CompilerParams(vmem_limit_bytes=20 * MIB),
        cost_estimate=pl.CostEstimate(flops=flops, bytes_accessed=moved, transcendentals=0),
    )(*args)


def prepare(frames, w, probe, tables, g):
    slots, modes, parts, rows, cols = w.shape
    sorter = sorting_tables(cols)
    weights = jax.ShapeDtypeStruct((slots, modes, rows, parts * cols), BF16)
    sort_flops = 8 * modes * rows * cols * rows
    scratch = [pltpu.VMEM(w.shape, BF16), pltpu.SemaphoreType.DMA((slots,))]
    outs = [jax.ShapeDtypeStruct(x.shape, x.dtype) for x in (sorter, probe, tables, g)]
    weights, sorter, probe, tables, g = call(
        prepare_kernel, [weights] + outs, 1, [frames, w, sorter, probe, tables, g],
        scratch + [pltpu.SemaphoreType.DMA((4,))], sort_flops, far=(1, 2, 3, 4, 5),
    )
    if slots > 1:
        weights = call(
            prepare_rest_kernel, [weights], 1, [frames, w, sorter, weights],
            scratch, (slots - 1) * sort_flops, {3: 0}, (1,),
        )[0]
    return (weights, probe, tables, g)


def local(gradient, probe_modes, mode_weights, offsets, counts):
    weights = mode_weights[0, 0]
    slots, modes = weights.shape[:2]
    rows, width = gradient.shape[1:]
    tall, blocks = (rows + 2 * HALO, width // 128 + 1)
    frames = jnp.concatenate([counts.reshape(-1), jnp.swapaxes(offsets, 2, 3).reshape(-1)])
    tables = half_tables(width)
    pass_flops = 8 * 2 * slots * modes * 2 * width * width * width
    extended = pltpu.VMEM((2, blocks, tall, 128), F32)
    patch = pltpu.VMEM((2, rows, width), F32)
    stage = pltpu.VMEM((2, modes, rows, width), BF16)
    whole = shape(2, blocks, tall, 128)

    row_sends = call(
        halo_rows_kernel, [shape(2, HALO, width)] * 2, 0, [gradient],
        [pltpu.SemaphoreType.DMA((2,))], far=(0,),
    )
    row2, row1 = (swap(row_sends[1], "wide", 1), swap(row_sends[0], "wide", 0))
    sorted_weights, probe_modes, tables, gradient = prepare(
        frames, weights, probe_modes, tables, gradient
    )
    col_sends = call(
        halo_cols_kernel, [shape(tall, 128)] * 2, 0, [row2, row1, gradient],
        [pltpu.VMEM((2, blocks, tall, 128), F32)],
    )
    col1, col2 = (swap(x, "narrow", i) for i, x in enumerate(col_sends))

    row_band, col_band = (shape(blocks * 2 * HALO, 128), shape(tall, 128))
    total, sums, sr1, sr2, si1, si2 = call(
        first_pass_kernel,
        [whole, shape(8, 128), row_band, row_band, col_band, col_band],
        1,
        [frames, gradient, row1, row2, col1, col2, probe_modes, sorted_weights, tables],
        [extended, patch, stage],
        pass_flops,
    )
    sr2, si1, si2, sr1 = (
        swap(sr2, "wide", 1), swap(si1, "narrow", 0), swap(si2, "narrow", 1), swap(sr1, "wide", 0)
    )
    total, sr1, sr2, si1, si2 = call(
        bands_kernel,
        [whole, col_band, col_band, row_band, row_band],
        0,
        [sr2, si1, si2, sr1, total],
        aliases={4: 0},
    )
    si2, sr1, sr2, si1 = (
        swap(si2, "wide", 1), swap(sr1, "narrow", 0), swap(sr2, "narrow", 1), swap(si1, "wide", 0)
    )
    image, projected, sums = call(
        functools.partial(
            second_forward_kernel, lax.axis_size("wide") - 1, lax.axis_size("narrow") - 1
        ),
        [shape(2, rows, width), shape(slots, rows, width), shape(8, 128)],
        1,
        [
            frames, si2, sr1, sr2, si1, total, sums, probe_modes, sorted_weights, tables,
        ],
        [extended, patch, stage],
        pass_flops // 2,
    )
    along_wide, along_narrow = (powers(lax.axis_size("wide")), powers(lax.axis_size("narrow")))
    rounds = [hops("wide", [step]) for step in along_wide[:-1]]
    rounds += [hops("narrow", [step]) for step in along_narrow[:-2]]
    beside_rows = hops("narrow", along_narrow[-2:]) if along_narrow else []
    beside_cols = hops("wide", along_wide[-1:]) if along_wide else []
    early = len(rounds)
    total = None
    for i in range(max(early, 1)):
        begin, end = (i * slots // max(early, 1), (i + 1) * slots // max(early, 1))
        if end > begin:
            total = call(
                functools.partial(second_backward_kernel, begin, end),
                [whole],
                1,
                [frames, projected, probe_modes, sorted_weights, tables]
                + ([] if begin == 0 else [total]),
                [stage],
                pass_flops // 2 * (end - begin) // slots,
                {} if begin == 0 else {5: 0},
            )[0]
        sums = add_hops(sums, rounds[i : i + 1])
        if end > 0:
            total, sums = lax.optimization_barrier((total, sums))
    margin = shape(2 * blocks * HALO, 128)
    f1, f2 = call(send_margins_kernel, [margin, margin], 0, [total])
    f2, f1 = (swap(f2, "wide", 1), swap(f1, "wide", 0))
    middle, f1, f2, sums = call(
        fold_rows_kernel,
        [shape(2, blocks, rows, 128), shape(rows, 128), shape(rows, 128), shape(8, 128)],
        0,
        [f2, f1, total] + take_hops(sums, beside_rows),
    )
    f2, f1 = (swap(f2, "narrow", 1), swap(f1, "narrow", 0))
    solved, left_over = call(
        finish_kernel,
        [shape(2, rows, width)] * 2,
        0,
        [f2, f1, gradient, image, middle] + take_hops(sums, beside_cols),
        [pltpu.VMEM((2, rows, width), F32)] * 2 + [pltpu.SemaphoreType.DMA((2, 2))],
        out_far=True,
    )
    return (solved, left_over)


def solution(mesh):
    placed = (
        P(None, "wide", "narrow"),
        P(),
        P("wide", "narrow", None, None, None, None, None),
        P("wide", "narrow", None, None),
        P("wide", "narrow"),
    )
    return jax.shard_map(
        local,
        mesh=mesh,
        in_specs=placed,
        out_specs=(P(None, "wide", "narrow"), P(None, "wide", "narrow")),
        check_vma=False,
    )
```

time: 105 us -> 82.4 us (0.78)
  starting transfers between devices: 58 us -> 42.4 us
  waiting for transfers between devices: 17.8 us -> 8.71 us
  Pallas kernels: 25.7 us -> 28.1 us
    ppermute x16, starting transfers between devices: 42.5 us -> 32.3 us  [swap(): return lax.ppermute(x, axis, wanted)]
    ppermute x16, waiting for transfers between devices: 9.06 us -> 2.15 us  [swap(): return lax.ppermute(x, axis, wanted)]
    ppermute x5 -> x6, starting transfers between devices: 15.4 us -> 10.1 us  [take_hops(): return [x] + [lax.ppermute(x, axis, perm) for axis, perm in wanted]]
    pallas_call x9 -> x14, Pallas kernels: 25.7 us -> 28.1 us  [call(): pl.pallas_call(kernel, out_shape=[place(o.shape, o.dtype) for o in outs],...]
    ppermute x5 -> x6, waiting for transfers between devices: 8.78 us -> 6.56 us  [take_hops(): return [x] + [lax.ppermute(x, axis, perm) for axis, perm in wanted]]
    unnamed x11 -> x0, local copies, waits for them, and re-layouts: 1.14 us -> none
  transfers between devices with their start and end apart: 21 -> 22, of which waited for: 9 -> 5; matrix products, arithmetic and copies ran while one was open for 0% -> 1% of each run, Pallas kernels for 10% -> 14%
where the time goes in v2:
time: 82.4 us; the launch traced here: 81.5 us
  starting transfers between devices  42.4 us (51%)
  Pallas kernels  28.1 us (34%)
  waiting for transfers between devices  8.71 us (11%)
  between operations  1.52 us (2%)
    ppermute x16, starting transfers between devices, swap(): return lax.ppermute(x, axis, wanted)  32.3 us
    pallas_call x14, Pallas kernels, call(): pl.pallas_call(kernel, out_shape=[place(o.shape, o.dtype) for o in outs],...  28.1 us
    ppermute x6, starting transfers between devices, take_hops(): return [x] + [lax.ppermute(x, axis, perm) for axis, perm in wanted]  10.1 us
    ppermute x6, waiting for transfers between devices, take_hops(): return [x] + [lax.ppermute(x, axis, perm) for axis, perm in wanted]  6.56 us
    ppermute x16, waiting for transfers between devices, swap(): return lax.ppermute(x, axis, wanted)  2.15 us
  transfers between devices with their start and end apart: 22, of which 5 were waited for; matrix products, arithmetic and copies ran while one was open for 1% of the time, Pallas kernels for 14%

profile of v2, /device:TPU:0, one launch (start us, length us, event | category | flops | bytes accessed | tf_op | source)
XLA Modules:
  0.0 81.5 jit_solution(5056241747426666640)
XLA Ops:
  0.6 1.0 %shard_map.87 = (f32[2,64,256]{2,1,0:T(8,128)S(1)}, f32[2,64,256]{2,1,0:T(8,128)S(1)}) custom-call(f32[2,256,256]{2,1,0:T(8,128)} %g.1), custom_call_target="tpu_custom_call" | custom-call | bytes 786432 | tf_op jit(solution)/shard_map/pallas_call | solution.py:539
  1.6 0.5 collective-permute-start
  2.2 0.7 collective-permute-start.1
  3.5 0.8 reshape.11
  4.2 0.1 pad_add_fusion.frames
  4.3 3.4 %shard_map.86 = (bf16[3,4,256,512]{3,2,1,0:T(8,128)(2,1)S(1)}, bf16[2,256,256]{2,1,0:T(8,128)(2,1)S(1)}, bf16[4,2,256,256]{3,2,1,0:T(8,128)(2,1)S(1)}, bf16[4,25...) custom-call(s32[7]{0:T(128)S(1)} %pad_add_fusion.frames, bf16[3,4,2,256,256]{4,3,2,1,0:T(8,128)(2,1)} %bitcast.4, ...), custom_call_target="tpu_custom_call" | custom-call | flops 536870912 | bytes 11010076 | tf_op jit(solution)/shard_map/pallas_call | solution.py:539
  7.7 0.0 collective-permute-done.first.row1
  7.7 0.0 collective-permute-done.1.second.row2
  7.7 0.2 shard_map.88
  7.9 2.7 %collective-permute-start.2 = (f32[384,128]{1,0:T(8,128)S(1)}, f32[384,128]{1,0:T(8,128)S(1)}, u32[]{:S(2)}, u32[]{:S(2)}) collective-permute-start(f32[384,128]{1,0:T(8,128)S(1)} %get-tuple-element.38), channel_id=1, source_target_pairs={{0,1},{1,0},{2,3},{3,2},{4,5},{5,4},{6,7},{7,6},{8,9},{9,8},{10,11... | collective-permute-start | bytes 589832 | tf_op jit(solution)/shard_map/ppermute | solution.py:30
  10.6 0.7 collective-permute-start.3
  11.3 3.4 %shard_map.89.weights = bf16[3,4,256,512]{3,2,1,0:T(8,128)(2,1)S(1)} custom-call(s32[7]{0:T(128)S(1)} %pad_add_fusion.frames, bf16[3,4,2,256,256]{4,3,2,1,0:T(8,128)(2,1)} %bitcast.5, bf16[2,256,256]{2,1,0:T(8,128)(2,1)S(1)} %get-tuple-element.41.sorter, bf16[3,4,256,512]{3,2,1,0:T(8,128)(2,1)S(1)} %get-tuple-element.42.first), custom_call_target="tpu_custom_call", output_to_operand_aliasing={{}: (3, {})} | custom-call | flops 1073741824 | bytes 9699356 | tf_op jit(solution)/shard_map/pallas_call | solution.py:539
  14.7 0.0 collective-permute-done.2.col1
  14.7 0.0 collective-permute-done.3.col2
  14.7 8.4 %shard_map.90 = (f32[2,3,384,128]{3,2,1,0:T(8,128)S(1)}, f32[8,128]{1,0:T(8,128)S(1)}, f32[384,128]{1,0:T(8,128)S(1)}, f32[384,128]{1,0:T(8,128)S(1)}, f32[384,128]{1,0:T(8,128)S(1)}, /*index=5*/f32[384,128]{1,0:T(8,128)S(1)}) custom-call(s32[7]{0:T(128)S(1)} %pad_add_fusion.frames, f32[2,256,256]{2,1,0:T(8,128)S(1)} %get-tuple-element.35.g, ...), custom_call_target="tpu_custom_call" | custom-call | flops 6442450944 | bytes 7868444 | tf_op jit(solution)/shard_map/pallas_call | solution.py:539
  23.1 0.7 collective-permute-start.4
  23.8 0.1 collective-permute-start.5
  23.9 0.7 collective-permute-start.6
  24.6 11.1 %collective-permute-start.7 = (f32[384,128]{1,0:T(8,128)S(1)}, f32[384,128]{1,0:T(8,128)S(1)}, u32[]{:S(2)}, u32[]{:S(2)}) collective-permute-start(f32[384,128]{1,0:T(8,128)S(1)} %get-tuple-element.47), channel_id=1, source_target_pairs={{0,4},{4,0},{8,12},{12,8},{16,20},{20,16},{24,28},{28,24},{1,5},{5... | collective-permute-start | bytes 589832 | tf_op jit(solution)/shard_map/ppermute | solution.py:30
  35.6 0.0 collective-permute-done.4.rr2
  35.6 0.0 collective-permute-done.5.ri1
  35.6 0.0 collective-permute-done.6.ri2
  35.6 1.1 %collective-permute-done.7.rr1 = f32[384,128]{1,0:T(8,128)S(1)} collective-permute-done((f32[384,128]{1,0:T(8,128)S(1)}, f32[384,128]{1,0:T(8,128)S(1)}, u32[]{:S(2)}, u32[]{:S(2)}) %collective-permute-start.7) | collective-permute-done | bytes 196640 | tf_op jit(solution)/shard_map/ppermute | solution.py:30
  36.7 0.2 shard_map.91
  36.9 0.7 collective-permute-start.8
  37.6 3.2 %collective-permute-start.9 = (f32[384,128]{1,0:T(8,128)S(1)}, f32[384,128]{1,0:T(8,128)S(1)}, u32[]{:S(2)}, u32[]{:S(2)}) collective-permute-start(f32[384,128]{1,0:T(8,128)S(1)} %get-tuple-element.50), channel_id=1, source_target_pairs={{0,1},{1,0},{2,3},{3,2},{4,5},{5,4},{6,7},{7,6},{8,9},{9,8},{10,11... | collective-permute-start | bytes 589832 | tf_op jit(solution)/shard_map/ppermute | solution.py:30
  40.8 0.7 collective-permute-start.10
  41.4 4.3 %collective-permute-start.11 = (f32[384,128]{1,0:T(8,128)S(1)}, f32[384,128]{1,0:T(8,128)S(1)}, u32[]{:S(2)}, u32[]{:S(2)}) collective-permute-start(f32[384,128]{1,0:T(8,128)S(1)} %get-tuple-element.52), channel_id=1, source_target_pairs={{0,4},{4,0},{8,12},{12,8},{16,20},{20,16},{24,28},{28,24},{1,5},{5... | collective-permute-start | bytes 589832 | tf_op jit(solution)/shard_map/ppermute | solution.py:30
  45.8 0.0 collective-permute-done.8.ri2
  45.8 0.0 collective-permute-done.9.rr1
  45.8 0.0 collective-permute-done.10.rr2
  45.8 1.1 %collective-permute-done.11.ri1 = f32[384,128]{1,0:T(8,128)S(1)} collective-permute-done((f32[384,128]{1,0:T(8,128)S(1)}, f32[384,128]{1,0:T(8,128)S(1)}, u32[]{:S(2)}, u32[]{:S(2)}) %collective-permute-start.11) | collective-permute-done | bytes 196640 | tf_op jit(solution)/shard_map/ppermute | solution.py:30
  46.8 5.1 %shard_map.92 = (f32[2,256,256]{2,1,0:T(8,128)S(1)}, f32[3,256,256]{2,1,0:T(8,128)S(1)}, f32[8,128]{1,0:T(8,128)S(1)}) custom-call(s32[7]{0:T(128)S(1)} %pad_add_fusion.frames, f32[384,128]{1,0:T(8,128)S(1)} %collective-permute-done.8.ri2, f32[384,128]{1,0:T(8,128)S(1)} %collective-permute-done.9.rr1, f32[384,128]{1,0:T(8,128)S(1)} %collective-permute-done.10.rr2, ...), custom_call_target="tpu_custom_call" | custom-call | flops 3221225472 | bytes 8003612 | tf_op jit(solution)/shard_map/pallas_call | solution.py:539
  51.9 0.1 collective-permute-start.12
  52.0 1.8 %shard_map.93.rest_0_ = f32[2,3,384,128]{3,2,1,0:T(8,128)S(1)} custom-call(s32[7]{0:T(128)S(1)} %pad_add_fusion.frames, f32[3,256,256]{2,1,0:T(8,128)S(1)} %get-tuple-element.55.projected, bf16[4,2,256,256]{3,2,1,0:T(8,128)(2,1)S(1)} %get-tuple-element.40.probe, bf16[3,4,256,512]{3,2,1,0:T(8,128)(2,1)S(1)} %shard_map.89.weights, ...), custom_call_target="tpu_custom_call" | custom-call | flops 1073741824 | bytes 6684700 | tf_op jit(solution)/shard_map/pallas_call | solution.py:539
  53.8 0.0 collective-permute-done.12.refs_1_
  53.9 2.7 %collective-permute-start.13 = (f32[8,128]{1,0:T(8,128)S(1)}, f32[8,128]{1,0:T(8,128)S(1)}, u32[]{:S(2)}, u32[]{:S(2)}) collective-permute-start(f32[8,128]{1,0:T(8,128)S(1)} %shard_map.94.refs_0_), channel_id=1, source_target_pairs={{0,8},{4,12},{8,0},{12,4},{16,24},{20,28},{24,16},{28,20},{1,9},{5... | collective-permute-start | bytes 12296 | tf_op jit(solution)/shard_map/ppermute | solution.py:514
  56.5 3.0 %shard_map.95.total = f32[2,3,384,128]{3,2,1,0:T(8,128)S(1)} custom-call(s32[7]{0:T(128)S(1)} %pad_add_fusion.frames, f32[3,256,256]{2,1,0:T(8,128)S(1)} %get-tuple-element.55.projected, bf16[4,2,256,256]{3,2,1,0:T(8,128)(2,1)S(1)} %get-tuple-element.40.probe, bf16[3,4,256,512]{3,2,1,0:T(8,128)(2,1)S(1)} %shard_map.89.weights, ...), custom_call_target="tpu_custom_call", output_to_operand_aliasing={{}: (5, {})} | custom-call | flops 2147483648 | bytes 7864348 | tf_op jit(solution)/shard_map/pallas_call | solution.py:539
  59.5 0.0 collective-permute-done.13.refs_1_
  59.6 0.7 collective-permute-start.14
  60.3 2.0 %collective-permute-start.15 = (f32[384,128]{1,0:T(8,128)S(1)}, f32[384,128]{1,0:T(8,128)S(1)}, u32[]{:S(2)}, u32[]{:S(2)}) collective-permute-start(f32[384,128]{1,0:T(8,128)S(1)} %get-tuple-element.61), channel_id=1, source_target_pairs={{0,4},{4,0},{8,12},{12,8},{16,20},{20,16},{24,28},{28,24},{1,5},{5... | collective-permute-start | bytes 589832 | tf_op jit(solution)/shard_map/ppermute | solution.py:30
  62.3 4.1 %collective-permute-start.18 = (f32[8,128]{1,0:T(8,128)S(1)}, f32[8,128]{1,0:T(8,128)S(1)}, u32[]{:S(2)}, u32[]{:S(2)}) collective-permute-start(f32[8,128]{1,0:T(8,128)S(1)} %shard_map.96.rest_0_), channel_id=1, source_target_pairs={{0,3},{1,2},{2,1},{3,0},{4,7},{5,6},{6,5},{7,4},{8,11},{9,10},{10,... | collective-permute-start | bytes 12296 | tf_op jit(solution)/shard_map/ppermute | solution.py:514
  66.3 2.6 %collective-permute-start.17 = (f32[8,128]{1,0:T(8,128)S(1)}, f32[8,128]{1,0:T(8,128)S(1)}, u32[]{:S(2)}, u32[]{:S(2)}) collective-permute-start(f32[8,128]{1,0:T(8,128)S(1)} %shard_map.96.rest_0_), channel_id=1, source_target_pairs={{0,2},{1,3},{2,0},{3,1},{4,6},{5,7},{6,4},{7,5},{8,10},{9,11},{10,... | collective-permute-start | bytes 12296 | tf_op jit(solution)/shard_map/ppermute | solution.py:514
  69.0 0.3 collective-permute-start.16
  69.2 0.0 collective-permute-done.18.rest_3_
  69.3 1.6 %collective-permute-done.17.rest_2_ = f32[8,128]{1,0:T(8,128)S(1)} collective-permute-done((f32[8,128]{1,0:T(8,128)S(1)}, f32[8,128]{1,0:T(8,128)S(1)}, u32[]{:S(2)}, u32[]{:S(2)}) %collective-permute-start.17) | collective-permute-done | bytes 4128 | tf_op jit(solution)/shard_map/ppermute | solution.py:514
  70.8 1.7 %collective-permute-done.16.rest_1_ = f32[8,128]{1,0:T(8,128)S(1)} collective-permute-done((f32[8,128]{1,0:T(8,128)S(1)}, f32[8,128]{1,0:T(8,128)S(1)}, u32[]{:S(2)}, u32[]{:S(2)}) %collective-permute-start.16) | collective-permute-done | bytes 4128 | tf_op jit(solution)/shard_map/ppermute | solution.py:514
  72.6 0.0 collective-permute-done.14.second
  72.6 0.0 collective-permute-done.15.first
  72.6 0.2 shard_map.98
  72.8 0.7 collective-permute-start.19
  73.4 3.1 %collective-permute-start.20 = (f32[256,128]{1,0:T(8,128)S(1)}, f32[256,128]{1,0:T(8,128)S(1)}, u32[]{:S(2)}, u32[]{:S(2)}) collective-permute-start(f32[256,128]{1,0:T(8,128)S(1)} %get-tuple-element.64), channel_id=1, source_target_pairs={{0,1},{1,0},{2,3},{3,2},{4,5},{5,4},{6,7},{7,6},{8,9},{9,8},{10,11... | collective-permute-start | bytes 393224 | tf_op jit(solution)/shard_map/ppermute | solution.py:30
  76.5 0.4 collective-permute-start.21
  76.9 3.2 %collective-permute-done.21.rest_1_ = f32[8,128]{1,0:T(8,128)S(1)} collective-permute-done((f32[8,128]{1,0:T(8,128)S(1)}, f32[8,128]{1,0:T(8,128)S(1)}, u32[]{:S(2)}, u32[]{:S(2)}) %collective-permute-start.21) | collective-permute-done | bytes 4128 | tf_op jit(solution)/shard_map/ppermute | solution.py:514
  80.1 0.0 collective-permute-done.19.second
  80.1 0.0 collective-permute-done.20.first
  80.2 1.3 %shard_map.99 = (f32[2,256,256]{2,1,0:T(8,128)}, f32[2,256,256]{2,1,0:T(8,128)}) custom-call(f32[256,128]{1,0:T(8,128)S(1)} %collective-permute-done.19.second, f32[256,128]{1,0:T(8,128)S(1)} %collective-permute-done.20.first, f32[2,256,256]{2,1,0:T(8,128)S(1)} %get-tuple-element.35.g, f32[2,256,256]{2,1,0:T(8,128)S(1)} %get-tuple-element.65.image, ...), custom_call_target="tpu_custom_call" | custom-call | bytes 3153920 | tf_op jit(solution)/shard_map/pallas_call | solution.py:539
  (3 shorter events, 0.1 us)
Async XLA Ops:
  1.6 6.1 %collective-permute-start = (f32[2,64,256]{2,1,0:T(8,128)S(1)}, f32[2,64,256]{2,1,0:T(8,128)S(1)}, u32[]{:S(2)}, u32[]{:S(2)}) collective-permute-start(f32[2,64,256]{2,1,0:T(8,128)S(1)} %get-tuple-element.36), channel_id=1, source_target_pairs={{0,4},{4,0},{8,12},{12,8},{16,20},{20,16},{24,28},{28,24},{1,5},{5... | collective-permute-start | bytes 393224 | tf_op jit(solution)/shard_map/ppermute | solution.py:30
  2.2 5.5 %collective-permute-start.1 = (f32[2,64,256]{2,1,0:T(8,128)S(1)}, f32[2,64,256]{2,1,0:T(8,128)S(1)}, u32[]{:S(2)}, u32[]{:S(2)}) collective-permute-start(f32[2,64,256]{2,1,0:T(8,128)S(1)} %get-tuple-element.37), channel_id=1, source_target_pairs={{4,8},{8,4},{12,16},{16,12},{20,24},{24,20},{5,9},{9,5},{13,17},{1... | collective-permute-start | bytes 393224 | tf_op jit(solution)/shard_map/ppermute | solution.py:30
  7.9 6.8 %collective-permute-start.2 = (f32[384,128]{1,0:T(8,128)S(1)}, f32[384,128]{1,0:T(8,128)S(1)}, u32[]{:S(2)}, u32[]{:S(2)}) collective-permute-start(f32[384,128]{1,0:T(8,128)S(1)} %get-tuple-element.38), channel_id=1, source_target_pairs={{0,1},{1,0},{2,3},{3,2},{4,5},{5,4},{6,7},{7,6},{8,9},{9,8},{10,11... | collective-permute-start | bytes 589832 | tf_op jit(solution)/shard_map/ppermute | solution.py:30
  10.6 4.1 %collective-permute-start.3 = (f32[384,128]{1,0:T(8,128)S(1)}, f32[384,128]{1,0:T(8,128)S(1)}, u32[]{:S(2)}, u32[]{:S(2)}) collective-permute-start(f32[384,128]{1,0:T(8,128)S(1)} %get-tuple-element.39), channel_id=1, source_target_pairs={{1,2},{2,1},{5,6},{6,5},{9,10},{10,9},{13,14},{14,13},{17,18},{18,... | collective-permute-start | bytes 589832 | tf_op jit(solution)/shard_map/ppermute | solution.py:30
  23.1 12.5 %collective-permute-start.4 = (f32[384,128]{1,0:T(8,128)S(1)}, f32[384,128]{1,0:T(8,128)S(1)}, u32[]{:S(2)}, u32[]{:S(2)}) collective-permute-start(f32[384,128]{1,0:T(8,128)S(1)} %get-tuple-element.44), channel_id=1, source_target_pairs={{4,8},{8,4},{12,16},{16,12},{20,24},{24,20},{5,9},{9,5},{13,17},{1... | collective-permute-start | bytes 589832 | tf_op jit(solution)/shard_map/ppermute | solution.py:30
  23.8 11.8 %collective-permute-start.5 = (f32[384,128]{1,0:T(8,128)S(1)}, f32[384,128]{1,0:T(8,128)S(1)}, u32[]{:S(2)}, u32[]{:S(2)}) collective-permute-start(f32[384,128]{1,0:T(8,128)S(1)} %get-tuple-element.45), channel_id=1, source_target_pairs={{0,1},{1,0},{2,3},{3,2},{4,5},{5,4},{6,7},{7,6},{8,9},{9,8},{10,11... | collective-permute-start | bytes 589832 | tf_op jit(solution)/shard_map/ppermute | solution.py:30
  23.9 11.7 %collective-permute-start.6 = (f32[384,128]{1,0:T(8,128)S(1)}, f32[384,128]{1,0:T(8,128)S(1)}, u32[]{:S(2)}, u32[]{:S(2)}) collective-permute-start(f32[384,128]{1,0:T(8,128)S(1)} %get-tuple-element.46), channel_id=1, source_target_pairs={{1,2},{2,1},{5,6},{6,5},{9,10},{10,9},{13,14},{14,13},{17,18},{18,... | collective-permute-start | bytes 589832 | tf_op jit(solution)/shard_map/ppermute | solution.py:30
  24.6 12.1 %collective-permute-start.7 = (f32[384,128]{1,0:T(8,128)S(1)}, f32[384,128]{1,0:T(8,128)S(1)}, u32[]{:S(2)}, u32[]{:S(2)}) collective-permute-start(f32[384,128]{1,0:T(8,128)S(1)} %get-tuple-element.47), channel_id=1, source_target_pairs={{0,4},{4,0},{8,12},{12,8},{16,20},{20,16},{24,28},{28,24},{1,5},{5... | collective-permute-start | bytes 589832 | tf_op jit(solution)/shard_map/ppermute | solution.py:30
  36.9 8.9 %collective-permute-start.8 = (f32[384,128]{1,0:T(8,128)S(1)}, f32[384,128]{1,0:T(8,128)S(1)}, u32[]{:S(2)}, u32[]{:S(2)}) collective-permute-start(f32[384,128]{1,0:T(8,128)S(1)} %get-tuple-element.49), channel_id=1, source_target_pairs={{4,8},{8,4},{12,16},{16,12},{20,24},{24,20},{5,9},{9,5},{13,17},{1... | collective-permute-start | bytes 589832 | tf_op jit(solution)/shard_map/ppermute | solution.py:30
  37.6 8.2 %collective-permute-start.9 = (f32[384,128]{1,0:T(8,128)S(1)}, f32[384,128]{1,0:T(8,128)S(1)}, u32[]{:S(2)}, u32[]{:S(2)}) collective-permute-start(f32[384,128]{1,0:T(8,128)S(1)} %get-tuple-element.50), channel_id=1, source_target_pairs={{0,1},{1,0},{2,3},{3,2},{4,5},{5,4},{6,7},{7,6},{8,9},{9,8},{10,11... | collective-permute-start | bytes 589832 | tf_op jit(solution)/shard_map/ppermute | solution.py:30
  40.8 5.0 %collective-permute-start.10 = (f32[384,128]{1,0:T(8,128)S(1)}, f32[384,128]{1,0:T(8,128)S(1)}, u32[]{:S(2)}, u32[]{:S(2)}) collective-permute-start(f32[384,128]{1,0:T(8,128)S(1)} %get-tuple-element.51), channel_id=1, source_target_pairs={{1,2},{2,1},{5,6},{6,5},{9,10},{10,9},{13,14},{14,13},{17,18},{18,... | collective-permute-start | bytes 589832 | tf_op jit(solution)/shard_map/ppermute | solution.py:30
  41.4 5.4 %collective-permute-start.11 = (f32[384,128]{1,0:T(8,128)S(1)}, f32[384,128]{1,0:T(8,128)S(1)}, u32[]{:S(2)}, u32[]{:S(2)}) collective-permute-start(f32[384,128]{1,0:T(8,128)S(1)} %get-tuple-element.52), channel_id=1, source_target_pairs={{0,4},{4,0},{8,12},{12,8},{16,20},{20,16},{24,28},{28,24},{1,5},{5... | collective-permute-start | bytes 589832 | tf_op jit(solution)/shard_map/ppermute | solution.py:30
  51.9 1.9 %collective-permute-start.12 = (f32[8,128]{1,0:T(8,128)S(1)}, f32[8,128]{1,0:T(8,128)S(1)}, u32[]{:S(2)}, u32[]{:S(2)}) collective-permute-start(f32[8,128]{1,0:T(8,128)S(1)} %get-tuple-element.56.refs_0_), channel_id=1, source_target_pairs={{0,4},{4,0},{8,12},{12,8},{16,20},{20,16},{24,28},{28,24},{1,5},{5... | collective-permute-start | bytes 12296 | tf_op jit(solution)/shard_map/ppermute | solution.py:514
  53.9 5.7 %collective-permute-start.13 = (f32[8,128]{1,0:T(8,128)S(1)}, f32[8,128]{1,0:T(8,128)S(1)}, u32[]{:S(2)}, u32[]{:S(2)}) collective-permute-start(f32[8,128]{1,0:T(8,128)S(1)} %shard_map.94.refs_0_), channel_id=1, source_target_pairs={{0,8},{4,12},{8,0},{12,4},{16,24},{20,28},{24,16},{28,20},{1,9},{5... | collective-permute-start | bytes 12296 | tf_op jit(solution)/shard_map/ppermute | solution.py:514
  59.6 13.0 %collective-permute-start.14 = (f32[384,128]{1,0:T(8,128)S(1)}, f32[384,128]{1,0:T(8,128)S(1)}, u32[]{:S(2)}, u32[]{:S(2)}) collective-permute-start(f32[384,128]{1,0:T(8,128)S(1)} %get-tuple-element.60), channel_id=1, source_target_pairs={{4,8},{8,4},{12,16},{16,12},{20,24},{24,20},{5,9},{9,5},{13,17},{1... | collective-permute-start | bytes 589832 | tf_op jit(solution)/shard_map/ppermute | solution.py:30
  60.3 12.3 %collective-permute-start.15 = (f32[384,128]{1,0:T(8,128)S(1)}, f32[384,128]{1,0:T(8,128)S(1)}, u32[]{:S(2)}, u32[]{:S(2)}) collective-permute-start(f32[384,128]{1,0:T(8,128)S(1)} %get-tuple-element.61), channel_id=1, source_target_pairs={{0,4},{4,0},{8,12},{12,8},{16,20},{20,16},{24,28},{28,24},{1,5},{5... | collective-permute-start | bytes 589832 | tf_op jit(solution)/shard_map/ppermute | solution.py:30
  62.3 7.0 %collective-permute-start.18 = (f32[8,128]{1,0:T(8,128)S(1)}, f32[8,128]{1,0:T(8,128)S(1)}, u32[]{:S(2)}, u32[]{:S(2)}) collective-permute-start(f32[8,128]{1,0:T(8,128)S(1)} %shard_map.96.rest_0_), channel_id=1, source_target_pairs={{0,3},{1,2},{2,1},{3,0},{4,7},{5,6},{6,5},{7,4},{8,11},{9,10},{10,... | collective-permute-start | bytes 12296 | tf_op jit(solution)/shard_map/ppermute | solution.py:514
  66.3 4.5 %collective-permute-start.17 = (f32[8,128]{1,0:T(8,128)S(1)}, f32[8,128]{1,0:T(8,128)S(1)}, u32[]{:S(2)}, u32[]{:S(2)}) collective-permute-start(f32[8,128]{1,0:T(8,128)S(1)} %shard_map.96.rest_0_), channel_id=1, source_target_pairs={{0,2},{1,3},{2,0},{3,1},{4,6},{5,7},{6,4},{7,5},{8,10},{9,11},{10,... | collective-permute-start | bytes 12296 | tf_op jit(solution)/shard_map/ppermute | solution.py:514
  69.0 3.6 %collective-permute-start.16 = (f32[8,128]{1,0:T(8,128)S(1)}, f32[8,128]{1,0:T(8,128)S(1)}, u32[]{:S(2)}, u32[]{:S(2)}) collective-permute-start(f32[8,128]{1,0:T(8,128)S(1)} %shard_map.96.rest_0_), channel_id=1, source_target_pairs={{0,1},{1,0},{2,3},{3,2},{4,5},{5,4},{6,7},{7,6},{8,9},{9,8},{10,11... | collective-permute-start | bytes 12296 | tf_op jit(solution)/shard_map/ppermute | solution.py:514
  72.8 7.4 %collective-permute-start.19 = (f32[256,128]{1,0:T(8,128)S(1)}, f32[256,128]{1,0:T(8,128)S(1)}, u32[]{:S(2)}, u32[]{:S(2)}) collective-permute-start(f32[256,128]{1,0:T(8,128)S(1)} %get-tuple-element.63), channel_id=1, source_target_pairs={{1,2},{2,1},{5,6},{6,5},{9,10},{10,9},{13,14},{14,13},{17,18},{18,... | collective-permute-start | bytes 393224 | tf_op jit(solution)/shard_map/ppermute | solution.py:30
  73.4 6.7 %collective-permute-start.20 = (f32[256,128]{1,0:T(8,128)S(1)}, f32[256,128]{1,0:T(8,128)S(1)}, u32[]{:S(2)}, u32[]{:S(2)}) collective-permute-start(f32[256,128]{1,0:T(8,128)S(1)} %get-tuple-element.64), channel_id=1, source_target_pairs={{0,1},{1,0},{2,3},{3,2},{4,5},{5,4},{6,7},{7,6},{8,9},{9,8},{10,11... | collective-permute-start | bytes 393224 | tf_op jit(solution)/shard_map/ppermute | solution.py:30
  76.5 3.6 %collective-permute-start.21 = (f32[8,128]{1,0:T(8,128)S(1)}, f32[8,128]{1,0:T(8,128)S(1)}, u32[]{:S(2)}, u32[]{:S(2)}) collective-permute-start(f32[8,128]{1,0:T(8,128)S(1)} %get-tuple-element.67.rest_0_), channel_id=1, source_target_pairs={{0,16},{4,20},{8,24},{12,28},{16,0},{20,4},{24,8},{28,12},{1,17},{... | collective-permute-start | bytes 12296 | tf_op jit(solution)/shard_map/ppermute | solution.py:514

commit v3 on v2

--- a/solution.py
+++ b/solution.py
@@ -65,8 +65,8 @@
 
 
 def shifted_place(frames, k, blocks):
-    row = HALO + frames[1 + k]
-    col = frames[1 + frames.shape[0] // 2 + k]
+    row = HALO + frames[1][0, k]
+    col = frames[1][1, k]
     first = jnp.where(col < 0, blocks - 1, 0)
     places = [lax.rem(first + i, blocks) for i in range(blocks)]
     return (row, places, jnp.where(col < 0, col + 128, col))
@@ -199,50 +199,77 @@
     return put
 
 
-def halo_rows_kernel(g, first, second, arrived):
-    n = g.shape[1]
-
+def halo_kernel(g, row1, row2, col1, col2, ends, arrived):
+    n, width = g.shape[1:]
+
+    def move(source, to, i):
+        return pltpu.make_async_copy(source, to, arrived.at[i])
+
+    sides = [move(g.at[:, :, at : at + 128], ends.at[i], i) for i, at in enumerate((0, width - 128))]
+    for side in sides:
+        side.start()
     low, high = (g.at[:, :HALO], g.at[:, n - HALO :])
     by_parity(
         "wide",
         lambda: low,
         lambda: high,
-        lambda source: pltpu.make_async_copy(source, first, arrived.at[0]).start(),
-        lambda source: pltpu.make_async_copy(source, second, arrived.at[1]).start(),
-    )
-    pltpu.make_async_copy(low, first, arrived.at[0]).wait()
-    pltpu.make_async_copy(low, second, arrived.at[1]).wait()
-
-
-def fill_rows(ext, g, first, second):
-    n, width = (g.shape[1], g.shape[2])
-    above, below = lower_upper("wide", first[...], second[...])
-    for b in range(width // 128):
+        lambda source: move(source, row1, 2).start(),
+        lambda source: move(source, row2, 3).start(),
+    )
+    for side in sides:
+        side.wait()
+    half = lanes_low(col1.shape)
+    by_parity(
+        "narrow",
+        lambda: jnp.where(half, ends[0, 0], pltpu.roll(ends[0, 1], HALO, 1)),
+        lambda: jnp.where(half, pltpu.roll(ends[1, 1], HALO, 1), ends[1, 0]),
+        store(col1),
+        store(col2),
+    )
+    move(low, row1, 2).wait()
+    move(low, row2, 3).wait()
+
+
+def fill_cols(put, first, second):
+    left, right = lower_upper("narrow", first[...], second[...])
+    low = lanes_low(right.shape)
+    put(0, jnp.where(low, right, left))
+    put(1, pltpu.roll(jnp.where(low, left, right), HALO, 1))
+
+
+def corners_kernel(col2, col1, first, second, beside):
+    n = beside.shape[1]
+
+    def put(q, value):
+        beside[q] = value
+
+    fill_cols(put, col1, col2)
+    by_parity(
+        "wide",
+        lambda: beside[:, :HALO],
+        lambda: beside[:, n - HALO :],
+        store(first),
+        store(second),
+    )
+
+
+def fill_tile(ext, g, row1, row2, col1, col2, corner1, corner2):
+    n, width = g.shape[1:]
+    last = width // 128
+    above, below = lower_upper("wide", row1[...], row2[...])
+    for b in range(last):
         cols = slice(128 * b, 128 * (b + 1))
         ext[:, b, :HALO] = above[:, :, cols]
         ext[:, b, HALO : HALO + n] = g[:, :, cols]
         ext[:, b, HALO + n :] = below[:, :, cols]
 
-
-def halo_cols_kernel(second, first, g, out_first, out_second, ext):
-    last = g.shape[2] // 128 - 1
-    fill_rows(ext, g, first, second)
-    low = lanes_low(out_first.shape)
-    by_parity(
-        "narrow",
-        lambda: jnp.where(low, ext[0, 0], pltpu.roll(ext[1, 0], HALO, 1)),
-        lambda: jnp.where(low, pltpu.roll(ext[1, last], HALO, 1), ext[0, last]),
-        store(out_first),
-        store(out_second),
-    )
-
-
-def fill_cols(ext, first, second):
-    left, right = lower_upper("narrow", first[...], second[...])
-    last = ext.shape[1] - 1
-    low = lanes_low(right.shape)
-    ext[0, last] = jnp.where(low, right, left)
-    ext[1, last] = pltpu.roll(jnp.where(low, left, right), HALO, 1)
+    def put(q, value):
+        ext[q, last, HALO : HALO + n] = value
+
+    fill_cols(put, col1, col2)
+    above, below = lower_upper("wide", corner1[...], corner2[...])
+    ext[:, last, :HALO] = above
+    ext[:, last, HALO + n :] = below
 
 
 def sort_weights(frames, w, sorter, out, held, arrived, begin, end, meanwhile):
@@ -255,7 +282,7 @@
 
     for k in range(begin, end):
 
-        @pl.when(k < frames[0])
+        @pl.when(k < frames[0][0])
         def _():
             fetch(k).start()
 
@@ -269,13 +296,14 @@
             out[k, m] = cat([re[:, :h], im[:, :h], re[:, h:], im[:, h:]], 1).astype(BF16)
         return carried
 
-    lax.fori_loop(begin, jnp.minimum(end, frames[0]), visit, 0)
+    lax.fori_loop(begin, jnp.minimum(end, frames[0][0]), visit, 0)
 
 
 def prepare_kernel(
-    frames, w, sorter_far, probe_far, tables_far, g_far,
-    out, sorter, probe, tables, g, held, arrived, loaded,
+    counts, corner, w, sorter_far, probe_far, tables_far, g_far,
+    out, probe, tables, g, held, sorter, arrived, loaded,
 ):
+    frames = (counts, None)
     moves = ((sorter_far, sorter), (g_far, g), (probe_far, probe), (tables_far, tables))
     moves = [pltpu.make_async_copy(a, b, loaded.at[i]) for i, (a, b) in enumerate(moves)]
     moves[0].start()
@@ -285,21 +313,17 @@
             move.start()
         moves[0].wait()
 
-    sort_weights(frames, w, sorter, out, held, arrived, 0, 1, meanwhile)
+    sort_weights(frames, w, sorter, out, held, arrived, 0, w.shape[0], meanwhile)
     for move in moves[1:]:
         move.wait()
 
 
-def prepare_rest_kernel(frames, w, sorter, first, out, held, arrived):
-    sort_weights(frames, w, sorter, out, held, arrived, 1, w.shape[0], lambda: None)
-
-
 def first_pass_kernel(
-    frames, g, row1, row2, col1, col2, probe, weights, tables,
+    counts, offsets, row2, row1, g, col1, col2, corner1, corner2, probe, weights, tables,
     total, sums, sr1, sr2, si1, si2, ext, patch, stage,
 ):
-    fill_rows(ext, g, row1, row2)
-    fill_cols(ext, col1, col2)
+    frames = (counts, offsets)
+    fill_tile(ext, g, row1, row2, col1, col2, corner1, corner2)
     total[...] = jnp.zeros_like(total)
 
     def visit(k, energy):
@@ -308,7 +332,7 @@
         put_patch(total, frames, k, back_project(pe, po, probe, weights, k, tables, stage))
         return energy + square_sum(pe) + square_sum(po)
 
-    energy = lax.fori_loop(0, frames[0], visit, F32(0.0))
+    energy = lax.fori_loop(0, frames[0][0], visit, F32(0.0))
     sums[...] = scalar_tile([square_sum(g[...]), energy])
     send_row_bands(total, 0, sr1, sr2)
     send_col_bands(total, 1, si1, si2)
@@ -361,9 +385,10 @@
 
 
 def second_forward_kernel(
-    last_row, last_col, frames, ri2, rr1, rr2, ri1, total, sums, probe, weights, tables,
+    last_row, last_col, counts, offsets, ri2, rr1, rr2, ri1, total, sums, probe, weights, tables,
     image, projected, all_sums, ext, patch, stage,
 ):
+    frames = (counts, offsets)
     last = ext.shape[1] - 1
     n = ext.shape[2]
     ext[...] = total[...]
@@ -397,14 +422,15 @@
         projected[k] = cat([pe, po], 1)
         return energy + square_sum(pe) + square_sum(po)
 
-    energy = lax.fori_loop(0, frames[0], visit, F32(0.0))
+    energy = lax.fori_loop(0, frames[0][0], visit, F32(0.0))
     rows = lax.broadcasted_iota(jnp.int32, (8, 128), 0)
     all_sums[...] = jnp.where(
         rows == 2, square_sum(image[...]), jnp.where(rows == 3, energy, sums[...])
     )
 
 
-def second_backward_kernel(begin, end, frames, projected, probe, weights, tables, *rest):
+def second_backward_kernel(begin, end, counts, offsets, projected, probe, weights, tables, *rest):
+    frames = (counts, offsets)
     total, stage = rest[-2:]
     h = projected.shape[2] // 2
     if begin == 0:
@@ -416,7 +442,7 @@
         put_patch(total, frames, k, parts)
         return carried
 
-    lax.fori_loop(begin, jnp.minimum(end, frames[0]), visit, 0)
+    lax.fori_loop(begin, jnp.minimum(end, frames[0][0]), visit, 0)
 
 
 def send_margins_kernel(total, first, second):
@@ -548,23 +574,17 @@
     )(*args)
 
 
-def prepare(frames, w, probe, tables, g):
+def prepare(counts, corner, w, probe, tables, g):
     slots, modes, parts, rows, cols = w.shape
     sorter = sorting_tables(cols)
     weights = jax.ShapeDtypeStruct((slots, modes, rows, parts * cols), BF16)
-    sort_flops = 8 * modes * rows * cols * rows
-    scratch = [pltpu.VMEM(w.shape, BF16), pltpu.SemaphoreType.DMA((slots,))]
-    outs = [jax.ShapeDtypeStruct(x.shape, x.dtype) for x in (sorter, probe, tables, g)]
-    weights, sorter, probe, tables, g = call(
-        prepare_kernel, [weights] + outs, 1, [frames, w, sorter, probe, tables, g],
-        scratch + [pltpu.SemaphoreType.DMA((4,))], sort_flops, far=(1, 2, 3, 4, 5),
-    )
-    if slots > 1:
-        weights = call(
-            prepare_rest_kernel, [weights], 1, [frames, w, sorter, weights],
-            scratch, (slots - 1) * sort_flops, {3: 0}, (1,),
-        )[0]
-    return (weights, probe, tables, g)
+    outs = [jax.ShapeDtypeStruct(x.shape, x.dtype) for x in (probe, tables, g)]
+    scratch = [pltpu.VMEM(x.shape, BF16) for x in (w, sorter)]
+    scratch += [pltpu.SemaphoreType.DMA((slots,)), pltpu.SemaphoreType.DMA((4,))]
+    return call(
+        prepare_kernel, [weights] + outs, 1, [counts, corner, w, sorter, probe, tables, g],
+        scratch, 8 * slots * modes * rows * cols * rows, far=(2, 3, 4, 5, 6),
+    )
 
 
 def local(gradient, probe_modes, mode_weights, offsets, counts):
@@ -572,7 +592,8 @@
     slots, modes = weights.shape[:2]
     rows, width = gradient.shape[1:]
     tall, blocks = (rows + 2 * HALO, width // 128 + 1)
-    frames = jnp.concatenate([counts.reshape(-1), jnp.swapaxes(offsets, 2, 3).reshape(-1)])
+    counts = counts.reshape(-1)
+    offsets = jnp.swapaxes(offsets, 2, 3).reshape(offsets.shape[3], offsets.shape[2])
     tables = half_tables(width)
     pass_flops = 8 * 2 * slots * modes * 2 * width * width * width
     extended = pltpu.VMEM((2, blocks, tall, 128), F32)
@@ -580,26 +601,30 @@
     stage = pltpu.VMEM((2, modes, rows, width), BF16)
     whole = shape(2, blocks, tall, 128)
 
-    row_sends = call(
-        halo_rows_kernel, [shape(2, HALO, width)] * 2, 0, [gradient],
-        [pltpu.SemaphoreType.DMA((2,))], far=(0,),
-    )
-    row2, row1 = (swap(row_sends[1], "wide", 1), swap(row_sends[0], "wide", 0))
+    row_strip, col_strip, corner = (shape(2, HALO, width), shape(rows, 128), shape(2, HALO, 128))
+    row1, row2, col1, col2 = call(
+        halo_kernel, [row_strip, row_strip, col_strip, col_strip], 0, [gradient],
+        [pltpu.VMEM((2, 2, rows, 128), F32), pltpu.SemaphoreType.DMA((4,))], far=(0,),
+    )
+    col1, col2 = (swap(col1, "narrow", 0), swap(col2, "narrow", 1))
+    row2, row1 = (swap(row2, "wide", 1), swap(row1, "wide", 0))
+    corner1, corner2 = call(
+        corners_kernel, [corner, corner], 0, [col2, col1], [pltpu.VMEM((2, rows, 128), F32)]
+    )
     sorted_weights, probe_modes, tables, gradient = prepare(
-        frames, weights, probe_modes, tables, gradient
-    )
-    col_sends = call(
-        halo_cols_kernel, [shape(tall, 128)] * 2, 0, [row2, row1, gradient],
-        [pltpu.VMEM((2, blocks, tall, 128), F32)],
-    )
-    col1, col2 = (swap(x, "narrow", i) for i, x in enumerate(col_sends))
+        counts, corner1, weights, probe_modes, tables, gradient
+    )
+    corner2, corner1 = (swap(corner2, "wide", 1), swap(corner1, "wide", 0))
 
     row_band, col_band = (shape(blocks * 2 * HALO, 128), shape(tall, 128))
     total, sums, sr1, sr2, si1, si2 = call(
         first_pass_kernel,
         [whole, shape(8, 128), row_band, row_band, col_band, col_band],
-        1,
-        [frames, gradient, row1, row2, col1, col2, probe_modes, sorted_weights, tables],
+        2,
+        [
+            counts, offsets, row2, row1, gradient, col1, col2, corner1, corner2,
+            probe_modes, sorted_weights, tables,
+        ],
         [extended, patch, stage],
         pass_flops,
     )
@@ -621,9 +646,9 @@
             second_forward_kernel, lax.axis_size("wide") - 1, lax.axis_size("narrow") - 1
         ),
         [shape(2, rows, width), shape(slots, rows, width), shape(8, 128)],
-        1,
+        2,
         [
-            frames, si2, sr1, sr2, si1, total, sums, probe_modes, sorted_weights, tables,
+            counts, offsets, si2, sr1, sr2, si1, total, sums, probe_modes, sorted_weights, tables,
         ],
         [extended, patch, stage],
         pass_flops // 2,
@@ -641,12 +666,12 @@
             total = call(
                 functools.partial(second_backward_kernel, begin, end),
                 [whole],
-                1,
-                [frames, projected, probe_modes, sorted_weights, tables]
+                2,
+                [counts, offsets, projected, probe_modes, sorted_weights, tables]
                 + ([] if begin == 0 else [total]),
                 [stage],
                 pass_flops // 2 * (end - begin) // slots,
-                {} if begin == 0 else {5: 0},
+                {} if begin == 0 else {6: 0},
             )[0]
         sums = add_hops(sums, rounds[i : i + 1])
         if end > 0:

time: 82.4 us -> 80.4 us (0.976)
  Pallas kernels: 28.1 us -> 19.1 us
  starting transfers between devices: 42.4 us -> 51 us
    pallas_call x14 -> x13, Pallas kernels: 28.1 us -> 19.1 us  [call(): pl.pallas_call(kernel, out_shape=[place(o.shape, o.dtype) for o in outs],...]
    ppermute x16 -> x18, starting transfers between devices: 32.3 us -> 40.7 us  [swap(): return lax.ppermute(x, axis, wanted)]
    ppermute x16 -> x18, waiting for transfers between devices: 2.15 us -> 2.16 us  [swap(): return lax.ppermute(x, axis, wanted)]
  transfers between devices with their start and end apart: 22 -> 24, of which waited for: 5 -> 7; matrix products, arithmetic and copies ran while one was open for 1% -> 0% of each run, Pallas kernels for 14% -> 8%
where the time goes in v3:
time: 80.4 us; the launch traced here: 80.1 us
  starting transfers between devices  51 us (63%)
  Pallas kernels  19.1 us (24%)
  waiting for transfers between devices  8.45 us (11%)
  between operations  1.53 us (2%)
    ppermute x18, starting transfers between devices, swap(): return lax.ppermute(x, axis, wanted)  40.7 us
    pallas_call x13, Pallas kernels, call(): pl.pallas_call(kernel, out_shape=[place(o.shape, o.dtype) for o in outs],...  19.1 us
    ppermute x6, starting transfers between devices, take_hops(): return [x] + [lax.ppermute(x, axis, perm) for axis, perm in wanted]  10.3 us
    ppermute x6, waiting for transfers between devices, take_hops(): return [x] + [lax.ppermute(x, axis, perm) for axis, perm in wanted]  6.29 us
    ppermute x18, waiting for transfers between devices, swap(): return lax.ppermute(x, axis, wanted)  2.16 us
  transfers between devices with their start and end apart: 24, of which 7 were waited for; matrix products, arithmetic and copies ran while one was open for 0% of the time, Pallas kernels for 8%

profile of v3, /device:TPU:0, one launch (start us, length us, event | category | flops | bytes accessed | tf_op | source)
XLA Modules:
  0.0 80.1 jit_solution(1676410885255393968)
XLA Ops:
  0.6 1.2 %shard_map.86 = (f32[2,64,256]{2,1,0:T(8,128)S(1)}, f32[2,64,256]{2,1,0:T(8,128)S(1)}, f32[256,128]{1,0:T(8,128)S(1)}, f32[256,128]{1,0:T(8,128)S(1)}) custom-call(f32[2,256,256]{2,1,0:T(8,128)} %g_far.1), custom_call_target="tpu_custom_call" | custom-call | bytes 1048576 | tf_op jit(solution)/shard_map/pallas_call | solution.py:565
  1.8 0.7 collective-permute-start.2
  2.5 5.9 %collective-permute-start.3 = (f32[256,128]{1,0:T(8,128)S(1)}, f32[256,128]{1,0:T(8,128)S(1)}, u32[]{:S(2)}, u32[]{:S(2)}) collective-permute-start(f32[256,128]{1,0:T(8,128)S(1)} %get-tuple-element.39), channel_id=1, source_target_pairs={{0,1},{1,0},{2,3},{3,2},{4,5},{5,4},{6,7},{7,6},{8,9},{9,8},{10,11... | collective-permute-start | bytes 393224 | tf_op jit(solution)/shard_map/ppermute | solution.py:30
  8.4 0.7 collective-permute-start
  9.1 2.9 %collective-permute-start.1 = (f32[2,64,256]{2,1,0:T(8,128)S(1)}, f32[2,64,256]{2,1,0:T(8,128)S(1)}, u32[]{:S(2)}, u32[]{:S(2)}) collective-permute-start(f32[2,64,256]{2,1,0:T(8,128)S(1)} %get-tuple-element.37), channel_id=1, source_target_pairs={{0,4},{4,0},{8,12},{12,8},{16,20},{20,16},{24,28},{28,24},{1,5},{5... | collective-permute-start | bytes 393224 | tf_op jit(solution)/shard_map/ppermute | solution.py:30
  12.7 0.0 collective-permute-done.2.col2
  12.7 0.0 collective-permute-done.3.col1
  12.7 0.1 shard_map.87
  12.8 0.7 collective-permute-start.5
  13.5 2.9 %collective-permute-start.4 = (f32[2,64,128]{2,1,0:T(8,128)S(1)}, f32[2,64,128]{2,1,0:T(8,128)S(1)}, u32[]{:S(2)}, u32[]{:S(2)}) collective-permute-start(f32[2,64,128]{2,1,0:T(8,128)S(1)} %get-tuple-element.40.corner), channel_id=1, source_target_pairs={{0,4},{4,0},{8,12},{12,8},{16,20},{20,16},{24,28},{28,24},{1,5},{5... | collective-permute-start | bytes 196616 | tf_op jit(solution)/shard_map/ppermute | solution.py:30
  16.4 0.0 copy-start
  16.4 3.0 %shard_map.88 = (bf16[3,4,256,512]{3,2,1,0:T(8,128)(2,1)S(1)}, bf16[4,2,256,256]{3,2,1,0:T(8,128)(2,1)S(1)}, bf16[4,256,256]{2,1,0:T(8,128)(2,1)S(1)}, f32[2,256,256]{2,1,0:T(8,128)S(1)}) custom-call(s32[1]{0:T(128)} %bitcast.5.counts, f32[2,64,128]{2,1,0:T(8,128)S(1)} %get-tuple-element.40.corner, bf16[3,4,2,256,256]{4,3,2,1,0:T(8,128)(2,1)} %bitcast.14, ...), custom_call_target="tpu_custom_call" | custom-call | flops 1610612736 | bytes 10813444 | tf_op jit(solution)/shard_map/pallas_call | solution.py:565
  19.4 0.0 collective-permute-done.row2
  19.4 0.0 collective-permute-done.1.row1
  19.4 0.0 collective-permute-done.5.corner2
  19.4 0.0 collective-permute-done.4.corner1
  19.5 0.0 copy-done
  19.5 5.7 %shard_map.89 = (f32[2,3,384,128]{3,2,1,0:T(8,128)S(1)}, f32[8,128]{1,0:T(8,128)S(1)}, f32[384,128]{1,0:T(8,128)S(1)}, f32[384,128]{1,0:T(8,128)S(1)}, f32[384,128]{1,0:T(8,128)S(1)}, /*index=5*/f32[384,128]{1,0:T(8,128)S(1)}) custom-call(s32[1]{0:T(128)} %bitcast.6.counts, s32[2,3]{1,0:T(2,128)S(1)} %bitcast.10, ...), custom_call_target="tpu_custom_call" | custom-call | flops 6442450944 | bytes 7868444 | tf_op jit(solution)/shard_map/pallas_call | solution.py:565
  25.2 0.7 collective-permute-start.6
  25.9 3.9 %collective-permute-start.7 = (f32[384,128]{1,0:T(8,128)S(1)}, f32[384,128]{1,0:T(8,128)S(1)}, u32[]{:S(2)}, u32[]{:S(2)}) collective-permute-start(f32[384,128]{1,0:T(8,128)S(1)} %get-tuple-element.47), channel_id=1, source_target_pairs={{0,1},{1,0},{2,3},{3,2},{4,5},{5,4},{6,7},{7,6},{8,9},{9,8},{10,11... | collective-permute-start | bytes 589832 | tf_op jit(solution)/shard_map/ppermute | solution.py:30
  29.8 0.7 collective-permute-start.8
  30.5 2.2 %collective-permute-start.9 = (f32[384,128]{1,0:T(8,128)S(1)}, f32[384,128]{1,0:T(8,128)S(1)}, u32[]{:S(2)}, u32[]{:S(2)}) collective-permute-start(f32[384,128]{1,0:T(8,128)S(1)} %get-tuple-element.49), channel_id=1, source_target_pairs={{0,4},{4,0},{8,12},{12,8},{16,20},{20,16},{24,28},{28,24},{1,5},{5... | collective-permute-start | bytes 589832 | tf_op jit(solution)/shard_map/ppermute | solution.py:30
  32.7 0.0 collective-permute-done.6.rr2
  32.7 0.9 %collective-permute-done.7.ri1 = f32[384,128]{1,0:T(8,128)S(1)} collective-permute-done((f32[384,128]{1,0:T(8,128)S(1)}, f32[384,128]{1,0:T(8,128)S(1)}, u32[]{:S(2)}, u32[]{:S(2)}) %collective-permute-start.7) | collective-permute-done | bytes 196640 | tf_op jit(solution)/shard_map/ppermute | solution.py:30
  33.6 0.0 collective-permute-done.8.ri2
  33.6 0.2 collective-permute-done.9.rr1
  33.8 0.2 shard_map.90
  34.0 0.7 collective-permute-start.10
  34.7 3.7 %collective-permute-start.11 = (f32[384,128]{1,0:T(8,128)S(1)}, f32[384,128]{1,0:T(8,128)S(1)}, u32[]{:S(2)}, u32[]{:S(2)}) collective-permute-start(f32[384,128]{1,0:T(8,128)S(1)} %get-tuple-element.52), channel_id=1, source_target_pairs={{0,1},{1,0},{2,3},{3,2},{4,5},{5,4},{6,7},{7,6},{8,9},{9,8},{10,11... | collective-permute-start | bytes 589832 | tf_op jit(solution)/shard_map/ppermute | solution.py:30
  38.3 0.7 collective-permute-start.12
  39.0 7.1 %collective-permute-start.13 = (f32[384,128]{1,0:T(8,128)S(1)}, f32[384,128]{1,0:T(8,128)S(1)}, u32[]{:S(2)}, u32[]{:S(2)}) collective-permute-start(f32[384,128]{1,0:T(8,128)S(1)} %get-tuple-element.54), channel_id=1, source_target_pairs={{0,4},{4,0},{8,12},{12,8},{16,20},{20,16},{24,28},{28,24},{1,5},{5... | collective-permute-start | bytes 589832 | tf_op jit(solution)/shard_map/ppermute | solution.py:30
  46.1 0.0 collective-permute-done.10.ri2
  46.1 0.0 collective-permute-done.11.rr1
  46.1 0.0 collective-permute-done.12.rr2
  46.1 1.1 %collective-permute-done.13.ri1 = f32[384,128]{1,0:T(8,128)S(1)} collective-permute-done((f32[384,128]{1,0:T(8,128)S(1)}, f32[384,128]{1,0:T(8,128)S(1)}, u32[]{:S(2)}, u32[]{:S(2)}) %collective-permute-start.13) | collective-permute-done | bytes 196640 | tf_op jit(solution)/shard_map/ppermute | solution.py:30
  47.2 3.7 %shard_map.91 = (f32[2,256,256]{2,1,0:T(8,128)S(1)}, f32[3,256,256]{2,1,0:T(8,128)S(1)}, f32[8,128]{1,0:T(8,128)S(1)}) custom-call(s32[1]{0:T(128)} %bitcast.7.counts, s32[2,3]{1,0:T(2,128)S(1)} %bitcast.11, f32[384,128]{1,0:T(8,128)S(1)} %collective-permute-done.10.ri2, f32[384,128]{1,0:T(8,128)S(1)} %collective-permute-done.11.rr1, ...), custom_call_target="tpu_custom_call" | custom-call | flops 3221225472 | bytes 8003612 | tf_op jit(solution)/shard_map/pallas_call | solution.py:565
  50.9 2.6 %collective-permute-start.14 = (f32[8,128]{1,0:T(8,128)S(1)}, f32[8,128]{1,0:T(8,128)S(1)}, u32[]{:S(2)}, u32[]{:S(2)}) collective-permute-start(f32[8,128]{1,0:T(8,128)S(1)} %get-tuple-element.58.refs_0_), channel_id=1, source_target_pairs={{0,4},{4,0},{8,12},{12,8},{16,20},{20,16},{24,28},{28,24},{1,5},{5... | collective-permute-start | bytes 12296 | tf_op jit(solution)/shard_map/ppermute | solution.py:540
  53.5 1.8 %shard_map.92.rest_0_ = f32[2,3,384,128]{3,2,1,0:T(8,128)S(1)} custom-call(s32[1]{0:T(128)} %bitcast.8.counts, s32[2,3]{1,0:T(2,128)S(1)} %bitcast.12, f32[3,256,256]{2,1,0:T(8,128)S(1)} %get-tuple-element.57.projected, bf16[4,2,256,256]{3,2,1,0:T(8,128)(2,1)S(1)} %get-tuple-element.43.probe, bf16[3,4,256,512]{3,2,1,0:T(8,128)(2,1)S(1)} %get-tuple-element.44.weights, ...), custom_call_target="tpu_custom_call" | custom-call | flops 1073741824 | bytes 6684700 | tf_op jit(solution)/shard_map/pallas_call | solution.py:565
  55.3 0.0 collective-permute-done.14.refs_1_
  55.3 2.9 %collective-permute-start.15 = (f32[8,128]{1,0:T(8,128)S(1)}, f32[8,128]{1,0:T(8,128)S(1)}, u32[]{:S(2)}, u32[]{:S(2)}) collective-permute-start(f32[8,128]{1,0:T(8,128)S(1)} %shard_map.93.refs_0_), channel_id=1, source_target_pairs={{0,8},{4,12},{8,0},{12,4},{16,24},{20,28},{24,16},{28,20},{1,9},{5... | collective-permute-start | bytes 12296 | tf_op jit(solution)/shard_map/ppermute | solution.py:540
  58.3 1.7 %shard_map.94.total = f32[2,3,384,128]{3,2,1,0:T(8,128)S(1)} custom-call(s32[1]{0:T(128)} %bitcast.9.counts, s32[2,3]{1,0:T(2,128)S(1)} %bitcast.13, f32[3,256,256]{2,1,0:T(8,128)S(1)} %get-tuple-element.57.projected, bf16[4,2,256,256]{3,2,1,0:T(8,128)(2,1)S(1)} %get-tuple-element.43.probe, ...), custom_call_target="tpu_custom_call", output_to_operand_aliasing={{}: (6, {})} | custom-call | flops 2147483648 | bytes 7864348 | tf_op jit(solution)/shard_map/pallas_call | solution.py:565
  60.0 0.0 collective-permute-done.15.refs_1_
  60.1 0.7 collective-permute-start.16
  60.8 3.2 %collective-permute-start.17 = (f32[384,128]{1,0:T(8,128)S(1)}, f32[384,128]{1,0:T(8,128)S(1)}, u32[]{:S(2)}, u32[]{:S(2)}) collective-permute-start(f32[384,128]{1,0:T(8,128)S(1)} %get-tuple-element.63), channel_id=1, source_target_pairs={{0,4},{4,0},{8,12},{12,8},{16,20},{20,16},{24,28},{28,24},{1,5},{5... | collective-permute-start | bytes 589832 | tf_op jit(solution)/shard_map/ppermute | solution.py:30
  64.0 1.1 %collective-permute-start.20 = (f32[8,128]{1,0:T(8,128)S(1)}, f32[8,128]{1,0:T(8,128)S(1)}, u32[]{:S(2)}, u32[]{:S(2)}) collective-permute-start(f32[8,128]{1,0:T(8,128)S(1)} %shard_map.95.rest_0_), channel_id=1, source_target_pairs={{0,3},{1,2},{2,1},{3,0},{4,7},{5,6},{6,5},{7,4},{8,11},{9,10},{10,... | collective-permute-start | bytes 12296 | tf_op jit(solution)/shard_map/ppermute | solution.py:540
  65.1 2.7 %collective-permute-start.19 = (f32[8,128]{1,0:T(8,128)S(1)}, f32[8,128]{1,0:T(8,128)S(1)}, u32[]{:S(2)}, u32[]{:S(2)}) collective-permute-start(f32[8,128]{1,0:T(8,128)S(1)} %shard_map.95.rest_0_), channel_id=1, source_target_pairs={{0,2},{1,3},{2,0},{3,1},{4,6},{5,7},{6,4},{7,5},{8,10},{9,11},{10,... | collective-permute-start | bytes 12296 | tf_op jit(solution)/shard_map/ppermute | solution.py:540
  67.8 0.6 collective-permute-start.18
  68.4 1.0 %collective-permute-done.20.rest_3_ = f32[8,128]{1,0:T(8,128)S(1)} collective-permute-done((f32[8,128]{1,0:T(8,128)S(1)}, f32[8,128]{1,0:T(8,128)S(1)}, u32[]{:S(2)}, u32[]{:S(2)}) %collective-permute-start.20) | collective-permute-done | bytes 4128 | tf_op jit(solution)/shard_map/ppermute | solution.py:540
  69.4 0.3 collective-permute-done.19.rest_2_
  69.7 1.8 %collective-permute-done.18.rest_1_ = f32[8,128]{1,0:T(8,128)S(1)} collective-permute-done((f32[8,128]{1,0:T(8,128)S(1)}, f32[8,128]{1,0:T(8,128)S(1)}, u32[]{:S(2)}, u32[]{:S(2)}) %collective-permute-start.18) | collective-permute-done | bytes 4128 | tf_op jit(solution)/shard_map/ppermute | solution.py:540
  71.5 0.0 collective-permute-done.16.second
  71.5 0.0 collective-permute-done.17.first
  71.5 0.2 shard_map.97
  71.7 0.7 collective-permute-start.21
  72.3 2.8 %collective-permute-start.22 = (f32[256,128]{1,0:T(8,128)S(1)}, f32[256,128]{1,0:T(8,128)S(1)}, u32[]{:S(2)}, u32[]{:S(2)}) collective-permute-start(f32[256,128]{1,0:T(8,128)S(1)} %get-tuple-element.66), channel_id=1, source_target_pairs={{0,1},{1,0},{2,3},{3,2},{4,5},{5,4},{6,7},{7,6},{8,9},{9,8},{10,11... | collective-permute-start | bytes 393224 | tf_op jit(solution)/shard_map/ppermute | solution.py:30
  75.1 0.4 collective-permute-start.23
  75.5 3.2 %collective-permute-done.23.rest_1_ = f32[8,128]{1,0:T(8,128)S(1)} collective-permute-done((f32[8,128]{1,0:T(8,128)S(1)}, f32[8,128]{1,0:T(8,128)S(1)}, u32[]{:S(2)}, u32[]{:S(2)}) %collective-permute-start.23) | collective-permute-done | bytes 4128 | tf_op jit(solution)/shard_map/ppermute | solution.py:540
  78.7 0.0 collective-permute-done.21.second
  78.7 0.0 collective-permute-done.22.first
  78.7 1.3 %shard_map.98 = (f32[2,256,256]{2,1,0:T(8,128)}, f32[2,256,256]{2,1,0:T(8,128)}) custom-call(f32[256,128]{1,0:T(8,128)S(1)} %collective-permute-done.21.second, f32[256,128]{1,0:T(8,128)S(1)} %collective-permute-done.22.first, f32[2,256,256]{2,1,0:T(8,128)S(1)} %get-tuple-element.41.g, f32[2,256,256]{2,1,0:T(8,128)S(1)} %get-tuple-element.67.image, ...), custom_call_target="tpu_custom_call" | custom-call | bytes 3153920 | tf_op jit(solution)/shard_map/pallas_call | solution.py:565
  (3 shorter events, 0.1 us)
Async XLA Ops:
  1.8 10.8 %collective-permute-start.2 = (f32[256,128]{1,0:T(8,128)S(1)}, f32[256,128]{1,0:T(8,128)S(1)}, u32[]{:S(2)}, u32[]{:S(2)}) collective-permute-start(f32[256,128]{1,0:T(8,128)S(1)} %get-tuple-element.38), channel_id=1, source_target_pairs={{1,2},{2,1},{5,6},{6,5},{9,10},{10,9},{13,14},{14,13},{17,18},{18,... | collective-permute-start | bytes 393224 | tf_op jit(solution)/shard_map/ppermute | solution.py:30
  2.5 10.1 %collective-permute-start.3 = (f32[256,128]{1,0:T(8,128)S(1)}, f32[256,128]{1,0:T(8,128)S(1)}, u32[]{:S(2)}, u32[]{:S(2)}) collective-permute-start(f32[256,128]{1,0:T(8,128)S(1)} %get-tuple-element.39), channel_id=1, source_target_pairs={{0,1},{1,0},{2,3},{3,2},{4,5},{5,4},{6,7},{7,6},{8,9},{9,8},{10,11... | collective-permute-start | bytes 393224 | tf_op jit(solution)/shard_map/ppermute | solution.py:30
  8.4 11.0 %collective-permute-start = (f32[2,64,256]{2,1,0:T(8,128)S(1)}, f32[2,64,256]{2,1,0:T(8,128)S(1)}, u32[]{:S(2)}, u32[]{:S(2)}) collective-permute-start(f32[2,64,256]{2,1,0:T(8,128)S(1)} %get-tuple-element.36), channel_id=1, source_target_pairs={{4,8},{8,4},{12,16},{16,12},{20,24},{24,20},{5,9},{9,5},{13,17},{1... | collective-permute-start | bytes 393224 | tf_op jit(solution)/shard_map/ppermute | solution.py:30
  9.1 10.3 %collective-permute-start.1 = (f32[2,64,256]{2,1,0:T(8,128)S(1)}, f32[2,64,256]{2,1,0:T(8,128)S(1)}, u32[]{:S(2)}, u32[]{:S(2)}) collective-permute-start(f32[2,64,256]{2,1,0:T(8,128)S(1)} %get-tuple-element.37), channel_id=1, source_target_pairs={{0,4},{4,0},{8,12},{12,8},{16,20},{20,16},{24,28},{28,24},{1,5},{5... | collective-permute-start | bytes 393224 | tf_op jit(solution)/shard_map/ppermute | solution.py:30
  12.8 6.6 %collective-permute-start.5 = (f32[2,64,128]{2,1,0:T(8,128)S(1)}, f32[2,64,128]{2,1,0:T(8,128)S(1)}, u32[]{:S(2)}, u32[]{:S(2)}) collective-permute-start(f32[2,64,128]{2,1,0:T(8,128)S(1)} %get-tuple-element.42), channel_id=1, source_target_pairs={{4,8},{8,4},{12,16},{16,12},{20,24},{24,20},{5,9},{9,5},{13,17},{1... | collective-permute-start | bytes 196616 | tf_op jit(solution)/shard_map/ppermute | solution.py:30
  13.5 6.0 %collective-permute-start.4 = (f32[2,64,128]{2,1,0:T(8,128)S(1)}, f32[2,64,128]{2,1,0:T(8,128)S(1)}, u32[]{:S(2)}, u32[]{:S(2)}) collective-permute-start(f32[2,64,128]{2,1,0:T(8,128)S(1)} %get-tuple-element.40.corner), channel_id=1, source_target_pairs={{0,4},{4,0},{8,12},{12,8},{16,20},{20,16},{24,28},{28,24},{1,5},{5... | collective-permute-start | bytes 196616 | tf_op jit(solution)/shard_map/ppermute | solution.py:30
  16.4 3.1 %copy-start = (s32[1,1,3,2]{2,3,1,0:T(2,128)S(1)}, s32[1,1,3,2]{2,3,1,0:T(2,128)}, u32[]{:S(2)}) copy-start(s32[1,1,3,2]{2,3,1,0:T(2,128)} %param.10) | copy-start | bytes 76
  25.2 7.5 %collective-permute-start.6 = (f32[384,128]{1,0:T(8,128)S(1)}, f32[384,128]{1,0:T(8,128)S(1)}, u32[]{:S(2)}, u32[]{:S(2)}) collective-permute-start(f32[384,128]{1,0:T(8,128)S(1)} %get-tuple-element.46), channel_id=1, source_target_pairs={{4,8},{8,4},{12,16},{16,12},{20,24},{24,20},{5,9},{9,5},{13,17},{1... | collective-permute-start | bytes 589832 | tf_op jit(solution)/shard_map/ppermute | solution.py:30
  25.9 7.7 %collective-permute-start.7 = (f32[384,128]{1,0:T(8,128)S(1)}, f32[384,128]{1,0:T(8,128)S(1)}, u32[]{:S(2)}, u32[]{:S(2)}) collective-permute-start(f32[384,128]{1,0:T(8,128)S(1)} %get-tuple-element.47), channel_id=1, source_target_pairs={{0,1},{1,0},{2,3},{3,2},{4,5},{5,4},{6,7},{7,6},{8,9},{9,8},{10,11... | collective-permute-start | bytes 589832 | tf_op jit(solution)/shard_map/ppermute | solution.py:30
  29.8 3.8 %collective-permute-start.8 = (f32[384,128]{1,0:T(8,128)S(1)}, f32[384,128]{1,0:T(8,128)S(1)}, u32[]{:S(2)}, u32[]{:S(2)}) collective-permute-start(f32[384,128]{1,0:T(8,128)S(1)} %get-tuple-element.48), channel_id=1, source_target_pairs={{1,2},{2,1},{5,6},{6,5},{9,10},{10,9},{13,14},{14,13},{17,18},{18,... | collective-permute-start | bytes 589832 | tf_op jit(solution)/shard_map/ppermute | solution.py:30
  30.5 3.3 %collective-permute-start.9 = (f32[384,128]{1,0:T(8,128)S(1)}, f32[384,128]{1,0:T(8,128)S(1)}, u32[]{:S(2)}, u32[]{:S(2)}) collective-permute-start(f32[384,128]{1,0:T(8,128)S(1)} %get-tuple-element.49), channel_id=1, source_target_pairs={{0,4},{4,0},{8,12},{12,8},{16,20},{20,16},{24,28},{28,24},{1,5},{5... | collective-permute-start | bytes 589832 | tf_op jit(solution)/shard_map/ppermute | solution.py:30
  34.0 12.1 %collective-permute-start.10 = (f32[384,128]{1,0:T(8,128)S(1)}, f32[384,128]{1,0:T(8,128)S(1)}, u32[]{:S(2)}, u32[]{:S(2)}) collective-permute-start(f32[384,128]{1,0:T(8,128)S(1)} %get-tuple-element.51), channel_id=1, source_target_pairs={{4,8},{8,4},{12,16},{16,12},{20,24},{24,20},{5,9},{9,5},{13,17},{1... | collective-permute-start | bytes 589832 | tf_op jit(solution)/shard_map/ppermute | solution.py:30
  34.7 11.4 %collective-permute-start.11 = (f32[384,128]{1,0:T(8,128)S(1)}, f32[384,128]{1,0:T(8,128)S(1)}, u32[]{:S(2)}, u32[]{:S(2)}) collective-permute-start(f32[384,128]{1,0:T(8,128)S(1)} %get-tuple-element.52), channel_id=1, source_target_pairs={{0,1},{1,0},{2,3},{3,2},{4,5},{5,4},{6,7},{7,6},{8,9},{9,8},{10,11... | collective-permute-start | bytes 589832 | tf_op jit(solution)/shard_map/ppermute | solution.py:30
  38.3 7.8 %collective-permute-start.12 = (f32[384,128]{1,0:T(8,128)S(1)}, f32[384,128]{1,0:T(8,128)S(1)}, u32[]{:S(2)}, u32[]{:S(2)}) collective-permute-start(f32[384,128]{1,0:T(8,128)S(1)} %get-tuple-element.53), channel_id=1, source_target_pairs={{1,2},{2,1},{5,6},{6,5},{9,10},{10,9},{13,14},{14,13},{17,18},{18,... | collective-permute-start | bytes 589832 | tf_op jit(solution)/shard_map/ppermute | solution.py:30
  39.0 8.2 %collective-permute-start.13 = (f32[384,128]{1,0:T(8,128)S(1)}, f32[384,128]{1,0:T(8,128)S(1)}, u32[]{:S(2)}, u32[]{:S(2)}) collective-permute-start(f32[384,128]{1,0:T(8,128)S(1)} %get-tuple-element.54), channel_id=1, source_target_pairs={{0,4},{4,0},{8,12},{12,8},{16,20},{20,16},{24,28},{28,24},{1,5},{5... | collective-permute-start | bytes 589832 | tf_op jit(solution)/shard_map/ppermute | solution.py:30
  50.9 4.4 %collective-permute-start.14 = (f32[8,128]{1,0:T(8,128)S(1)}, f32[8,128]{1,0:T(8,128)S(1)}, u32[]{:S(2)}, u32[]{:S(2)}) collective-permute-start(f32[8,128]{1,0:T(8,128)S(1)} %get-tuple-element.58.refs_0_), channel_id=1, source_target_pairs={{0,4},{4,0},{8,12},{12,8},{16,20},{20,16},{24,28},{28,24},{1,5},{5... | collective-permute-start | bytes 12296 | tf_op jit(solution)/shard_map/ppermute | solution.py:540
  55.3 4.7 %collective-permute-start.15 = (f32[8,128]{1,0:T(8,128)S(1)}, f32[8,128]{1,0:T(8,128)S(1)}, u32[]{:S(2)}, u32[]{:S(2)}) collective-permute-start(f32[8,128]{1,0:T(8,128)S(1)} %shard_map.93.refs_0_), channel_id=1, source_target_pairs={{0,8},{4,12},{8,0},{12,4},{16,24},{20,28},{24,16},{28,20},{1,9},{5... | collective-permute-start | bytes 12296 | tf_op jit(solution)/shard_map/ppermute | solution.py:540
  60.1 11.4 %collective-permute-start.16 = (f32[384,128]{1,0:T(8,128)S(1)}, f32[384,128]{1,0:T(8,128)S(1)}, u32[]{:S(2)}, u32[]{:S(2)}) collective-permute-start(f32[384,128]{1,0:T(8,128)S(1)} %get-tuple-element.62), channel_id=1, source_target_pairs={{4,8},{8,4},{12,16},{16,12},{20,24},{24,20},{5,9},{9,5},{13,17},{1... | collective-permute-start | bytes 589832 | tf_op jit(solution)/shard_map/ppermute | solution.py:30
  60.8 10.7 %collective-permute-start.17 = (f32[384,128]{1,0:T(8,128)S(1)}, f32[384,128]{1,0:T(8,128)S(1)}, u32[]{:S(2)}, u32[]{:S(2)}) collective-permute-start(f32[384,128]{1,0:T(8,128)S(1)} %get-tuple-element.63), channel_id=1, source_target_pairs={{0,4},{4,0},{8,12},{12,8},{16,20},{20,16},{24,28},{28,24},{1,5},{5... | collective-permute-start | bytes 589832 | tf_op jit(solution)/shard_map/ppermute | solution.py:30
  64.0 5.4 %collective-permute-start.20 = (f32[8,128]{1,0:T(8,128)S(1)}, f32[8,128]{1,0:T(8,128)S(1)}, u32[]{:S(2)}, u32[]{:S(2)}) collective-permute-start(f32[8,128]{1,0:T(8,128)S(1)} %shard_map.95.rest_0_), channel_id=1, source_target_pairs={{0,3},{1,2},{2,1},{3,0},{4,7},{5,6},{6,5},{7,4},{8,11},{9,10},{10,... | collective-permute-start | bytes 12296 | tf_op jit(solution)/shard_map/ppermute | solution.py:540
  65.1 4.5 %collective-permute-start.19 = (f32[8,128]{1,0:T(8,128)S(1)}, f32[8,128]{1,0:T(8,128)S(1)}, u32[]{:S(2)}, u32[]{:S(2)}) collective-permute-start(f32[8,128]{1,0:T(8,128)S(1)} %shard_map.95.rest_0_), channel_id=1, source_target_pairs={{0,2},{1,3},{2,0},{3,1},{4,6},{5,7},{6,4},{7,5},{8,10},{9,11},{10,... | collective-permute-start | bytes 12296 | tf_op jit(solution)/shard_map/ppermute | solution.py:540
  67.8 3.6 %collective-permute-start.18 = (f32[8,128]{1,0:T(8,128)S(1)}, f32[8,128]{1,0:T(8,128)S(1)}, u32[]{:S(2)}, u32[]{:S(2)}) collective-permute-start(f32[8,128]{1,0:T(8,128)S(1)} %shard_map.95.rest_0_), channel_id=1, source_target_pairs={{0,1},{1,0},{2,3},{3,2},{4,5},{5,4},{6,7},{7,6},{8,9},{9,8},{10,11... | collective-permute-start | bytes 12296 | tf_op jit(solution)/shard_map/ppermute | solution.py:540
  71.7 7.1 %collective-permute-start.21 = (f32[256,128]{1,0:T(8,128)S(1)}, f32[256,128]{1,0:T(8,128)S(1)}, u32[]{:S(2)}, u32[]{:S(2)}) collective-permute-start(f32[256,128]{1,0:T(8,128)S(1)} %get-tuple-element.65), channel_id=1, source_target_pairs={{1,2},{2,1},{5,6},{6,5},{9,10},{10,9},{13,14},{14,13},{17,18},{18,... | collective-permute-start | bytes 393224 | tf_op jit(solution)/shard_map/ppermute | solution.py:30
  72.3 6.4 %collective-permute-start.22 = (f32[256,128]{1,0:T(8,128)S(1)}, f32[256,128]{1,0:T(8,128)S(1)}, u32[]{:S(2)}, u32[]{:S(2)}) collective-permute-start(f32[256,128]{1,0:T(8,128)S(1)} %get-tuple-element.66), channel_id=1, source_target_pairs={{0,1},{1,0},{2,3},{3,2},{4,5},{5,4},{6,7},{7,6},{8,9},{9,8},{10,11... | collective-permute-start | bytes 393224 | tf_op jit(solution)/shard_map/ppermute | solution.py:30
  75.1 3.6 %collective-permute-start.23 = (f32[8,128]{1,0:T(8,128)S(1)}, f32[8,128]{1,0:T(8,128)S(1)}, u32[]{:S(2)}, u32[]{:S(2)}) collective-permute-start(f32[8,128]{1,0:T(8,128)S(1)} %get-tuple-element.69.rest_0_), channel_id=1, source_target_pairs={{0,16},{4,20},{8,24},{12,28},{16,0},{20,4},{24,8},{28,12},{1,17},{... | collective-permute-start | bytes 12296 | tf_op jit(solution)/shard_map/ppermute | solution.py:540

commit v4 on v3

--- a/solution.py
+++ b/solution.py
@@ -470,18 +470,21 @@
         "narrow",
         lambda: jnp.where(low, im, re),
         lambda: jnp.where(low, re, im),
-        store(out_first),
-        store(out_second),
-    )
-    out_sums[...] = total_of(parts)
-
-
-def finish_kernel(second, first, g, image, middle, *rest):
-    parts, (solved_out, left_out, solved, left_over, sent) = (rest[:-5], rest[-5:])
+        store(out_first.at[:n]),
+        store(out_second.at[:n]),
+    )
+    out_first[n:] = total_of(parts)
+    out_second[n:] = out_first[n:]
+    out_sums[...] = out_first[n:]
+
+
+def finish_kernel(
+    second, first, g, image, middle, sums, solved_out, left_out, solved, left_over, sent
+):
     n, width = g.shape[1:]
-    left, right = lower_upper("narrow", first[...], second[...])
+    left, right = lower_upper("narrow", first[:n], second[:n])
     low = lanes_low(right.shape)
-    total = total_of(parts)
+    total = sums[...] + first[n:]
     n0, s0, uu, s1 = (total[i : i + 1, :1] for i in range(4))
     mu = s0 / n0
     a0 = n0 / (s0 + damping * n0)
@@ -523,10 +526,18 @@
     refs[-1][...] = total_of(refs[:-1])
 
 
-def hops(axis, steps):
-    size = lax.axis_size(axis)
-    masks = list(steps) + [sum(steps)] * (len(steps) > 1)
-    return [(axis, [(i, i ^ mask) for i in range(size)]) for mask in masks]
+def hops(over_wide, over_narrow):
+    rows, cols = (lax.axis_size("wide"), lax.axis_size("narrow"))
+    pairs_of = [(down, right) for down in {0, over_wide} for right in {0, over_narrow}]
+    return [
+        [
+            (i * cols + j, (i ^ down) * cols + (j ^ right))
+            for i in range(rows)
+            for j in range(cols)
+        ]
+        for down, right in sorted(pairs_of)
+        if down or right
+    ]
 
 
 def powers(size):
@@ -537,7 +548,7 @@
 
 
 def take_hops(x, wanted):
-    return [x] + [lax.ppermute(x, axis, perm) for axis, perm in wanted]
+    return [x] + [lax.ppermute(x, ("wide", "narrow"), perm) for perm in wanted]
 
 
 def add_hops(x, rounds):
@@ -654,10 +665,9 @@
         pass_flops // 2,
     )
     along_wide, along_narrow = (powers(lax.axis_size("wide")), powers(lax.axis_size("narrow")))
-    rounds = [hops("wide", [step]) for step in along_wide[:-1]]
-    rounds += [hops("narrow", [step]) for step in along_narrow[:-2]]
-    beside_rows = hops("narrow", along_narrow[-2:]) if along_narrow else []
-    beside_cols = hops("wide", along_wide[-1:]) if along_wide else []
+    rounds = [hops(step, 0) for step in along_wide[:-1]]
+    rounds += [hops(0, step) for step in along_narrow[1:-1]]
+    beside_rows = hops(sum(along_wide[-1:]), sum(along_narrow[1:][-1:]))
     early = len(rounds)
     total = None
     for i in range(max(early, 1)):
@@ -681,7 +691,7 @@
     f2, f1 = (swap(f2, "wide", 1), swap(f1, "wide", 0))
     middle, f1, f2, sums = call(
         fold_rows_kernel,
-        [shape(2, blocks, rows, 128), shape(rows, 128), shape(rows, 128), shape(8, 128)],
+        [shape(2, blocks, rows, 128), shape(rows + 8, 128), shape(rows + 8, 128), shape(8, 128)],
         0,
         [f2, f1, total] + take_hops(sums, beside_rows),
     )
@@ -690,7 +700,7 @@
         finish_kernel,
         [shape(2, rows, width)] * 2,
         0,
-        [f2, f1, gradient, image, middle] + take_hops(sums, beside_cols),
+        [f2, f1, gradient, image, middle, sums],
         [pltpu.VMEM((2, rows, width), F32)] * 2 + [pltpu.SemaphoreType.DMA((2, 2))],
         out_far=True,
     )

time: 80.4 us -> 79.3 us (0.986)
  starting transfers between devices: 51 us -> 48.3 us
  waiting for transfers between devices: 8.45 us -> 9.65 us
    ppermute x18, waiting for transfers between devices: 2.16 us -> 5.15 us  [swap(): return lax.ppermute(x, axis, wanted)]
    ppermute x18, starting transfers between devices: 40.7 us -> 37.8 us  [swap(): return lax.ppermute(x, axis, wanted)]
    ppermute x6 -> x5, waiting for transfers between devices: 6.29 us -> 4.51 us  [take_hops(): return [x] + [lax.ppermute(x, ('wide', 'narrow'), perm) for perm in wanted]]
    ppermute x6 -> x5, starting transfers between devices: 10.3 us -> 10.5 us  [take_hops(): return [x] + [lax.ppermute(x, ('wide', 'narrow'), perm) for perm in wanted]]
  transfers between devices with their start and end apart: 24 -> 23, of which waited for: 7 -> 7; matrix products, arithmetic and copies ran while one was open for 0% -> 0% of each run, Pallas kernels for 8% -> 9%
where the time goes in v4:
time: 79.3 us; the launch traced here: 78.6 us
  starting transfers between devices  48.3 us (61%)
  Pallas kernels  19.1 us (24%)
  waiting for transfers between devices  9.65 us (12%)
  between operations  1.53 us (2%)
    ppermute x18, starting transfers between devices, swap(): return lax.ppermute(x, axis, wanted)  37.8 us
    pallas_call x13, Pallas kernels, call(): pl.pallas_call(kernel, out_shape=[place(o.shape, o.dtype) for o in outs],...  19.1 us
    ppermute x5, starting transfers between devices, take_hops(): return [x] + [lax.ppermute(x, ('wide', 'narrow'), perm) for perm in wanted]  10.5 us
    ppermute x18, waiting for transfers between devices, swap(): return lax.ppermute(x, axis, wanted)  5.15 us
    ppermute x5, waiting for transfers between devices, take_hops(): return [x] + [lax.ppermute(x, ('wide', 'narrow'), perm) for perm in wanted]  4.51 us
  transfers between devices with their start and end apart: 23, of which 7 were waited for; matrix products, arithmetic and copies ran while one was open for 0% of the time, Pallas kernels for 9%

profile of v4, /device:TPU:0, one launch (start us, length us, event | category | flops | bytes accessed | tf_op | source)
XLA Modules:
  0.0 78.6 jit_solution(17415530446120545874)
XLA Ops:
  0.6 1.2 %shard_map.86 = (f32[2,64,256]{2,1,0:T(8,128)S(1)}, f32[2,64,256]{2,1,0:T(8,128)S(1)}, f32[256,128]{1,0:T(8,128)S(1)}, f32[256,128]{1,0:T(8,128)S(1)}) custom-call(f32[2,256,256]{2,1,0:T(8,128)} %g_far.1), custom_call_target="tpu_custom_call" | custom-call | bytes 1048576 | tf_op jit(solution)/shard_map/pallas_call | solution.py:576
  1.8 0.7 collective-permute-start.2
  2.5 5.9 %collective-permute-start.3 = (f32[256,128]{1,0:T(8,128)S(1)}, f32[256,128]{1,0:T(8,128)S(1)}, u32[]{:S(2)}, u32[]{:S(2)}) collective-permute-start(f32[256,128]{1,0:T(8,128)S(1)} %get-tuple-element.39), channel_id=1, source_target_pairs={{0,1},{1,0},{2,3},{3,2},{4,5},{5,4},{6,7},{7,6},{8,9},{9,8},{10,11... | collective-permute-start | bytes 393224 | tf_op jit(solution)/shard_map/ppermute | solution.py:30
  8.4 0.7 collective-permute-start
  9.1 2.9 %collective-permute-start.1 = (f32[2,64,256]{2,1,0:T(8,128)S(1)}, f32[2,64,256]{2,1,0:T(8,128)S(1)}, u32[]{:S(2)}, u32[]{:S(2)}) collective-permute-start(f32[2,64,256]{2,1,0:T(8,128)S(1)} %get-tuple-element.37), channel_id=1, source_target_pairs={{0,4},{4,0},{8,12},{12,8},{16,20},{20,16},{24,28},{28,24},{1,5},{5... | collective-permute-start | bytes 393224 | tf_op jit(solution)/shard_map/ppermute | solution.py:30
  12.7 0.0 collective-permute-done.2.col2
  12.7 0.0 collective-permute-done.3.col1
  12.7 0.1 shard_map.87
  12.8 0.7 collective-permute-start.5
  13.5 2.9 %collective-permute-start.4 = (f32[2,64,128]{2,1,0:T(8,128)S(1)}, f32[2,64,128]{2,1,0:T(8,128)S(1)}, u32[]{:S(2)}, u32[]{:S(2)}) collective-permute-start(f32[2,64,128]{2,1,0:T(8,128)S(1)} %get-tuple-element.40.corner), channel_id=1, source_target_pairs={{0,4},{4,0},{8,12},{12,8},{16,20},{20,16},{24,28},{28,24},{1,5},{5... | collective-permute-start | bytes 196616 | tf_op jit(solution)/shard_map/ppermute | solution.py:30
  16.4 0.0 copy-start
  16.4 3.0 %shard_map.88 = (bf16[3,4,256,512]{3,2,1,0:T(8,128)(2,1)S(1)}, bf16[4,2,256,256]{3,2,1,0:T(8,128)(2,1)S(1)}, bf16[4,256,256]{2,1,0:T(8,128)(2,1)S(1)}, f32[2,256,256]{2,1,0:T(8,128)S(1)}) custom-call(s32[1]{0:T(128)} %bitcast.5.counts, f32[2,64,128]{2,1,0:T(8,128)S(1)} %get-tuple-element.40.corner, bf16[3,4,2,256,256]{4,3,2,1,0:T(8,128)(2,1)} %bitcast.14, ...), custom_call_target="tpu_custom_call" | custom-call | flops 1610612736 | bytes 10813444 | tf_op jit(solution)/shard_map/pallas_call | solution.py:576
  19.4 0.0 collective-permute-done.row2
  19.4 0.0 collective-permute-done.1.row1
  19.4 0.0 collective-permute-done.5.corner2
  19.4 0.0 collective-permute-done.4.corner1
  19.5 0.0 copy-done
  19.5 5.7 %shard_map.89 = (f32[2,3,384,128]{3,2,1,0:T(8,128)S(1)}, f32[8,128]{1,0:T(8,128)S(1)}, f32[384,128]{1,0:T(8,128)S(1)}, f32[384,128]{1,0:T(8,128)S(1)}, f32[384,128]{1,0:T(8,128)S(1)}, /*index=5*/f32[384,128]{1,0:T(8,128)S(1)}) custom-call(s32[1]{0:T(128)} %bitcast.6.counts, s32[2,3]{1,0:T(2,128)S(1)} %bitcast.10, ...), custom_call_target="tpu_custom_call" | custom-call | flops 6442450944 | bytes 7868444 | tf_op jit(solution)/shard_map/pallas_call | solution.py:576
  25.2 0.7 collective-permute-start.6
  25.9 3.9 %collective-permute-start.7 = (f32[384,128]{1,0:T(8,128)S(1)}, f32[384,128]{1,0:T(8,128)S(1)}, u32[]{:S(2)}, u32[]{:S(2)}) collective-permute-start(f32[384,128]{1,0:T(8,128)S(1)} %get-tuple-element.47), channel_id=1, source_target_pairs={{0,1},{1,0},{2,3},{3,2},{4,5},{5,4},{6,7},{7,6},{8,9},{9,8},{10,11... | collective-permute-start | bytes 589832 | tf_op jit(solution)/shard_map/ppermute | solution.py:30
  29.8 0.7 collective-permute-start.8
  30.5 2.6 %collective-permute-start.9 = (f32[384,128]{1,0:T(8,128)S(1)}, f32[384,128]{1,0:T(8,128)S(1)}, u32[]{:S(2)}, u32[]{:S(2)}) collective-permute-start(f32[384,128]{1,0:T(8,128)S(1)} %get-tuple-element.49), channel_id=1, source_target_pairs={{0,4},{4,0},{8,12},{12,8},{16,20},{20,16},{24,28},{28,24},{1,5},{5... | collective-permute-start | bytes 589832 | tf_op jit(solution)/shard_map/ppermute | solution.py:30
  33.1 0.0 collective-permute-done.6.rr2
  33.1 0.3 collective-permute-done.7.ri1
  33.5 0.0 collective-permute-done.8.ri2
  33.5 0.7 collective-permute-done.9.rr1
  34.2 0.2 shard_map.90
  34.4 0.7 collective-permute-start.10
  35.1 4.3 %collective-permute-start.11 = (f32[384,128]{1,0:T(8,128)S(1)}, f32[384,128]{1,0:T(8,128)S(1)}, u32[]{:S(2)}, u32[]{:S(2)}) collective-permute-start(f32[384,128]{1,0:T(8,128)S(1)} %get-tuple-element.52), channel_id=1, source_target_pairs={{0,1},{1,0},{2,3},{3,2},{4,5},{5,4},{6,7},{7,6},{8,9},{9,8},{10,11... | collective-permute-start | bytes 589832 | tf_op jit(solution)/shard_map/ppermute | solution.py:30
  39.4 0.7 collective-permute-start.12
  40.0 3.9 %collective-permute-start.13 = (f32[384,128]{1,0:T(8,128)S(1)}, f32[384,128]{1,0:T(8,128)S(1)}, u32[]{:S(2)}, u32[]{:S(2)}) collective-permute-start(f32[384,128]{1,0:T(8,128)S(1)} %get-tuple-element.54), channel_id=1, source_target_pairs={{0,4},{4,0},{8,12},{12,8},{16,20},{20,16},{24,28},{28,24},{1,5},{5... | collective-permute-start | bytes 589832 | tf_op jit(solution)/shard_map/ppermute | solution.py:30
  43.9 0.0 collective-permute-done.10.ri2
  43.9 0.0 collective-permute-done.11.rr1
  43.9 0.0 collective-permute-done.12.rr2
  43.9 1.1 %collective-permute-done.13.ri1 = f32[384,128]{1,0:T(8,128)S(1)} collective-permute-done((f32[384,128]{1,0:T(8,128)S(1)}, f32[384,128]{1,0:T(8,128)S(1)}, u32[]{:S(2)}, u32[]{:S(2)}) %collective-permute-start.13) | collective-permute-done | bytes 196640 | tf_op jit(solution)/shard_map/ppermute | solution.py:30
  45.0 3.7 %shard_map.91 = (f32[2,256,256]{2,1,0:T(8,128)S(1)}, f32[3,256,256]{2,1,0:T(8,128)S(1)}, f32[8,128]{1,0:T(8,128)S(1)}) custom-call(s32[1]{0:T(128)} %bitcast.7.counts, s32[2,3]{1,0:T(2,128)S(1)} %bitcast.11, f32[384,128]{1,0:T(8,128)S(1)} %collective-permute-done.10.ri2, f32[384,128]{1,0:T(8,128)S(1)} %collective-permute-done.11.rr1, ...), custom_call_target="tpu_custom_call" | custom-call | flops 3221225472 | bytes 8003612 | tf_op jit(solution)/shard_map/pallas_call | solution.py:576
  48.7 1.3 %collective-permute-start.14 = (f32[8,128]{1,0:T(8,128)S(1)}, f32[8,128]{1,0:T(8,128)S(1)}, u32[]{:S(2)}, u32[]{:S(2)}) collective-permute-start(f32[8,128]{1,0:T(8,128)S(1)} %get-tuple-element.58.refs_0_), channel_id=1, source_target_pairs={{0,4},{1,5},{2,6},{3,7},{4,0},{5,1},{6,2},{7,3},{8,12},{9,13},{10,... | collective-permute-start | bytes 12296 | tf_op jit(solution)/shard_map/ppermute | solution.py:551
  50.0 1.8 %shard_map.92.rest_0_ = f32[2,3,384,128]{3,2,1,0:T(8,128)S(1)} custom-call(s32[1]{0:T(128)} %bitcast.8.counts, s32[2,3]{1,0:T(2,128)S(1)} %bitcast.12, f32[3,256,256]{2,1,0:T(8,128)S(1)} %get-tuple-element.57.projected, bf16[4,2,256,256]{3,2,1,0:T(8,128)(2,1)S(1)} %get-tuple-element.43.probe, bf16[3,4,256,512]{3,2,1,0:T(8,128)(2,1)S(1)} %get-tuple-element.44.weights, ...), custom_call_target="tpu_custom_call" | custom-call | flops 1073741824 | bytes 6684700 | tf_op jit(solution)/shard_map/pallas_call | solution.py:576
  51.8 0.0 collective-permute-done.14.refs_1_
  51.9 2.8 %collective-permute-start.15 = (f32[8,128]{1,0:T(8,128)S(1)}, f32[8,128]{1,0:T(8,128)S(1)}, u32[]{:S(2)}, u32[]{:S(2)}) collective-permute-start(f32[8,128]{1,0:T(8,128)S(1)} %shard_map.93.refs_0_), channel_id=1, source_target_pairs={{0,8},{1,9},{2,10},{3,11},{4,12},{5,13},{6,14},{7,15},{8,0},{9,1},... | collective-permute-start | bytes 12296 | tf_op jit(solution)/shard_map/ppermute | solution.py:551
  54.6 1.7 %shard_map.94.total = f32[2,3,384,128]{3,2,1,0:T(8,128)S(1)} custom-call(s32[1]{0:T(128)} %bitcast.9.counts, s32[2,3]{1,0:T(2,128)S(1)} %bitcast.13, f32[3,256,256]{2,1,0:T(8,128)S(1)} %get-tuple-element.57.projected, bf16[4,2,256,256]{3,2,1,0:T(8,128)(2,1)S(1)} %get-tuple-element.43.probe, ...), custom_call_target="tpu_custom_call", output_to_operand_aliasing={{}: (6, {})} | custom-call | flops 2147483648 | bytes 7864348 | tf_op jit(solution)/shard_map/pallas_call | solution.py:576
  56.4 0.0 collective-permute-done.15.refs_1_
  56.5 0.7 collective-permute-start.16
  57.1 3.2 %collective-permute-start.17 = (f32[384,128]{1,0:T(8,128)S(1)}, f32[384,128]{1,0:T(8,128)S(1)}, u32[]{:S(2)}, u32[]{:S(2)}) collective-permute-start(f32[384,128]{1,0:T(8,128)S(1)} %get-tuple-element.63), channel_id=1, source_target_pairs={{0,4},{4,0},{8,12},{12,8},{16,20},{20,16},{24,28},{28,24},{1,5},{5... | collective-permute-start | bytes 589832 | tf_op jit(solution)/shard_map/ppermute | solution.py:30
  60.4 5.8 %collective-permute-start.20 = (f32[8,128]{1,0:T(8,128)S(1)}, f32[8,128]{1,0:T(8,128)S(1)}, u32[]{:S(2)}, u32[]{:S(2)}) collective-permute-start(f32[8,128]{1,0:T(8,128)S(1)} %shard_map.95.rest_0_), channel_id=1, source_target_pairs={{0,18},{1,19},{2,16},{3,17},{4,22},{5,23},{6,20},{7,21},{8,26},{9,... | collective-permute-start | bytes 12296 | tf_op jit(solution)/shard_map/ppermute | solution.py:551
  66.1 0.7 collective-permute-start.19
  66.8 0.0 collective-permute-start.18
  66.8 0.9 %collective-permute-done.20.rest_3_ = f32[8,128]{1,0:T(8,128)S(1)} collective-permute-done((f32[8,128]{1,0:T(8,128)S(1)}, f32[8,128]{1,0:T(8,128)S(1)}, u32[]{:S(2)}, u32[]{:S(2)}) %collective-permute-start.20) | collective-permute-done | bytes 4128 | tf_op jit(solution)/shard_map/ppermute | solution.py:551
  67.7 2.0 %collective-permute-done.19.rest_2_ = f32[8,128]{1,0:T(8,128)S(1)} collective-permute-done((f32[8,128]{1,0:T(8,128)S(1)}, f32[8,128]{1,0:T(8,128)S(1)}, u32[]{:S(2)}, u32[]{:S(2)}) %collective-permute-start.19) | collective-permute-done | bytes 4128 | tf_op jit(solution)/shard_map/ppermute | solution.py:551
  69.7 1.6 %collective-permute-done.18.rest_1_ = f32[8,128]{1,0:T(8,128)S(1)} collective-permute-done((f32[8,128]{1,0:T(8,128)S(1)}, f32[8,128]{1,0:T(8,128)S(1)}, u32[]{:S(2)}, u32[]{:S(2)}) %collective-permute-start.18) | collective-permute-done | bytes 4128 | tf_op jit(solution)/shard_map/ppermute | solution.py:551
  71.3 0.0 collective-permute-done.16.second
  71.3 0.0 collective-permute-done.17.first
  71.3 0.2 shard_map.97
  71.5 0.7 collective-permute-start.21
  72.1 2.1 %collective-permute-start.22 = (f32[264,128]{1,0:T(8,128)S(1)}, f32[264,128]{1,0:T(8,128)S(1)}, u32[]{:S(2)}, u32[]{:S(2)}) collective-permute-start(f32[264,128]{1,0:T(8,128)S(1)} %get-tuple-element.66), channel_id=1, source_target_pairs={{0,1},{1,0},{2,3},{3,2},{4,5},{5,4},{6,7},{7,6},{8,9},{9,8},{10,11... | collective-permute-start | bytes 405512 | tf_op jit(solution)/shard_map/ppermute | solution.py:30
  74.2 0.0 collective-permute-done.21.second
  74.2 3.0 %collective-permute-done.22.first = f32[264,128]{1,0:T(8,128)S(1)} collective-permute-done((f32[264,128]{1,0:T(8,128)S(1)}, f32[264,128]{1,0:T(8,128)S(1)}, u32[]{:S(2)}, u32[]{:S(2)}) %collective-permute-start.22) | collective-permute-done | bytes 135200 | tf_op jit(solution)/shard_map/ppermute | solution.py:30
  77.2 1.3 %shard_map.98 = (f32[2,256,256]{2,1,0:T(8,128)}, f32[2,256,256]{2,1,0:T(8,128)}) custom-call(f32[264,128]{1,0:T(8,128)S(1)} %collective-permute-done.21.second, f32[264,128]{1,0:T(8,128)S(1)} %collective-permute-done.22.first, f32[2,256,256]{2,1,0:T(8,128)S(1)} %get-tuple-element.41.g, f32[2,256,256]{2,1,0:T(8,128)S(1)} %get-tuple-element.67.image, ...), custom_call_target="tpu_custom_call" | custom-call | bytes 3158016 | tf_op jit(solution)/shard_map/pallas_call | solution.py:576
  (3 shorter events, 0.1 us)
Async XLA Ops:
  1.8 10.8 %collective-permute-start.2 = (f32[256,128]{1,0:T(8,128)S(1)}, f32[256,128]{1,0:T(8,128)S(1)}, u32[]{:S(2)}, u32[]{:S(2)}) collective-permute-start(f32[256,128]{1,0:T(8,128)S(1)} %get-tuple-element.38), channel_id=1, source_target_pairs={{1,2},{2,1},{5,6},{6,5},{9,10},{10,9},{13,14},{14,13},{17,18},{18,... | collective-permute-start | bytes 393224 | tf_op jit(solution)/shard_map/ppermute | solution.py:30
  2.5 10.1 %collective-permute-start.3 = (f32[256,128]{1,0:T(8,128)S(1)}, f32[256,128]{1,0:T(8,128)S(1)}, u32[]{:S(2)}, u32[]{:S(2)}) collective-permute-start(f32[256,128]{1,0:T(8,128)S(1)} %get-tuple-element.39), channel_id=1, source_target_pairs={{0,1},{1,0},{2,3},{3,2},{4,5},{5,4},{6,7},{7,6},{8,9},{9,8},{10,11... | collective-permute-start | bytes 393224 | tf_op jit(solution)/shard_map/ppermute | solution.py:30
  8.4 11.0 %collective-permute-start = (f32[2,64,256]{2,1,0:T(8,128)S(1)}, f32[2,64,256]{2,1,0:T(8,128)S(1)}, u32[]{:S(2)}, u32[]{:S(2)}) collective-permute-start(f32[2,64,256]{2,1,0:T(8,128)S(1)} %get-tuple-element.36), channel_id=1, source_target_pairs={{4,8},{8,4},{12,16},{16,12},{20,24},{24,20},{5,9},{9,5},{13,17},{1... | collective-permute-start | bytes 393224 | tf_op jit(solution)/shard_map/ppermute | solution.py:30
  9.1 10.3 %collective-permute-start.1 = (f32[2,64,256]{2,1,0:T(8,128)S(1)}, f32[2,64,256]{2,1,0:T(8,128)S(1)}, u32[]{:S(2)}, u32[]{:S(2)}) collective-permute-start(f32[2,64,256]{2,1,0:T(8,128)S(1)} %get-tuple-element.37), channel_id=1, source_target_pairs={{0,4},{4,0},{8,12},{12,8},{16,20},{20,16},{24,28},{28,24},{1,5},{5... | collective-permute-start | bytes 393224 | tf_op jit(solution)/shard_map/ppermute | solution.py:30
  12.8 6.6 %collective-permute-start.5 = (f32[2,64,128]{2,1,0:T(8,128)S(1)}, f32[2,64,128]{2,1,0:T(8,128)S(1)}, u32[]{:S(2)}, u32[]{:S(2)}) collective-permute-start(f32[2,64,128]{2,1,0:T(8,128)S(1)} %get-tuple-element.42), channel_id=1, source_target_pairs={{4,8},{8,4},{12,16},{16,12},{20,24},{24,20},{5,9},{9,5},{13,17},{1... | collective-permute-start | bytes 196616 | tf_op jit(solution)/shard_map/ppermute | solution.py:30
  13.5 6.0 %collective-permute-start.4 = (f32[2,64,128]{2,1,0:T(8,128)S(1)}, f32[2,64,128]{2,1,0:T(8,128)S(1)}, u32[]{:S(2)}, u32[]{:S(2)}) collective-permute-start(f32[2,64,128]{2,1,0:T(8,128)S(1)} %get-tuple-element.40.corner), channel_id=1, source_target_pairs={{0,4},{4,0},{8,12},{12,8},{16,20},{20,16},{24,28},{28,24},{1,5},{5... | collective-permute-start | bytes 196616 | tf_op jit(solution)/shard_map/ppermute | solution.py:30
  16.4 3.1 %copy-start = (s32[1,1,3,2]{2,3,1,0:T(2,128)S(1)}, s32[1,1,3,2]{2,3,1,0:T(2,128)}, u32[]{:S(2)}) copy-start(s32[1,1,3,2]{2,3,1,0:T(2,128)} %param.10) | copy-start | bytes 76
  25.2 7.9 %collective-permute-start.6 = (f32[384,128]{1,0:T(8,128)S(1)}, f32[384,128]{1,0:T(8,128)S(1)}, u32[]{:S(2)}, u32[]{:S(2)}) collective-permute-start(f32[384,128]{1,0:T(8,128)S(1)} %get-tuple-element.46), channel_id=1, source_target_pairs={{4,8},{8,4},{12,16},{16,12},{20,24},{24,20},{5,9},{9,5},{13,17},{1... | collective-permute-start | bytes 589832 | tf_op jit(solution)/shard_map/ppermute | solution.py:30
  25.9 7.6 %collective-permute-start.7 = (f32[384,128]{1,0:T(8,128)S(1)}, f32[384,128]{1,0:T(8,128)S(1)}, u32[]{:S(2)}, u32[]{:S(2)}) collective-permute-start(f32[384,128]{1,0:T(8,128)S(1)} %get-tuple-element.47), channel_id=1, source_target_pairs={{0,1},{1,0},{2,3},{3,2},{4,5},{5,4},{6,7},{7,6},{8,9},{9,8},{10,11... | collective-permute-start | bytes 589832 | tf_op jit(solution)/shard_map/ppermute | solution.py:30
  29.8 3.7 %collective-permute-start.8 = (f32[384,128]{1,0:T(8,128)S(1)}, f32[384,128]{1,0:T(8,128)S(1)}, u32[]{:S(2)}, u32[]{:S(2)}) collective-permute-start(f32[384,128]{1,0:T(8,128)S(1)} %get-tuple-element.48), channel_id=1, source_target_pairs={{1,2},{2,1},{5,6},{6,5},{9,10},{10,9},{13,14},{14,13},{17,18},{18,... | collective-permute-start | bytes 589832 | tf_op jit(solution)/shard_map/ppermute | solution.py:30
  30.5 3.7 %collective-permute-start.9 = (f32[384,128]{1,0:T(8,128)S(1)}, f32[384,128]{1,0:T(8,128)S(1)}, u32[]{:S(2)}, u32[]{:S(2)}) collective-permute-start(f32[384,128]{1,0:T(8,128)S(1)} %get-tuple-element.49), channel_id=1, source_target_pairs={{0,4},{4,0},{8,12},{12,8},{16,20},{20,16},{24,28},{28,24},{1,5},{5... | collective-permute-start | bytes 589832 | tf_op jit(solution)/shard_map/ppermute | solution.py:30
  34.4 9.5 %collective-permute-start.10 = (f32[384,128]{1,0:T(8,128)S(1)}, f32[384,128]{1,0:T(8,128)S(1)}, u32[]{:S(2)}, u32[]{:S(2)}) collective-permute-start(f32[384,128]{1,0:T(8,128)S(1)} %get-tuple-element.51), channel_id=1, source_target_pairs={{4,8},{8,4},{12,16},{16,12},{20,24},{24,20},{5,9},{9,5},{13,17},{1... | collective-permute-start | bytes 589832 | tf_op jit(solution)/shard_map/ppermute | solution.py:30
  35.1 8.8 %collective-permute-start.11 = (f32[384,128]{1,0:T(8,128)S(1)}, f32[384,128]{1,0:T(8,128)S(1)}, u32[]{:S(2)}, u32[]{:S(2)}) collective-permute-start(f32[384,128]{1,0:T(8,128)S(1)} %get-tuple-element.52), channel_id=1, source_target_pairs={{0,1},{1,0},{2,3},{3,2},{4,5},{5,4},{6,7},{7,6},{8,9},{9,8},{10,11... | collective-permute-start | bytes 589832 | tf_op jit(solution)/shard_map/ppermute | solution.py:30
  39.4 4.6 %collective-permute-start.12 = (f32[384,128]{1,0:T(8,128)S(1)}, f32[384,128]{1,0:T(8,128)S(1)}, u32[]{:S(2)}, u32[]{:S(2)}) collective-permute-start(f32[384,128]{1,0:T(8,128)S(1)} %get-tuple-element.53), channel_id=1, source_target_pairs={{1,2},{2,1},{5,6},{6,5},{9,10},{10,9},{13,14},{14,13},{17,18},{18,... | collective-permute-start | bytes 589832 | tf_op jit(solution)/shard_map/ppermute | solution.py:30
  40.0 5.0 %collective-permute-start.13 = (f32[384,128]{1,0:T(8,128)S(1)}, f32[384,128]{1,0:T(8,128)S(1)}, u32[]{:S(2)}, u32[]{:S(2)}) collective-permute-start(f32[384,128]{1,0:T(8,128)S(1)} %get-tuple-element.54), channel_id=1, source_target_pairs={{0,4},{4,0},{8,12},{12,8},{16,20},{20,16},{24,28},{28,24},{1,5},{5... | collective-permute-start | bytes 589832 | tf_op jit(solution)/shard_map/ppermute | solution.py:30
  48.7 3.2 %collective-permute-start.14 = (f32[8,128]{1,0:T(8,128)S(1)}, f32[8,128]{1,0:T(8,128)S(1)}, u32[]{:S(2)}, u32[]{:S(2)}) collective-permute-start(f32[8,128]{1,0:T(8,128)S(1)} %get-tuple-element.58.refs_0_), channel_id=1, source_target_pairs={{0,4},{1,5},{2,6},{3,7},{4,0},{5,1},{6,2},{7,3},{8,12},{9,13},{10,... | collective-permute-start | bytes 12296 | tf_op jit(solution)/shard_map/ppermute | solution.py:551
  51.9 4.5 %collective-permute-start.15 = (f32[8,128]{1,0:T(8,128)S(1)}, f32[8,128]{1,0:T(8,128)S(1)}, u32[]{:S(2)}, u32[]{:S(2)}) collective-permute-start(f32[8,128]{1,0:T(8,128)S(1)} %shard_map.93.refs_0_), channel_id=1, source_target_pairs={{0,8},{1,9},{2,10},{3,11},{4,12},{5,13},{6,14},{7,15},{8,0},{9,1},... | collective-permute-start | bytes 12296 | tf_op jit(solution)/shard_map/ppermute | solution.py:551
  56.5 14.8 %collective-permute-start.16 = (f32[384,128]{1,0:T(8,128)S(1)}, f32[384,128]{1,0:T(8,128)S(1)}, u32[]{:S(2)}, u32[]{:S(2)}) collective-permute-start(f32[384,128]{1,0:T(8,128)S(1)} %get-tuple-element.62), channel_id=1, source_target_pairs={{4,8},{8,4},{12,16},{16,12},{20,24},{24,20},{5,9},{9,5},{13,17},{1... | collective-permute-start | bytes 589832 | tf_op jit(solution)/shard_map/ppermute | solution.py:30
  57.1 14.1 %collective-permute-start.17 = (f32[384,128]{1,0:T(8,128)S(1)}, f32[384,128]{1,0:T(8,128)S(1)}, u32[]{:S(2)}, u32[]{:S(2)}) collective-permute-start(f32[384,128]{1,0:T(8,128)S(1)} %get-tuple-element.63), channel_id=1, source_target_pairs={{0,4},{4,0},{8,12},{12,8},{16,20},{20,16},{24,28},{28,24},{1,5},{5... | collective-permute-start | bytes 589832 | tf_op jit(solution)/shard_map/ppermute | solution.py:30
  60.4 7.3 %collective-permute-start.20 = (f32[8,128]{1,0:T(8,128)S(1)}, f32[8,128]{1,0:T(8,128)S(1)}, u32[]{:S(2)}, u32[]{:S(2)}) collective-permute-start(f32[8,128]{1,0:T(8,128)S(1)} %shard_map.95.rest_0_), channel_id=1, source_target_pairs={{0,18},{1,19},{2,16},{3,17},{4,22},{5,23},{6,20},{7,21},{8,26},{9,... | collective-permute-start | bytes 12296 | tf_op jit(solution)/shard_map/ppermute | solution.py:551
  66.1 3.6 %collective-permute-start.19 = (f32[8,128]{1,0:T(8,128)S(1)}, f32[8,128]{1,0:T(8,128)S(1)}, u32[]{:S(2)}, u32[]{:S(2)}) collective-permute-start(f32[8,128]{1,0:T(8,128)S(1)} %shard_map.95.rest_0_), channel_id=1, source_target_pairs={{0,16},{1,17},{2,18},{3,19},{4,20},{5,21},{6,22},{7,23},{8,24},{9,... | collective-permute-start | bytes 12296 | tf_op jit(solution)/shard_map/ppermute | solution.py:551
  66.8 4.5 %collective-permute-start.18 = (f32[8,128]{1,0:T(8,128)S(1)}, f32[8,128]{1,0:T(8,128)S(1)}, u32[]{:S(2)}, u32[]{:S(2)}) collective-permute-start(f32[8,128]{1,0:T(8,128)S(1)} %shard_map.95.rest_0_), channel_id=1, source_target_pairs={{0,2},{1,3},{2,0},{3,1},{4,6},{5,7},{6,4},{7,5},{8,10},{9,11},{10,... | collective-permute-start | bytes 12296 | tf_op jit(solution)/shard_map/ppermute | solution.py:551
  71.5 2.8 %collective-permute-start.21 = (f32[264,128]{1,0:T(8,128)S(1)}, f32[264,128]{1,0:T(8,128)S(1)}, u32[]{:S(2)}, u32[]{:S(2)}) collective-permute-start(f32[264,128]{1,0:T(8,128)S(1)} %get-tuple-element.65), channel_id=1, source_target_pairs={{1,2},{2,1},{5,6},{6,5},{9,10},{10,9},{13,14},{14,13},{17,18},{18,... | collective-permute-start | bytes 405512 | tf_op jit(solution)/shard_map/ppermute | solution.py:30
  72.1 5.1 %collective-permute-start.22 = (f32[264,128]{1,0:T(8,128)S(1)}, f32[264,128]{1,0:T(8,128)S(1)}, u32[]{:S(2)}, u32[]{:S(2)}) collective-permute-start(f32[264,128]{1,0:T(8,128)S(1)} %get-tuple-element.66), channel_id=1, source_target_pairs={{0,1},{1,0},{2,3},{3,2},{4,5},{5,4},{6,7},{7,6},{8,9},{9,8},{10,11... | collective-permute-start | bytes 405512 | tf_op jit(solution)/shard_map/ppermute | solution.py:30

commit v5 on v4

--- a/solution.py
+++ b/solution.py
@@ -291,9 +291,13 @@
     def visit(k, carried):
         fetch(k).wait()
         for m in range(modes):
-            re = dot(dot(sorter[0], held[k, m, 0]).astype(BF16), sorter[1])
-            im = dot(dot(sorter[0], held[k, m, 1]).astype(BF16), sorter[1])
-            out[k, m] = cat([re[:, :h], im[:, :h], re[:, h:], im[:, h:]], 1).astype(BF16)
+            for q in range(2):
+                held[k, m, q] = dot(sorter[0], held[k, m, q]).astype(BF16)
+        for m in range(modes):
+            for q in range(2):
+                x = dot(held[k, m, q], sorter[1]).astype(BF16)
+                out[k, m, :, q * h : (q + 1) * h] = x[:, :h]
+                out[k, m, :, width + q * h : width + (q + 1) * h] = x[:, h:]
         return carried
 
     lax.fori_loop(begin, jnp.minimum(end, frames[0][0]), visit, 0)

time: 79.3 us -> 79.9 us (level); the launches traced: 78.6 us -> 80.2 us
  starting transfers between devices: 48.3 us -> 41.7 us
  Pallas kernels: 19.1 us -> 24.5 us
  waiting for transfers between devices: 9.65 us -> 12.5 us
    pallas_call x13, Pallas kernels: 19.1 us -> 24.5 us  [call(): pl.pallas_call(kernel, out_shape=[place(o.shape, o.dtype) for o in outs],...]
    ppermute x18, waiting for transfers between devices: 5.15 us -> 9.92 us  [swap(): return lax.ppermute(x, axis, wanted)]
    ppermute x18, starting transfers between devices: 37.8 us -> 33 us  [swap(): return lax.ppermute(x, axis, wanted)]
    ppermute x5, waiting for transfers between devices: 4.51 us -> 2.57 us  [take_hops(): return [x] + [lax.ppermute(x, ('wide', 'narrow'), perm) for perm in wanted]]
    ppermute x5, starting transfers between devices: 10.5 us -> 8.69 us  [take_hops(): return [x] + [lax.ppermute(x, ('wide', 'narrow'), perm) for perm in wanted]]
  transfers between devices with their start and end apart: 23 -> 23, of which waited for: 7 -> 5; matrix products, arithmetic and copies ran while one was open for 0% -> 0% of each run, Pallas kernels for 9% -> 10%
where the time goes in v5:
time: 79.9 us; the launch traced here: 80.2 us
  starting transfers between devices  41.7 us (52%)
  Pallas kernels  24.5 us (31%)
  waiting for transfers between devices  12.5 us (16%)
  between operations  1.54 us (2%)
    ppermute x18, starting transfers between devices, swap(): return lax.ppermute(x, axis, wanted)  33 us
    pallas_call x13, Pallas kernels, call(): pl.pallas_call(kernel, out_shape=[place(o.shape, o.dtype) for o in outs],...  24.5 us
    ppermute x18, waiting for transfers between devices, swap(): return lax.ppermute(x, axis, wanted)  9.92 us
    ppermute x5, starting transfers between devices, take_hops(): return [x] + [lax.ppermute(x, ('wide', 'narrow'), perm) for perm in wanted]  8.69 us
    ppermute x5, waiting for transfers between devices, take_hops(): return [x] + [lax.ppermute(x, ('wide', 'narrow'), perm) for perm in wanted]  2.57 us
  transfers between devices with their start and end apart: 23, of which 5 were waited for; matrix products, arithmetic and copies ran while one was open for 0% of the time, Pallas kernels for 10%

profile of v5, /device:TPU:0, one launch (start us, length us, event | category | flops | bytes accessed | tf_op | source)
XLA Modules:
  0.0 80.2 jit_solution(826112662979547890)
XLA Ops:
  0.6 1.2 %shard_map.86 = (f32[2,64,256]{2,1,0:T(8,128)S(1)}, f32[2,64,256]{2,1,0:T(8,128)S(1)}, f32[256,128]{1,0:T(8,128)S(1)}, f32[256,128]{1,0:T(8,128)S(1)}) custom-call(f32[2,256,256]{2,1,0:T(8,128)} %g_far.1), custom_call_target="tpu_custom_call" | custom-call | bytes 1048576 | tf_op jit(solution)/shard_map/pallas_call | solution.py:580
  1.8 0.7 collective-permute-start.2
  2.5 5.9 %collective-permute-start.3 = (f32[256,128]{1,0:T(8,128)S(1)}, f32[256,128]{1,0:T(8,128)S(1)}, u32[]{:S(2)}, u32[]{:S(2)}) collective-permute-start(f32[256,128]{1,0:T(8,128)S(1)} %get-tuple-element.39), channel_id=1, source_target_pairs={{0,1},{1,0},{2,3},{3,2},{4,5},{5,4},{6,7},{7,6},{8,9},{9,8},{10,11... | collective-permute-start | bytes 393224 | tf_op jit(solution)/shard_map/ppermute | solution.py:30
  8.4 0.7 collective-permute-start
  9.1 2.9 %collective-permute-start.1 = (f32[2,64,256]{2,1,0:T(8,128)S(1)}, f32[2,64,256]{2,1,0:T(8,128)S(1)}, u32[]{:S(2)}, u32[]{:S(2)}) collective-permute-start(f32[2,64,256]{2,1,0:T(8,128)S(1)} %get-tuple-element.37), channel_id=1, source_target_pairs={{0,4},{4,0},{8,12},{12,8},{16,20},{20,16},{24,28},{28,24},{1,5},{5... | collective-permute-start | bytes 393224 | tf_op jit(solution)/shard_map/ppermute | solution.py:30
  12.7 0.0 collective-permute-done.2.col2
  12.7 0.0 collective-permute-done.3.col1
  12.7 0.1 shard_map.87
  12.8 0.7 collective-permute-start.5
  13.5 2.9 %collective-permute-start.4 = (f32[2,64,128]{2,1,0:T(8,128)S(1)}, f32[2,64,128]{2,1,0:T(8,128)S(1)}, u32[]{:S(2)}, u32[]{:S(2)}) collective-permute-start(f32[2,64,128]{2,1,0:T(8,128)S(1)} %get-tuple-element.40.corner), channel_id=1, source_target_pairs={{0,4},{4,0},{8,12},{12,8},{16,20},{20,16},{24,28},{28,24},{1,5},{5... | collective-permute-start | bytes 196616 | tf_op jit(solution)/shard_map/ppermute | solution.py:30
  16.4 0.0 copy-start
  16.4 3.5 %shard_map.88 = (bf16[3,4,256,512]{3,2,1,0:T(8,128)(2,1)S(1)}, bf16[4,2,256,256]{3,2,1,0:T(8,128)(2,1)S(1)}, bf16[4,256,256]{2,1,0:T(8,128)(2,1)S(1)}, f32[2,256,256]{2,1,0:T(8,128)S(1)}) custom-call(s32[1]{0:T(128)} %bitcast.5.counts, f32[2,64,128]{2,1,0:T(8,128)S(1)} %get-tuple-element.40.corner, bf16[3,4,2,256,256]{4,3,2,1,0:T(8,128)(2,1)} %bitcast.14, ...), custom_call_target="tpu_custom_call" | custom-call | flops 1610612736 | bytes 10813444 | tf_op jit(solution)/shard_map/pallas_call | solution.py:580
  19.9 0.0 collective-permute-done.row2
  19.9 0.0 collective-permute-done.1.row1
  20.0 0.0 collective-permute-done.5.corner2
  20.0 0.0 collective-permute-done.4.corner1
  20.0 0.0 copy-done
  20.0 8.1 %shard_map.89 = (f32[2,3,384,128]{3,2,1,0:T(8,128)S(1)}, f32[8,128]{1,0:T(8,128)S(1)}, f32[384,128]{1,0:T(8,128)S(1)}, f32[384,128]{1,0:T(8,128)S(1)}, f32[384,128]{1,0:T(8,128)S(1)}, /*index=5*/f32[384,128]{1,0:T(8,128)S(1)}) custom-call(s32[1]{0:T(128)} %bitcast.6.counts, s32[2,3]{1,0:T(2,128)S(1)} %bitcast.10, ...), custom_call_target="tpu_custom_call" | custom-call | flops 6442450944 | bytes 7868444 | tf_op jit(solution)/shard_map/pallas_call | solution.py:580
  28.1 0.7 collective-permute-start.6
  28.7 0.1 collective-permute-start.7
  28.8 0.7 collective-permute-start.8
  29.5 1.4 %collective-permute-start.9 = (f32[384,128]{1,0:T(8,128)S(1)}, f32[384,128]{1,0:T(8,128)S(1)}, u32[]{:S(2)}, u32[]{:S(2)}) collective-permute-start(f32[384,128]{1,0:T(8,128)S(1)} %get-tuple-element.49), channel_id=1, source_target_pairs={{0,4},{4,0},{8,12},{12,8},{16,20},{20,16},{24,28},{28,24},{1,5},{5... | collective-permute-start | bytes 589832 | tf_op jit(solution)/shard_map/ppermute | solution.py:30
  30.9 0.0 collective-permute-done.6.rr2
  30.9 5.4 %collective-permute-done.7.ri1 = f32[384,128]{1,0:T(8,128)S(1)} collective-permute-done((f32[384,128]{1,0:T(8,128)S(1)}, f32[384,128]{1,0:T(8,128)S(1)}, u32[]{:S(2)}, u32[]{:S(2)}) %collective-permute-start.7) | collective-permute-done | bytes 196640 | tf_op jit(solution)/shard_map/ppermute | solution.py:30
  36.3 0.0 collective-permute-done.8.ri2
  36.3 0.0 collective-permute-done.9.rr1
  36.3 0.2 shard_map.90
  36.5 0.7 collective-permute-start.10
  37.2 4.2 %collective-permute-start.11 = (f32[384,128]{1,0:T(8,128)S(1)}, f32[384,128]{1,0:T(8,128)S(1)}, u32[]{:S(2)}, u32[]{:S(2)}) collective-permute-start(f32[384,128]{1,0:T(8,128)S(1)} %get-tuple-element.52), channel_id=1, source_target_pairs={{0,1},{1,0},{2,3},{3,2},{4,5},{5,4},{6,7},{7,6},{8,9},{9,8},{10,11... | collective-permute-start | bytes 589832 | tf_op jit(solution)/shard_map/ppermute | solution.py:30
  41.4 0.7 collective-permute-start.12
  42.1 3.7 %collective-permute-start.13 = (f32[384,128]{1,0:T(8,128)S(1)}, f32[384,128]{1,0:T(8,128)S(1)}, u32[]{:S(2)}, u32[]{:S(2)}) collective-permute-start(f32[384,128]{1,0:T(8,128)S(1)} %get-tuple-element.54), channel_id=1, source_target_pairs={{0,4},{4,0},{8,12},{12,8},{16,20},{20,16},{24,28},{28,24},{1,5},{5... | collective-permute-start | bytes 589832 | tf_op jit(solution)/shard_map/ppermute | solution.py:30
  45.8 0.0 collective-permute-done.10.ri2
  45.8 0.0 collective-permute-done.11.rr1
  45.8 0.0 collective-permute-done.12.rr2
  45.8 1.1 %collective-permute-done.13.ri1 = f32[384,128]{1,0:T(8,128)S(1)} collective-permute-done((f32[384,128]{1,0:T(8,128)S(1)}, f32[384,128]{1,0:T(8,128)S(1)}, u32[]{:S(2)}, u32[]{:S(2)}) %collective-permute-start.13) | collective-permute-done | bytes 196640 | tf_op jit(solution)/shard_map/ppermute | solution.py:30
  46.9 5.0 %shard_map.91 = (f32[2,256,256]{2,1,0:T(8,128)S(1)}, f32[3,256,256]{2,1,0:T(8,128)S(1)}, f32[8,128]{1,0:T(8,128)S(1)}) custom-call(s32[1]{0:T(128)} %bitcast.7.counts, s32[2,3]{1,0:T(2,128)S(1)} %bitcast.11, f32[384,128]{1,0:T(8,128)S(1)} %collective-permute-done.10.ri2, f32[384,128]{1,0:T(8,128)S(1)} %collective-permute-done.11.rr1, ...), custom_call_target="tpu_custom_call" | custom-call | flops 3221225472 | bytes 8003612 | tf_op jit(solution)/shard_map/pallas_call | solution.py:580
  51.9 1.3 %collective-permute-start.14 = (f32[8,128]{1,0:T(8,128)S(1)}, f32[8,128]{1,0:T(8,128)S(1)}, u32[]{:S(2)}, u32[]{:S(2)}) collective-permute-start(f32[8,128]{1,0:T(8,128)S(1)} %get-tuple-element.58.refs_0_), channel_id=1, source_target_pairs={{0,4},{1,5},{2,6},{3,7},{4,0},{5,1},{6,2},{7,3},{8,12},{9,13},{10,... | collective-permute-start | bytes 12296 | tf_op jit(solution)/shard_map/ppermute | solution.py:555
  53.2 1.8 %shard_map.92.rest_0_ = f32[2,3,384,128]{3,2,1,0:T(8,128)S(1)} custom-call(s32[1]{0:T(128)} %bitcast.8.counts, s32[2,3]{1,0:T(2,128)S(1)} %bitcast.12, f32[3,256,256]{2,1,0:T(8,128)S(1)} %get-tuple-element.57.projected, bf16[4,2,256,256]{3,2,1,0:T(8,128)(2,1)S(1)} %get-tuple-element.43.probe, bf16[3,4,256,512]{3,2,1,0:T(8,128)(2,1)S(1)} %get-tuple-element.44.weights, ...), custom_call_target="tpu_custom_call" | custom-call | flops 1073741824 | bytes 6684700 | tf_op jit(solution)/shard_map/pallas_call | solution.py:580
  55.0 0.0 collective-permute-done.14.refs_1_
  55.0 3.0 %collective-permute-start.15 = (f32[8,128]{1,0:T(8,128)S(1)}, f32[8,128]{1,0:T(8,128)S(1)}, u32[]{:S(2)}, u32[]{:S(2)}) collective-permute-start(f32[8,128]{1,0:T(8,128)S(1)} %shard_map.93.refs_0_), channel_id=1, source_target_pairs={{0,8},{1,9},{2,10},{3,11},{4,12},{5,13},{6,14},{7,15},{8,0},{9,1},... | collective-permute-start | bytes 12296 | tf_op jit(solution)/shard_map/ppermute | solution.py:555
  58.0 2.9 %shard_map.94.total = f32[2,3,384,128]{3,2,1,0:T(8,128)S(1)} custom-call(s32[1]{0:T(128)} %bitcast.9.counts, s32[2,3]{1,0:T(2,128)S(1)} %bitcast.13, f32[3,256,256]{2,1,0:T(8,128)S(1)} %get-tuple-element.57.projected, bf16[4,2,256,256]{3,2,1,0:T(8,128)(2,1)S(1)} %get-tuple-element.43.probe, ...), custom_call_target="tpu_custom_call", output_to_operand_aliasing={{}: (6, {})} | custom-call | flops 2147483648 | bytes 7864348 | tf_op jit(solution)/shard_map/pallas_call | solution.py:580
  61.0 0.0 collective-permute-done.15.refs_1_
  61.1 0.7 collective-permute-start.16
  61.7 2.0 %collective-permute-start.17 = (f32[384,128]{1,0:T(8,128)S(1)}, f32[384,128]{1,0:T(8,128)S(1)}, u32[]{:S(2)}, u32[]{:S(2)}) collective-permute-start(f32[384,128]{1,0:T(8,128)S(1)} %get-tuple-element.63), channel_id=1, source_target_pairs={{0,4},{4,0},{8,12},{12,8},{16,20},{20,16},{24,28},{28,24},{1,5},{5... | collective-permute-start | bytes 589832 | tf_op jit(solution)/shard_map/ppermute | solution.py:30
  63.8 1.0 %collective-permute-start.20 = (f32[8,128]{1,0:T(8,128)S(1)}, f32[8,128]{1,0:T(8,128)S(1)}, u32[]{:S(2)}, u32[]{:S(2)}) collective-permute-start(f32[8,128]{1,0:T(8,128)S(1)} %shard_map.95.rest_0_), channel_id=1, source_target_pairs={{0,18},{1,19},{2,16},{3,17},{4,22},{5,23},{6,20},{7,21},{8,26},{9,... | collective-permute-start | bytes 12296 | tf_op jit(solution)/shard_map/ppermute | solution.py:555
  64.8 1.5 %collective-permute-start.19 = (f32[8,128]{1,0:T(8,128)S(1)}, f32[8,128]{1,0:T(8,128)S(1)}, u32[]{:S(2)}, u32[]{:S(2)}) collective-permute-start(f32[8,128]{1,0:T(8,128)S(1)} %shard_map.95.rest_0_), channel_id=1, source_target_pairs={{0,16},{1,17},{2,18},{3,19},{4,20},{5,21},{6,22},{7,23},{8,24},{9,... | collective-permute-start | bytes 12296 | tf_op jit(solution)/shard_map/ppermute | solution.py:555
  66.2 1.9 %collective-permute-start.18 = (f32[8,128]{1,0:T(8,128)S(1)}, f32[8,128]{1,0:T(8,128)S(1)}, u32[]{:S(2)}, u32[]{:S(2)}) collective-permute-start(f32[8,128]{1,0:T(8,128)S(1)} %shard_map.95.rest_0_), channel_id=1, source_target_pairs={{0,2},{1,3},{2,0},{3,1},{4,6},{5,7},{6,4},{7,5},{8,10},{9,11},{10,... | collective-permute-start | bytes 12296 | tf_op jit(solution)/shard_map/ppermute | solution.py:555
  68.2 1.0 %collective-permute-done.20.rest_3_ = f32[8,128]{1,0:T(8,128)S(1)} collective-permute-done((f32[8,128]{1,0:T(8,128)S(1)}, f32[8,128]{1,0:T(8,128)S(1)}, u32[]{:S(2)}, u32[]{:S(2)}) %collective-permute-start.20) | collective-permute-done | bytes 4128 | tf_op jit(solution)/shard_map/ppermute | solution.py:555
  69.2 0.0 collective-permute-done.19.rest_2_
  69.2 1.5 %collective-permute-done.18.rest_1_ = f32[8,128]{1,0:T(8,128)S(1)} collective-permute-done((f32[8,128]{1,0:T(8,128)S(1)}, f32[8,128]{1,0:T(8,128)S(1)}, u32[]{:S(2)}, u32[]{:S(2)}) %collective-permute-start.18) | collective-permute-done | bytes 4128 | tf_op jit(solution)/shard_map/ppermute | solution.py:555
  70.7 0.0 collective-permute-done.16.second
  70.7 0.0 collective-permute-done.17.first
  70.7 0.2 shard_map.97
  70.9 0.7 collective-permute-start.21
  71.6 3.9 %collective-permute-start.22 = (f32[264,128]{1,0:T(8,128)S(1)}, f32[264,128]{1,0:T(8,128)S(1)}, u32[]{:S(2)}, u32[]{:S(2)}) collective-permute-start(f32[264,128]{1,0:T(8,128)S(1)} %get-tuple-element.66), channel_id=1, source_target_pairs={{0,1},{1,0},{2,3},{3,2},{4,5},{5,4},{6,7},{7,6},{8,9},{9,8},{10,11... | collective-permute-start | bytes 405512 | tf_op jit(solution)/shard_map/ppermute | solution.py:30
  75.5 0.0 collective-permute-done.21.second
  75.5 3.4 %collective-permute-done.22.first = f32[264,128]{1,0:T(8,128)S(1)} collective-permute-done((f32[264,128]{1,0:T(8,128)S(1)}, f32[264,128]{1,0:T(8,128)S(1)}, u32[]{:S(2)}, u32[]{:S(2)}) %collective-permute-start.22) | collective-permute-done | bytes 135200 | tf_op jit(solution)/shard_map/ppermute | solution.py:30
  78.9 1.3 %shard_map.98 = (f32[2,256,256]{2,1,0:T(8,128)}, f32[2,256,256]{2,1,0:T(8,128)}) custom-call(f32[264,128]{1,0:T(8,128)S(1)} %collective-permute-done.21.second, f32[264,128]{1,0:T(8,128)S(1)} %collective-permute-done.22.first, f32[2,256,256]{2,1,0:T(8,128)S(1)} %get-tuple-element.41.g, f32[2,256,256]{2,1,0:T(8,128)S(1)} %get-tuple-element.67.image, ...), custom_call_target="tpu_custom_call" | custom-call | bytes 3158016 | tf_op jit(solution)/shard_map/pallas_call | solution.py:580
  (3 shorter events, 0.1 us)
Async XLA Ops:
  1.8 10.8 %collective-permute-start.2 = (f32[256,128]{1,0:T(8,128)S(1)}, f32[256,128]{1,0:T(8,128)S(1)}, u32[]{:S(2)}, u32[]{:S(2)}) collective-permute-start(f32[256,128]{1,0:T(8,128)S(1)} %get-tuple-element.38), channel_id=1, source_target_pairs={{1,2},{2,1},{5,6},{6,5},{9,10},{10,9},{13,14},{14,13},{17,18},{18,... | collective-permute-start | bytes 393224 | tf_op jit(solution)/shard_map/ppermute | solution.py:30
  2.5 10.1 %collective-permute-start.3 = (f32[256,128]{1,0:T(8,128)S(1)}, f32[256,128]{1,0:T(8,128)S(1)}, u32[]{:S(2)}, u32[]{:S(2)}) collective-permute-start(f32[256,128]{1,0:T(8,128)S(1)} %get-tuple-element.39), channel_id=1, source_target_pairs={{0,1},{1,0},{2,3},{3,2},{4,5},{5,4},{6,7},{7,6},{8,9},{9,8},{10,11... | collective-permute-start | bytes 393224 | tf_op jit(solution)/shard_map/ppermute | solution.py:30
  8.4 11.5 %collective-permute-start = (f32[2,64,256]{2,1,0:T(8,128)S(1)}, f32[2,64,256]{2,1,0:T(8,128)S(1)}, u32[]{:S(2)}, u32[]{:S(2)}) collective-permute-start(f32[2,64,256]{2,1,0:T(8,128)S(1)} %get-tuple-element.36), channel_id=1, source_target_pairs={{4,8},{8,4},{12,16},{16,12},{20,24},{24,20},{5,9},{9,5},{13,17},{1... | collective-permute-start | bytes 393224 | tf_op jit(solution)/shard_map/ppermute | solution.py:30
  9.1 10.9 %collective-permute-start.1 = (f32[2,64,256]{2,1,0:T(8,128)S(1)}, f32[2,64,256]{2,1,0:T(8,128)S(1)}, u32[]{:S(2)}, u32[]{:S(2)}) collective-permute-start(f32[2,64,256]{2,1,0:T(8,128)S(1)} %get-tuple-element.37), channel_id=1, source_target_pairs={{0,4},{4,0},{8,12},{12,8},{16,20},{20,16},{24,28},{28,24},{1,5},{5... | collective-permute-start | bytes 393224 | tf_op jit(solution)/shard_map/ppermute | solution.py:30
  12.8 7.2 %collective-permute-start.5 = (f32[2,64,128]{2,1,0:T(8,128)S(1)}, f32[2,64,128]{2,1,0:T(8,128)S(1)}, u32[]{:S(2)}, u32[]{:S(2)}) collective-permute-start(f32[2,64,128]{2,1,0:T(8,128)S(1)} %get-tuple-element.42), channel_id=1, source_target_pairs={{4,8},{8,4},{12,16},{16,12},{20,24},{24,20},{5,9},{9,5},{13,17},{1... | collective-permute-start | bytes 196616 | tf_op jit(solution)/shard_map/ppermute | solution.py:30
  13.5 6.5 %collective-permute-start.4 = (f32[2,64,128]{2,1,0:T(8,128)S(1)}, f32[2,64,128]{2,1,0:T(8,128)S(1)}, u32[]{:S(2)}, u32[]{:S(2)}) collective-permute-start(f32[2,64,128]{2,1,0:T(8,128)S(1)} %get-tuple-element.40.corner), channel_id=1, source_target_pairs={{0,4},{4,0},{8,12},{12,8},{16,20},{20,16},{24,28},{28,24},{1,5},{5... | collective-permute-start | bytes 196616 | tf_op jit(solution)/shard_map/ppermute | solution.py:30
  16.4 3.6 %copy-start = (s32[1,1,3,2]{2,3,1,0:T(2,128)S(1)}, s32[1,1,3,2]{2,3,1,0:T(2,128)}, u32[]{:S(2)}) copy-start(s32[1,1,3,2]{2,3,1,0:T(2,128)} %param.10) | copy-start | bytes 76
  28.1 2.8 %collective-permute-start.6 = (f32[384,128]{1,0:T(8,128)S(1)}, f32[384,128]{1,0:T(8,128)S(1)}, u32[]{:S(2)}, u32[]{:S(2)}) collective-permute-start(f32[384,128]{1,0:T(8,128)S(1)} %get-tuple-element.46), channel_id=1, source_target_pairs={{4,8},{8,4},{12,16},{16,12},{20,24},{24,20},{5,9},{9,5},{13,17},{1... | collective-permute-start | bytes 589832 | tf_op jit(solution)/shard_map/ppermute | solution.py:30
  28.7 7.5 %collective-permute-start.7 = (f32[384,128]{1,0:T(8,128)S(1)}, f32[384,128]{1,0:T(8,128)S(1)}, u32[]{:S(2)}, u32[]{:S(2)}) collective-permute-start(f32[384,128]{1,0:T(8,128)S(1)} %get-tuple-element.47), channel_id=1, source_target_pairs={{0,1},{1,0},{2,3},{3,2},{4,5},{5,4},{6,7},{7,6},{8,9},{9,8},{10,11... | collective-permute-start | bytes 589832 | tf_op jit(solution)/shard_map/ppermute | solution.py:30
  28.8 7.4 %collective-permute-start.8 = (f32[384,128]{1,0:T(8,128)S(1)}, f32[384,128]{1,0:T(8,128)S(1)}, u32[]{:S(2)}, u32[]{:S(2)}) collective-permute-start(f32[384,128]{1,0:T(8,128)S(1)} %get-tuple-element.48), channel_id=1, source_target_pairs={{1,2},{2,1},{5,6},{6,5},{9,10},{10,9},{13,14},{14,13},{17,18},{18,... | collective-permute-start | bytes 589832 | tf_op jit(solution)/shard_map/ppermute | solution.py:30
  29.5 6.8 %collective-permute-start.9 = (f32[384,128]{1,0:T(8,128)S(1)}, f32[384,128]{1,0:T(8,128)S(1)}, u32[]{:S(2)}, u32[]{:S(2)}) collective-permute-start(f32[384,128]{1,0:T(8,128)S(1)} %get-tuple-element.49), channel_id=1, source_target_pairs={{0,4},{4,0},{8,12},{12,8},{16,20},{20,16},{24,28},{28,24},{1,5},{5... | collective-permute-start | bytes 589832 | tf_op jit(solution)/shard_map/ppermute | solution.py:30
  36.5 9.3 %collective-permute-start.10 = (f32[384,128]{1,0:T(8,128)S(1)}, f32[384,128]{1,0:T(8,128)S(1)}, u32[]{:S(2)}, u32[]{:S(2)}) collective-permute-start(f32[384,128]{1,0:T(8,128)S(1)} %get-tuple-element.51), channel_id=1, source_target_pairs={{4,8},{8,4},{12,16},{16,12},{20,24},{24,20},{5,9},{9,5},{13,17},{1... | collective-permute-start | bytes 589832 | tf_op jit(solution)/shard_map/ppermute | solution.py:30
  37.2 8.7 %collective-permute-start.11 = (f32[384,128]{1,0:T(8,128)S(1)}, f32[384,128]{1,0:T(8,128)S(1)}, u32[]{:S(2)}, u32[]{:S(2)}) collective-permute-start(f32[384,128]{1,0:T(8,128)S(1)} %get-tuple-element.52), channel_id=1, source_target_pairs={{0,1},{1,0},{2,3},{3,2},{4,5},{5,4},{6,7},{7,6},{8,9},{9,8},{10,11... | collective-permute-start | bytes 589832 | tf_op jit(solution)/shard_map/ppermute | solution.py:30
  41.4 4.4 %collective-permute-start.12 = (f32[384,128]{1,0:T(8,128)S(1)}, f32[384,128]{1,0:T(8,128)S(1)}, u32[]{:S(2)}, u32[]{:S(2)}) collective-permute-start(f32[384,128]{1,0:T(8,128)S(1)} %get-tuple-element.53), channel_id=1, source_target_pairs={{1,2},{2,1},{5,6},{6,5},{9,10},{10,9},{13,14},{14,13},{17,18},{18,... | collective-permute-start | bytes 589832 | tf_op jit(solution)/shard_map/ppermute | solution.py:30
  42.1 4.8 %collective-permute-start.13 = (f32[384,128]{1,0:T(8,128)S(1)}, f32[384,128]{1,0:T(8,128)S(1)}, u32[]{:S(2)}, u32[]{:S(2)}) collective-permute-start(f32[384,128]{1,0:T(8,128)S(1)} %get-tuple-element.54), channel_id=1, source_target_pairs={{0,4},{4,0},{8,12},{12,8},{16,20},{20,16},{24,28},{28,24},{1,5},{5... | collective-permute-start | bytes 589832 | tf_op jit(solution)/shard_map/ppermute | solution.py:30
  51.9 3.1 %collective-permute-start.14 = (f32[8,128]{1,0:T(8,128)S(1)}, f32[8,128]{1,0:T(8,128)S(1)}, u32[]{:S(2)}, u32[]{:S(2)}) collective-permute-start(f32[8,128]{1,0:T(8,128)S(1)} %get-tuple-element.58.refs_0_), channel_id=1, source_target_pairs={{0,4},{1,5},{2,6},{3,7},{4,0},{5,1},{6,2},{7,3},{8,12},{9,13},{10,... | collective-permute-start | bytes 12296 | tf_op jit(solution)/shard_map/ppermute | solution.py:555
  55.0 5.9 %collective-permute-start.15 = (f32[8,128]{1,0:T(8,128)S(1)}, f32[8,128]{1,0:T(8,128)S(1)}, u32[]{:S(2)}, u32[]{:S(2)}) collective-permute-start(f32[8,128]{1,0:T(8,128)S(1)} %shard_map.93.refs_0_), channel_id=1, source_target_pairs={{0,8},{1,9},{2,10},{3,11},{4,12},{5,13},{6,14},{7,15},{8,0},{9,1},... | collective-permute-start | bytes 12296 | tf_op jit(solution)/shard_map/ppermute | solution.py:555
  61.1 9.7 %collective-permute-start.16 = (f32[384,128]{1,0:T(8,128)S(1)}, f32[384,128]{1,0:T(8,128)S(1)}, u32[]{:S(2)}, u32[]{:S(2)}) collective-permute-start(f32[384,128]{1,0:T(8,128)S(1)} %get-tuple-element.62), channel_id=1, source_target_pairs={{4,8},{8,4},{12,16},{16,12},{20,24},{24,20},{5,9},{9,5},{13,17},{1... | collective-permute-start | bytes 589832 | tf_op jit(solution)/shard_map/ppermute | solution.py:30
  61.7 9.0 %collective-permute-start.17 = (f32[384,128]{1,0:T(8,128)S(1)}, f32[384,128]{1,0:T(8,128)S(1)}, u32[]{:S(2)}, u32[]{:S(2)}) collective-permute-start(f32[384,128]{1,0:T(8,128)S(1)} %get-tuple-element.63), channel_id=1, source_target_pairs={{0,4},{4,0},{8,12},{12,8},{16,20},{20,16},{24,28},{28,24},{1,5},{5... | collective-permute-start | bytes 589832 | tf_op jit(solution)/shard_map/ppermute | solution.py:30
  63.8 5.4 %collective-permute-start.20 = (f32[8,128]{1,0:T(8,128)S(1)}, f32[8,128]{1,0:T(8,128)S(1)}, u32[]{:S(2)}, u32[]{:S(2)}) collective-permute-start(f32[8,128]{1,0:T(8,128)S(1)} %shard_map.95.rest_0_), channel_id=1, source_target_pairs={{0,18},{1,19},{2,16},{3,17},{4,22},{5,23},{6,20},{7,21},{8,26},{9,... | collective-permute-start | bytes 12296 | tf_op jit(solution)/shard_map/ppermute | solution.py:555
  64.8 4.4 %collective-permute-start.19 = (f32[8,128]{1,0:T(8,128)S(1)}, f32[8,128]{1,0:T(8,128)S(1)}, u32[]{:S(2)}, u32[]{:S(2)}) collective-permute-start(f32[8,128]{1,0:T(8,128)S(1)} %shard_map.95.rest_0_), channel_id=1, source_target_pairs={{0,16},{1,17},{2,18},{3,19},{4,20},{5,21},{6,22},{7,23},{8,24},{9,... | collective-permute-start | bytes 12296 | tf_op jit(solution)/shard_map/ppermute | solution.py:555
  66.2 4.5 %collective-permute-start.18 = (f32[8,128]{1,0:T(8,128)S(1)}, f32[8,128]{1,0:T(8,128)S(1)}, u32[]{:S(2)}, u32[]{:S(2)}) collective-permute-start(f32[8,128]{1,0:T(8,128)S(1)} %shard_map.95.rest_0_), channel_id=1, source_target_pairs={{0,2},{1,3},{2,0},{3,1},{4,6},{5,7},{6,4},{7,5},{8,10},{9,11},{10,... | collective-permute-start | bytes 12296 | tf_op jit(solution)/shard_map/ppermute | solution.py:555
  70.9 4.5 %collective-permute-start.21 = (f32[264,128]{1,0:T(8,128)S(1)}, f32[264,128]{1,0:T(8,128)S(1)}, u32[]{:S(2)}, u32[]{:S(2)}) collective-permute-start(f32[264,128]{1,0:T(8,128)S(1)} %get-tuple-element.65), channel_id=1, source_target_pairs={{1,2},{2,1},{5,6},{6,5},{9,10},{10,9},{13,14},{14,13},{17,18},{18,... | collective-permute-start | bytes 405512 | tf_op jit(solution)/shard_map/ppermute | solution.py:30
  71.6 7.3 %collective-permute-start.22 = (f32[264,128]{1,0:T(8,128)S(1)}, f32[264,128]{1,0:T(8,128)S(1)}, u32[]{:S(2)}, u32[]{:S(2)}) collective-permute-start(f32[264,128]{1,0:T(8,128)S(1)} %get-tuple-element.66), channel_id=1, source_target_pairs={{0,1},{1,0},{2,3},{3,2},{4,5},{5,4},{6,7},{7,6},{8,9},{9,8},{10,11... | collective-permute-start | bytes 405512 | tf_op jit(solution)/shard_map/ppermute | solution.py:30

commit v6 on v5

--- a/solution.py
+++ b/solution.py
@@ -395,7 +395,6 @@
     frames = (counts, offsets)
     last = ext.shape[1] - 1
     n = ext.shape[2]
-    ext[...] = total[...]
     add_col_bands(ext, 0, rr1, rr2)
     add_row_bands(ext, 1, ri1, ri2)
 
@@ -656,17 +655,18 @@
     si2, sr1, sr2, si1 = (
         swap(si2, "wide", 1), swap(sr1, "narrow", 0), swap(sr2, "narrow", 1), swap(si1, "wide", 0)
     )
-    image, projected, sums = call(
+    image, projected, sums, _ = call(
         functools.partial(
             second_forward_kernel, lax.axis_size("wide") - 1, lax.axis_size("narrow") - 1
         ),
-        [shape(2, rows, width), shape(slots, rows, width), shape(8, 128)],
+        [shape(2, rows, width), shape(slots, rows, width), shape(8, 128), whole],
         2,
         [
             counts, offsets, si2, sr1, sr2, si1, total, sums, probe_modes, sorted_weights, tables,
         ],
-        [extended, patch, stage],
+        [patch, stage],
         pass_flops // 2,
+        {6: 3},
     )
     along_wide, along_narrow = (powers(lax.axis_size("wide")), powers(lax.axis_size("narrow")))
     rounds = [hops(step, 0) for step in along_wide[:-1]]

time: 79.9 us -> 79.5 us (level)
  starting transfers between devices: 41.7 us -> 53.3 us
  Pallas kernels: 24.5 us -> 13.3 us
  waiting for transfers between devices: 12.5 us -> 11.2 us
    pallas_call x13, Pallas kernels: 24.5 us -> 13.3 us  [call(): pl.pallas_call(kernel, out_shape=[place(o.shape, o.dtype) for o in outs],...]
    ppermute x18, starting transfers between devices: 33 us -> 41.6 us  [swap(): return lax.ppermute(x, axis, wanted)]
    ppermute x18, waiting for transfers between devices: 9.92 us -> 5.62 us  [swap(): return lax.ppermute(x, axis, wanted)]
    ppermute x5, starting transfers between devices: 8.69 us -> 11.7 us  [take_hops(): return [x] + [lax.ppermute(x, ('wide', 'narrow'), perm) for perm in wanted]]
    ppermute x5, waiting for transfers between devices: 2.57 us -> 5.54 us  [take_hops(): return [x] + [lax.ppermute(x, ('wide', 'narrow'), perm) for perm in wanted]]
  transfers between devices with their start and end apart: 23 -> 23, of which waited for: 5 -> 6; matrix products, arithmetic and copies ran while one was open for 0% -> 0% of each run, Pallas kernels for 10% -> 6%
where the time goes in v6:
time: 79.5 us; the launch traced here: 79.2 us
  starting transfers between devices  53.3 us (67%)
  Pallas kernels  13.3 us (17%)
  waiting for transfers between devices  11.2 us (14%)
  between operations  1.52 us (2%)
    ppermute x18, starting transfers between devices, swap(): return lax.ppermute(x, axis, wanted)  41.6 us
    pallas_call x13, Pallas kernels, call(): pl.pallas_call(kernel, out_shape=[place(o.shape, o.dtype) for o in outs],...  13.3 us
    ppermute x5, starting transfers between devices, take_hops(): return [x] + [lax.ppermute(x, ('wide', 'narrow'), perm) for perm in wanted]  11.7 us
    ppermute x18, waiting for transfers between devices, swap(): return lax.ppermute(x, axis, wanted)  5.62 us
    ppermute x5, waiting for transfers between devices, take_hops(): return [x] + [lax.ppermute(x, ('wide', 'narrow'), perm) for perm in wanted]  5.54 us
  transfers between devices with their start and end apart: 23, of which 6 were waited for; matrix products, arithmetic and copies ran while one was open for 0% of the time, Pallas kernels for 6%

profile of v6, /device:TPU:0, one launch (start us, length us, event | category | flops | bytes accessed | tf_op | source)
XLA Modules:
  0.0 79.2 jit_solution(14063576445787670802)
XLA Ops:
  0.6 1.2 %shard_map.86 = (f32[2,64,256]{2,1,0:T(8,128)S(1)}, f32[2,64,256]{2,1,0:T(8,128)S(1)}, f32[256,128]{1,0:T(8,128)S(1)}, f32[256,128]{1,0:T(8,128)S(1)}) custom-call(f32[2,256,256]{2,1,0:T(8,128)} %g_far.1), custom_call_target="tpu_custom_call" | custom-call | bytes 1048576 | tf_op jit(solution)/shard_map/pallas_call | solution.py:579
  1.8 0.7 collective-permute-start.2
  2.5 5.9 %collective-permute-start.3 = (f32[256,128]{1,0:T(8,128)S(1)}, f32[256,128]{1,0:T(8,128)S(1)}, u32[]{:S(2)}, u32[]{:S(2)}) collective-permute-start(f32[256,128]{1,0:T(8,128)S(1)} %get-tuple-element.39), channel_id=1, source_target_pairs={{0,1},{1,0},{2,3},{3,2},{4,5},{5,4},{6,7},{7,6},{8,9},{9,8},{10,11... | collective-permute-start | bytes 393224 | tf_op jit(solution)/shard_map/ppermute | solution.py:30
  8.4 0.7 collective-permute-start
  9.1 2.9 %collective-permute-start.1 = (f32[2,64,256]{2,1,0:T(8,128)S(1)}, f32[2,64,256]{2,1,0:T(8,128)S(1)}, u32[]{:S(2)}, u32[]{:S(2)}) collective-permute-start(f32[2,64,256]{2,1,0:T(8,128)S(1)} %get-tuple-element.37), channel_id=1, source_target_pairs={{0,4},{4,0},{8,12},{12,8},{16,20},{20,16},{24,28},{28,24},{1,5},{5... | collective-permute-start | bytes 393224 | tf_op jit(solution)/shard_map/ppermute | solution.py:30
  12.7 0.0 collective-permute-done.2.col2
  12.7 0.0 collective-permute-done.3.col1
  12.7 0.1 shard_map.87
  12.8 0.7 collective-permute-start.5
  13.5 2.9 %collective-permute-start.4 = (f32[2,64,128]{2,1,0:T(8,128)S(1)}, f32[2,64,128]{2,1,0:T(8,128)S(1)}, u32[]{:S(2)}, u32[]{:S(2)}) collective-permute-start(f32[2,64,128]{2,1,0:T(8,128)S(1)} %get-tuple-element.40.corner), channel_id=1, source_target_pairs={{0,4},{4,0},{8,12},{12,8},{16,20},{20,16},{24,28},{28,24},{1,5},{5... | collective-permute-start | bytes 196616 | tf_op jit(solution)/shard_map/ppermute | solution.py:30
  16.4 0.0 copy-start
  16.4 2.1 %shard_map.88 = (bf16[3,4,256,512]{3,2,1,0:T(8,128)(2,1)S(1)}, bf16[4,2,256,256]{3,2,1,0:T(8,128)(2,1)S(1)}, bf16[4,256,256]{2,1,0:T(8,128)(2,1)S(1)}, f32[2,256,256]{2,1,0:T(8,128)S(1)}) custom-call(s32[1]{0:T(128)} %bitcast.5.counts, f32[2,64,128]{2,1,0:T(8,128)S(1)} %get-tuple-element.40.corner, bf16[3,4,2,256,256]{4,3,2,1,0:T(8,128)(2,1)} %bitcast.14, ...), custom_call_target="tpu_custom_call" | custom-call | flops 1610612736 | bytes 10813444 | tf_op jit(solution)/shard_map/pallas_call | solution.py:579
  18.5 0.0 collective-permute-done.row2
  18.5 0.0 collective-permute-done.1.row1
  18.5 0.0 collective-permute-done.5.corner2
  18.5 0.0 collective-permute-done.4.corner1
  18.5 0.0 copy-done
  18.5 3.4 %shard_map.89 = (f32[2,3,384,128]{3,2,1,0:T(8,128)S(1)}, f32[8,128]{1,0:T(8,128)S(1)}, f32[384,128]{1,0:T(8,128)S(1)}, f32[384,128]{1,0:T(8,128)S(1)}, f32[384,128]{1,0:T(8,128)S(1)}, /*index=5*/f32[384,128]{1,0:T(8,128)S(1)}) custom-call(s32[1]{0:T(128)} %bitcast.6.counts, s32[2,3]{1,0:T(2,128)S(1)} %bitcast.10, ...), custom_call_target="tpu_custom_call" | custom-call | flops 6442450944 | bytes 7868444 | tf_op jit(solution)/shard_map/pallas_call | solution.py:579
  21.9 0.7 collective-permute-start.6
  22.6 3.8 %collective-permute-start.7 = (f32[384,128]{1,0:T(8,128)S(1)}, f32[384,128]{1,0:T(8,128)S(1)}, u32[]{:S(2)}, u32[]{:S(2)}) collective-permute-start(f32[384,128]{1,0:T(8,128)S(1)} %get-tuple-element.47), channel_id=1, source_target_pairs={{0,1},{1,0},{2,3},{3,2},{4,5},{5,4},{6,7},{7,6},{8,9},{9,8},{10,11... | collective-permute-start | bytes 589832 | tf_op jit(solution)/shard_map/ppermute | solution.py:30
  26.5 0.7 collective-permute-start.8
  27.1 5.7 %collective-permute-start.9 = (f32[384,128]{1,0:T(8,128)S(1)}, f32[384,128]{1,0:T(8,128)S(1)}, u32[]{:S(2)}, u32[]{:S(2)}) collective-permute-start(f32[384,128]{1,0:T(8,128)S(1)} %get-tuple-element.49), channel_id=1, source_target_pairs={{0,4},{4,0},{8,12},{12,8},{16,20},{20,16},{24,28},{28,24},{1,5},{5... | collective-permute-start | bytes 589832 | tf_op jit(solution)/shard_map/ppermute | solution.py:30
  32.8 0.0 collective-permute-done.6.rr2
  32.8 0.0 collective-permute-done.7.ri1
  32.8 0.0 collective-permute-done.8.ri2
  32.8 1.1 %collective-permute-done.9.rr1 = f32[384,128]{1,0:T(8,128)S(1)} collective-permute-done((f32[384,128]{1,0:T(8,128)S(1)}, f32[384,128]{1,0:T(8,128)S(1)}, u32[]{:S(2)}, u32[]{:S(2)}) %collective-permute-start.9) | collective-permute-done | bytes 196640 | tf_op jit(solution)/shard_map/ppermute | solution.py:30
  33.9 0.2 shard_map.90
  34.1 0.7 collective-permute-start.10
  34.8 1.7 %collective-permute-start.11 = (f32[384,128]{1,0:T(8,128)S(1)}, f32[384,128]{1,0:T(8,128)S(1)}, u32[]{:S(2)}, u32[]{:S(2)}) collective-permute-start(f32[384,128]{1,0:T(8,128)S(1)} %get-tuple-element.52), channel_id=1, source_target_pairs={{0,1},{1,0},{2,3},{3,2},{4,5},{5,4},{6,7},{7,6},{8,9},{9,8},{10,11... | collective-permute-start | bytes 589832 | tf_op jit(solution)/shard_map/ppermute | solution.py:30
  36.5 0.7 collective-permute-start.12
  37.2 7.3 %collective-permute-start.13 = (f32[384,128]{1,0:T(8,128)S(1)}, f32[384,128]{1,0:T(8,128)S(1)}, u32[]{:S(2)}, u32[]{:S(2)}) collective-permute-start(f32[384,128]{1,0:T(8,128)S(1)} %get-tuple-element.54), channel_id=1, source_target_pairs={{0,4},{4,0},{8,12},{12,8},{16,20},{20,16},{24,28},{28,24},{1,5},{5... | collective-permute-start | bytes 589832 | tf_op jit(solution)/shard_map/ppermute | solution.py:30
  44.5 0.0 collective-permute-done.10.ri2
  44.5 0.0 collective-permute-done.11.rr1
  44.5 0.0 collective-permute-done.12.rr2
  44.5 1.1 %collective-permute-done.13.ri1 = f32[384,128]{1,0:T(8,128)S(1)} collective-permute-done((f32[384,128]{1,0:T(8,128)S(1)}, f32[384,128]{1,0:T(8,128)S(1)}, u32[]{:S(2)}, u32[]{:S(2)}) %collective-permute-start.13) | collective-permute-done | bytes 196640 | tf_op jit(solution)/shard_map/ppermute | solution.py:30
  45.6 2.3 %shard_map.91 = (f32[2,256,256]{2,1,0:T(8,128)S(1)}, f32[3,256,256]{2,1,0:T(8,128)S(1)}, f32[8,128]{1,0:T(8,128)S(1)}, f32[2,3,384,128]{3,2,1,0:T(8,128)S(1)}) custom-call(s32[1]{0:T(128)} %bitcast.7.counts, s32[2,3]{1,0:T(2,128)S(1)} %bitcast.11, f32[384,128]{1,0:T(8,128)S(1)} %collective-permute-done.10.ri2, ...), custom_call_target="tpu_custom_call", output_to_operand_aliasing={{3}: (6, {})} | custom-call | flops 3221225472 | bytes 9183260 | tf_op jit(solution)/shard_map/pallas_call | solution.py:579
  47.9 1.3 %collective-permute-start.14 = (f32[8,128]{1,0:T(8,128)S(1)}, f32[8,128]{1,0:T(8,128)S(1)}, u32[]{:S(2)}, u32[]{:S(2)}) collective-permute-start(f32[8,128]{1,0:T(8,128)S(1)} %get-tuple-element.58.refs_0_), channel_id=1, source_target_pairs={{0,4},{1,5},{2,6},{3,7},{4,0},{5,1},{6,2},{7,3},{8,12},{9,13},{10,... | collective-permute-start | bytes 12296 | tf_op jit(solution)/shard_map/ppermute | solution.py:554
  49.2 1.8 %shard_map.92.rest_0_ = f32[2,3,384,128]{3,2,1,0:T(8,128)S(1)} custom-call(s32[1]{0:T(128)} %bitcast.8.counts, s32[2,3]{1,0:T(2,128)S(1)} %bitcast.12, f32[3,256,256]{2,1,0:T(8,128)S(1)} %get-tuple-element.57.projected, bf16[4,2,256,256]{3,2,1,0:T(8,128)(2,1)S(1)} %get-tuple-element.43.probe, bf16[3,4,256,512]{3,2,1,0:T(8,128)(2,1)S(1)} %get-tuple-element.44.weights, ...), custom_call_target="tpu_custom_call" | custom-call | flops 1073741824 | bytes 6684700 | tf_op jit(solution)/shard_map/pallas_call | solution.py:579
  51.0 0.0 collective-permute-done.14.refs_1_
  51.0 2.8 %collective-permute-start.15 = (f32[8,128]{1,0:T(8,128)S(1)}, f32[8,128]{1,0:T(8,128)S(1)}, u32[]{:S(2)}, u32[]{:S(2)}) collective-permute-start(f32[8,128]{1,0:T(8,128)S(1)} %shard_map.93.refs_0_), channel_id=1, source_target_pairs={{0,8},{1,9},{2,10},{3,11},{4,12},{5,13},{6,14},{7,15},{8,0},{9,1},... | collective-permute-start | bytes 12296 | tf_op jit(solution)/shard_map/ppermute | solution.py:554
  53.8 0.6 shard_map.94.total
  54.4 1.0 %collective-permute-done.15.refs_1_ = f32[8,128]{1,0:T(8,128)S(1)} collective-permute-done((f32[8,128]{1,0:T(8,128)S(1)}, f32[8,128]{1,0:T(8,128)S(1)}, u32[]{:S(2)}, u32[]{:S(2)}) %collective-permute-start.15) | collective-permute-done | bytes 4128 | tf_op jit(solution)/shard_map/ppermute | solution.py:554
  55.4 0.7 collective-permute-start.16
  56.1 3.4 %collective-permute-start.17 = (f32[384,128]{1,0:T(8,128)S(1)}, f32[384,128]{1,0:T(8,128)S(1)}, u32[]{:S(2)}, u32[]{:S(2)}) collective-permute-start(f32[384,128]{1,0:T(8,128)S(1)} %get-tuple-element.63), channel_id=1, source_target_pairs={{0,4},{4,0},{8,12},{12,8},{16,20},{20,16},{24,28},{28,24},{1,5},{5... | collective-permute-start | bytes 589832 | tf_op jit(solution)/shard_map/ppermute | solution.py:30
  59.6 6.0 %collective-permute-start.20 = (f32[8,128]{1,0:T(8,128)S(1)}, f32[8,128]{1,0:T(8,128)S(1)}, u32[]{:S(2)}, u32[]{:S(2)}) collective-permute-start(f32[8,128]{1,0:T(8,128)S(1)} %shard_map.95.rest_0_), channel_id=1, source_target_pairs={{0,18},{1,19},{2,16},{3,17},{4,22},{5,23},{6,20},{7,21},{8,26},{9,... | collective-permute-start | bytes 12296 | tf_op jit(solution)/shard_map/ppermute | solution.py:554
  65.5 1.7 %collective-permute-start.19 = (f32[8,128]{1,0:T(8,128)S(1)}, f32[8,128]{1,0:T(8,128)S(1)}, u32[]{:S(2)}, u32[]{:S(2)}) collective-permute-start(f32[8,128]{1,0:T(8,128)S(1)} %shard_map.95.rest_0_), channel_id=1, source_target_pairs={{0,16},{1,17},{2,18},{3,19},{4,20},{5,21},{6,22},{7,23},{8,24},{9,... | collective-permute-start | bytes 12296 | tf_op jit(solution)/shard_map/ppermute | solution.py:554
  67.2 0.0 collective-permute-start.18
  67.2 0.0 collective-permute-done.20.rest_3_
  67.2 1.9 %collective-permute-done.19.rest_2_ = f32[8,128]{1,0:T(8,128)S(1)} collective-permute-done((f32[8,128]{1,0:T(8,128)S(1)}, f32[8,128]{1,0:T(8,128)S(1)}, u32[]{:S(2)}, u32[]{:S(2)}) %collective-permute-start.19) | collective-permute-done | bytes 4128 | tf_op jit(solution)/shard_map/ppermute | solution.py:554
  69.1 2.6 %collective-permute-done.18.rest_1_ = f32[8,128]{1,0:T(8,128)S(1)} collective-permute-done((f32[8,128]{1,0:T(8,128)S(1)}, f32[8,128]{1,0:T(8,128)S(1)}, u32[]{:S(2)}, u32[]{:S(2)}) %collective-permute-start.18) | collective-permute-done | bytes 4128 | tf_op jit(solution)/shard_map/ppermute | solution.py:554
  71.7 0.0 collective-permute-done.16.second
  71.7 0.0 collective-permute-done.17.first
  71.7 0.2 shard_map.97
  71.9 0.7 collective-permute-start.21
  72.5 1.9 %collective-permute-start.22 = (f32[264,128]{1,0:T(8,128)S(1)}, f32[264,128]{1,0:T(8,128)S(1)}, u32[]{:S(2)}, u32[]{:S(2)}) collective-permute-start(f32[264,128]{1,0:T(8,128)S(1)} %get-tuple-element.66), channel_id=1, source_target_pairs={{0,1},{1,0},{2,3},{3,2},{4,5},{5,4},{6,7},{7,6},{8,9},{9,8},{10,11... | collective-permute-start | bytes 405512 | tf_op jit(solution)/shard_map/ppermute | solution.py:30
  74.4 0.0 collective-permute-done.21.second
  74.4 3.5 %collective-permute-done.22.first = f32[264,128]{1,0:T(8,128)S(1)} collective-permute-done((f32[264,128]{1,0:T(8,128)S(1)}, f32[264,128]{1,0:T(8,128)S(1)}, u32[]{:S(2)}, u32[]{:S(2)}) %collective-permute-start.22) | collective-permute-done | bytes 135200 | tf_op jit(solution)/shard_map/ppermute | solution.py:30
  77.9 1.3 %shard_map.98 = (f32[2,256,256]{2,1,0:T(8,128)}, f32[2,256,256]{2,1,0:T(8,128)}) custom-call(f32[264,128]{1,0:T(8,128)S(1)} %collective-permute-done.21.second, f32[264,128]{1,0:T(8,128)S(1)} %collective-permute-done.22.first, f32[2,256,256]{2,1,0:T(8,128)S(1)} %get-tuple-element.41.g, f32[2,256,256]{2,1,0:T(8,128)S(1)} %get-tuple-element.67.image, ...), custom_call_target="tpu_custom_call" | custom-call | bytes 3158016 | tf_op jit(solution)/shard_map/pallas_call | solution.py:579
  (3 shorter events, 0.0 us)
Async XLA Ops:
  1.8 10.8 %collective-permute-start.2 = (f32[256,128]{1,0:T(8,128)S(1)}, f32[256,128]{1,0:T(8,128)S(1)}, u32[]{:S(2)}, u32[]{:S(2)}) collective-permute-start(f32[256,128]{1,0:T(8,128)S(1)} %get-tuple-element.38), channel_id=1, source_target_pairs={{1,2},{2,1},{5,6},{6,5},{9,10},{10,9},{13,14},{14,13},{17,18},{18,... | collective-permute-start | bytes 393224 | tf_op jit(solution)/shard_map/ppermute | solution.py:30
  2.5 10.1 %collective-permute-start.3 = (f32[256,128]{1,0:T(8,128)S(1)}, f32[256,128]{1,0:T(8,128)S(1)}, u32[]{:S(2)}, u32[]{:S(2)}) collective-permute-start(f32[256,128]{1,0:T(8,128)S(1)} %get-tuple-element.39), channel_id=1, source_target_pairs={{0,1},{1,0},{2,3},{3,2},{4,5},{5,4},{6,7},{7,6},{8,9},{9,8},{10,11... | collective-permute-start | bytes 393224 | tf_op jit(solution)/shard_map/ppermute | solution.py:30
  8.4 10.1 %collective-permute-start = (f32[2,64,256]{2,1,0:T(8,128)S(1)}, f32[2,64,256]{2,1,0:T(8,128)S(1)}, u32[]{:S(2)}, u32[]{:S(2)}) collective-permute-start(f32[2,64,256]{2,1,0:T(8,128)S(1)} %get-tuple-element.36), channel_id=1, source_target_pairs={{4,8},{8,4},{12,16},{16,12},{20,24},{24,20},{5,9},{9,5},{13,17},{1... | collective-permute-start | bytes 393224 | tf_op jit(solution)/shard_map/ppermute | solution.py:30
  9.1 9.4 %collective-permute-start.1 = (f32[2,64,256]{2,1,0:T(8,128)S(1)}, f32[2,64,256]{2,1,0:T(8,128)S(1)}, u32[]{:S(2)}, u32[]{:S(2)}) collective-permute-start(f32[2,64,256]{2,1,0:T(8,128)S(1)} %get-tuple-element.37), channel_id=1, source_target_pairs={{0,4},{4,0},{8,12},{12,8},{16,20},{20,16},{24,28},{28,24},{1,5},{5... | collective-permute-start | bytes 393224 | tf_op jit(solution)/shard_map/ppermute | solution.py:30
  12.8 5.7 %collective-permute-start.5 = (f32[2,64,128]{2,1,0:T(8,128)S(1)}, f32[2,64,128]{2,1,0:T(8,128)S(1)}, u32[]{:S(2)}, u32[]{:S(2)}) collective-permute-start(f32[2,64,128]{2,1,0:T(8,128)S(1)} %get-tuple-element.42), channel_id=1, source_target_pairs={{4,8},{8,4},{12,16},{16,12},{20,24},{24,20},{5,9},{9,5},{13,17},{1... | collective-permute-start | bytes 196616 | tf_op jit(solution)/shard_map/ppermute | solution.py:30
  13.5 5.1 %collective-permute-start.4 = (f32[2,64,128]{2,1,0:T(8,128)S(1)}, f32[2,64,128]{2,1,0:T(8,128)S(1)}, u32[]{:S(2)}, u32[]{:S(2)}) collective-permute-start(f32[2,64,128]{2,1,0:T(8,128)S(1)} %get-tuple-element.40.corner), channel_id=1, source_target_pairs={{0,4},{4,0},{8,12},{12,8},{16,20},{20,16},{24,28},{28,24},{1,5},{5... | collective-permute-start | bytes 196616 | tf_op jit(solution)/shard_map/ppermute | solution.py:30
  16.4 2.2 %copy-start = (s32[1,1,3,2]{2,3,1,0:T(2,128)S(1)}, s32[1,1,3,2]{2,3,1,0:T(2,128)}, u32[]{:S(2)}) copy-start(s32[1,1,3,2]{2,3,1,0:T(2,128)} %param.10) | copy-start | bytes 76
  21.9 10.9 %collective-permute-start.6 = (f32[384,128]{1,0:T(8,128)S(1)}, f32[384,128]{1,0:T(8,128)S(1)}, u32[]{:S(2)}, u32[]{:S(2)}) collective-permute-start(f32[384,128]{1,0:T(8,128)S(1)} %get-tuple-element.46), channel_id=1, source_target_pairs={{4,8},{8,4},{12,16},{16,12},{20,24},{24,20},{5,9},{9,5},{13,17},{1... | collective-permute-start | bytes 589832 | tf_op jit(solution)/shard_map/ppermute | solution.py:30
  22.6 10.2 %collective-permute-start.7 = (f32[384,128]{1,0:T(8,128)S(1)}, f32[384,128]{1,0:T(8,128)S(1)}, u32[]{:S(2)}, u32[]{:S(2)}) collective-permute-start(f32[384,128]{1,0:T(8,128)S(1)} %get-tuple-element.47), channel_id=1, source_target_pairs={{0,1},{1,0},{2,3},{3,2},{4,5},{5,4},{6,7},{7,6},{8,9},{9,8},{10,11... | collective-permute-start | bytes 589832 | tf_op jit(solution)/shard_map/ppermute | solution.py:30
  26.5 6.4 %collective-permute-start.8 = (f32[384,128]{1,0:T(8,128)S(1)}, f32[384,128]{1,0:T(8,128)S(1)}, u32[]{:S(2)}, u32[]{:S(2)}) collective-permute-start(f32[384,128]{1,0:T(8,128)S(1)} %get-tuple-element.48), channel_id=1, source_target_pairs={{1,2},{2,1},{5,6},{6,5},{9,10},{10,9},{13,14},{14,13},{17,18},{18,... | collective-permute-start | bytes 589832 | tf_op jit(solution)/shard_map/ppermute | solution.py:30
  27.1 6.8 %collective-permute-start.9 = (f32[384,128]{1,0:T(8,128)S(1)}, f32[384,128]{1,0:T(8,128)S(1)}, u32[]{:S(2)}, u32[]{:S(2)}) collective-permute-start(f32[384,128]{1,0:T(8,128)S(1)} %get-tuple-element.49), channel_id=1, source_target_pairs={{0,4},{4,0},{8,12},{12,8},{16,20},{20,16},{24,28},{28,24},{1,5},{5... | collective-permute-start | bytes 589832 | tf_op jit(solution)/shard_map/ppermute | solution.py:30
  34.1 10.4 %collective-permute-start.10 = (f32[384,128]{1,0:T(8,128)S(1)}, f32[384,128]{1,0:T(8,128)S(1)}, u32[]{:S(2)}, u32[]{:S(2)}) collective-permute-start(f32[384,128]{1,0:T(8,128)S(1)} %get-tuple-element.51), channel_id=1, source_target_pairs={{4,8},{8,4},{12,16},{16,12},{20,24},{24,20},{5,9},{9,5},{13,17},{1... | collective-permute-start | bytes 589832 | tf_op jit(solution)/shard_map/ppermute | solution.py:30
  34.8 9.7 %collective-permute-start.11 = (f32[384,128]{1,0:T(8,128)S(1)}, f32[384,128]{1,0:T(8,128)S(1)}, u32[]{:S(2)}, u32[]{:S(2)}) collective-permute-start(f32[384,128]{1,0:T(8,128)S(1)} %get-tuple-element.52), channel_id=1, source_target_pairs={{0,1},{1,0},{2,3},{3,2},{4,5},{5,4},{6,7},{7,6},{8,9},{9,8},{10,11... | collective-permute-start | bytes 589832 | tf_op jit(solution)/shard_map/ppermute | solution.py:30
  36.5 8.0 %collective-permute-start.12 = (f32[384,128]{1,0:T(8,128)S(1)}, f32[384,128]{1,0:T(8,128)S(1)}, u32[]{:S(2)}, u32[]{:S(2)}) collective-permute-start(f32[384,128]{1,0:T(8,128)S(1)} %get-tuple-element.53), channel_id=1, source_target_pairs={{1,2},{2,1},{5,6},{6,5},{9,10},{10,9},{13,14},{14,13},{17,18},{18,... | collective-permute-start | bytes 589832 | tf_op jit(solution)/shard_map/ppermute | solution.py:30
  37.2 8.4 %collective-permute-start.13 = (f32[384,128]{1,0:T(8,128)S(1)}, f32[384,128]{1,0:T(8,128)S(1)}, u32[]{:S(2)}, u32[]{:S(2)}) collective-permute-start(f32[384,128]{1,0:T(8,128)S(1)} %get-tuple-element.54), channel_id=1, source_target_pairs={{0,4},{4,0},{8,12},{12,8},{16,20},{20,16},{24,28},{28,24},{1,5},{5... | collective-permute-start | bytes 589832 | tf_op jit(solution)/shard_map/ppermute | solution.py:30
  47.9 3.1 %collective-permute-start.14 = (f32[8,128]{1,0:T(8,128)S(1)}, f32[8,128]{1,0:T(8,128)S(1)}, u32[]{:S(2)}, u32[]{:S(2)}) collective-permute-start(f32[8,128]{1,0:T(8,128)S(1)} %get-tuple-element.58.refs_0_), channel_id=1, source_target_pairs={{0,4},{1,5},{2,6},{3,7},{4,0},{5,1},{6,2},{7,3},{8,12},{9,13},{10,... | collective-permute-start | bytes 12296 | tf_op jit(solution)/shard_map/ppermute | solution.py:554
  51.0 4.4 %collective-permute-start.15 = (f32[8,128]{1,0:T(8,128)S(1)}, f32[8,128]{1,0:T(8,128)S(1)}, u32[]{:S(2)}, u32[]{:S(2)}) collective-permute-start(f32[8,128]{1,0:T(8,128)S(1)} %shard_map.93.refs_0_), channel_id=1, source_target_pairs={{0,8},{1,9},{2,10},{3,11},{4,12},{5,13},{6,14},{7,15},{8,0},{9,1},... | collective-permute-start | bytes 12296 | tf_op jit(solution)/shard_map/ppermute | solution.py:554
  55.4 16.2 %collective-permute-start.16 = (f32[384,128]{1,0:T(8,128)S(1)}, f32[384,128]{1,0:T(8,128)S(1)}, u32[]{:S(2)}, u32[]{:S(2)}) collective-permute-start(f32[384,128]{1,0:T(8,128)S(1)} %get-tuple-element.62), channel_id=1, source_target_pairs={{4,8},{8,4},{12,16},{16,12},{20,24},{24,20},{5,9},{9,5},{13,17},{1... | collective-permute-start | bytes 589832 | tf_op jit(solution)/shard_map/ppermute | solution.py:30
  56.1 15.6 %collective-permute-start.17 = (f32[384,128]{1,0:T(8,128)S(1)}, f32[384,128]{1,0:T(8,128)S(1)}, u32[]{:S(2)}, u32[]{:S(2)}) collective-permute-start(f32[384,128]{1,0:T(8,128)S(1)} %get-tuple-element.63), channel_id=1, source_target_pairs={{0,4},{4,0},{8,12},{12,8},{16,20},{20,16},{24,28},{28,24},{1,5},{5... | collective-permute-start | bytes 589832 | tf_op jit(solution)/shard_map/ppermute | solution.py:30
  59.6 7.6 %collective-permute-start.20 = (f32[8,128]{1,0:T(8,128)S(1)}, f32[8,128]{1,0:T(8,128)S(1)}, u32[]{:S(2)}, u32[]{:S(2)}) collective-permute-start(f32[8,128]{1,0:T(8,128)S(1)} %shard_map.95.rest_0_), channel_id=1, source_target_pairs={{0,18},{1,19},{2,16},{3,17},{4,22},{5,23},{6,20},{7,21},{8,26},{9,... | collective-permute-start | bytes 12296 | tf_op jit(solution)/shard_map/ppermute | solution.py:554
  65.5 3.6 %collective-permute-start.19 = (f32[8,128]{1,0:T(8,128)S(1)}, f32[8,128]{1,0:T(8,128)S(1)}, u32[]{:S(2)}, u32[]{:S(2)}) collective-permute-start(f32[8,128]{1,0:T(8,128)S(1)} %shard_map.95.rest_0_), channel_id=1, source_target_pairs={{0,16},{1,17},{2,18},{3,19},{4,20},{5,21},{6,22},{7,23},{8,24},{9,... | collective-permute-start | bytes 12296 | tf_op jit(solution)/shard_map/ppermute | solution.py:554
  67.2 4.5 %collective-permute-start.18 = (f32[8,128]{1,0:T(8,128)S(1)}, f32[8,128]{1,0:T(8,128)S(1)}, u32[]{:S(2)}, u32[]{:S(2)}) collective-permute-start(f32[8,128]{1,0:T(8,128)S(1)} %shard_map.95.rest_0_), channel_id=1, source_target_pairs={{0,2},{1,3},{2,0},{3,1},{4,6},{5,7},{6,4},{7,5},{8,10},{9,11},{10,... | collective-permute-start | bytes 12296 | tf_op jit(solution)/shard_map/ppermute | solution.py:554
  71.9 2.5 %collective-permute-start.21 = (f32[264,128]{1,0:T(8,128)S(1)}, f32[264,128]{1,0:T(8,128)S(1)}, u32[]{:S(2)}, u32[]{:S(2)}) collective-permute-start(f32[264,128]{1,0:T(8,128)S(1)} %get-tuple-element.65), channel_id=1, source_target_pairs={{1,2},{2,1},{5,6},{6,5},{9,10},{10,9},{13,14},{14,13},{17,18},{18,... | collective-permute-start | bytes 405512 | tf_op jit(solution)/shard_map/ppermute | solution.py:30
  72.5 5.3 %collective-permute-start.22 = (f32[264,128]{1,0:T(8,128)S(1)}, f32[264,128]{1,0:T(8,128)S(1)}, u32[]{:S(2)}, u32[]{:S(2)}) collective-permute-start(f32[264,128]{1,0:T(8,128)S(1)} %get-tuple-element.66), channel_id=1, source_target_pairs={{0,1},{1,0},{2,3},{3,2},{4,5},{5,4},{6,7},{7,6},{8,9},{9,8},{10,11... | collective-permute-start | bytes 405512 | tf_op jit(solution)/shard_map/ppermute | solution.py:30
